TPU v7x, 512 devices: a whole 4x8x8 slice. The times are simulated.
512 devices in a mesh: expert: 32 (over x, z), seq: 8 (over y), dp: 2 (over core).
Axes of the slice: x: 4, y: 8, z: 8, core: 2. Of those that a mesh axis runs over, the one named last changes fastest.
Arguments:
- moe_input: bfloat16 [65536, 2048], P(('expert', 'seq', 'dp')), may hold values from -6 to 6
- lm_grad: bfloat16 [65536, 2048], P(('expert', 'seq', 'dp')), may hold values from -6 to 6
- frame_grad: bfloat16 [16384, 2048], P(('expert', 'seq', 'dp')), may hold values from -6 to 6
- span_token: int32 [4096], P(('expert', 'seq', 'dp')), may hold values from 0 to 1023
- expert_ids: int32 [65536, 2], P(('expert', 'seq', 'dp')), may hold values from 0 to 31, all different within a row; in each aligned block of 128 rows (0 to 127, 128 to 255, ...) at most 16 rows name the same one
- gate_weights: bfloat16 [65536, 2], P(('expert', 'seq', 'dp')), may hold values from 0.049804688 to 0.5
- w_gate_up: bfloat16 [32, 2048, 2, 384], P('expert', ('seq', 'dp')), may hold values from -0.125 to 0.125
- w_down: bfloat16 [32, 2048, 384], P('expert', ('seq', 'dp')), may hold values from -0.3125 to 0.3125
Outputs:
- grad_input: bfloat16 [65536, 2048], P(('expert', 'seq', 'dp'))
- grad_gates: bfloat16 [65536, 2], P(('expert', 'seq', 'dp'))
- grad_gate_up: float32 [32, 2048, 2, 384], P('expert', ('seq', 'dp'))
Inputs may be any that keep to these rules, and one draw needn't show every extreme that they name: `span_token`: every value names a token of the span's own dialogue group. `expert_ids`: A token's experts are distinct. Of one device's rows at most 16 name one expert, and in every draw some expert is named by exactly 16 rows of some device.
All inputs are finite; a program needn't handle non-finite values.
Results may differ from a plain program's by a relative error of at most 0.02.
Values may be sent and summed in bfloat16 or wider, within the bound.
No kernel may reach another device: no remote copies, remote signals or barrier semaphores. Data moves between devices by JAX's collectives and lax.ppermute only.
A program may use at most 64 MiB of HBM per device.

v0:
```python
import jax
import jax.numpy as jnp
from jax import lax
from jax.sharding import PartitionSpec as P


def silu_parts(gate_pre):
    sigmoid_gate = jax.nn.sigmoid(gate_pre)
    activated = gate_pre * sigmoid_gate
    slope = sigmoid_gate * (1.0 + gate_pre * (1.0 - sigmoid_gate))
    return (activated, slope)


def on_device(
    moe_input, lm_grad, frame_grad, span_token, expert_ids, gate_weights, w_gate_up, w_down
):
    tok_count, model_width = moe_input.shape
    top_count = expert_ids.shape[1]
    frames_per_span = frame_grad.shape[0] // span_token.shape[0]
    expert_count = lax.axis_size("expert")
    capacity = 2 * tok_count * top_count // expert_count
    slot_rows = expert_count * capacity
    slot_expert = expert_ids.reshape(-1)
    slot_token = lax.iota(jnp.int32, tok_count * top_count) // top_count
    member = (slot_expert[:, None] == lax.iota(jnp.int32, expert_count)[None, :]).astype(jnp.int32)
    position = jnp.sum((jnp.cumsum(member, axis=0) - member) * member, axis=1)
    target = slot_expert * capacity + position
    send_input = (
        jnp.zeros((slot_rows, model_width), jnp.bfloat16).at[target].set(moe_input[slot_token])
    )
    send_gate = jnp.zeros((slot_rows,), jnp.bfloat16).at[target].set(gate_weights.reshape(-1))
    own_tokens = lax.axis_index("seq") * tok_count + lax.iota(jnp.int32, tok_count)
    frame_rows = lax.all_gather(frame_grad, "seq", axis=0, tiled=True)
    span_names = lax.all_gather(span_token, "seq", axis=0, tiled=True)
    frame_names = jnp.repeat(span_names, frames_per_span)
    select = (own_tokens[:, None] == frame_names[None, :]).astype(jnp.bfloat16)
    cond_sum = jnp.dot(select, frame_rows, preferred_element_type=jnp.float32)
    upstream = (lm_grad.astype(jnp.float32) + cond_sum).astype(jnp.bfloat16)
    send_grad = (
        jnp.zeros((slot_rows, model_width), jnp.bfloat16).at[target].set(upstream[slot_token])
    )
    got_input, got_grad, got_gate = (
        lax.all_to_all(
            send_input.reshape(expert_count, capacity, model_width),
            "expert",
            split_axis=0,
            concat_axis=0,
            tiled=True,
        ),
        lax.all_to_all(
            send_grad.reshape(expert_count, capacity, model_width),
            "expert",
            split_axis=0,
            concat_axis=0,
            tiled=True,
        ),
        lax.all_to_all(
            send_gate.reshape(expert_count, capacity),
            "expert",
            split_axis=0,
            concat_axis=0,
            tiled=True,
        ),
    )
    slot_input = got_input.reshape(slot_rows, model_width)
    gate_up_full, down_full = (
        lax.all_gather(w_gate_up, ("seq", "dp"), axis=1, tiled=True),
        lax.all_gather(w_down, ("seq", "dp"), axis=1, tiled=True),
    )
    pre_acts = jnp.einsum(
        "rd,dcf->rcf", slot_input, gate_up_full[0], preferred_element_type=jnp.float32
    )
    gate_pre = pre_acts[:, 0]
    up_pre = pre_acts[:, 1]
    activated, slope = silu_parts(gate_pre)
    hidden = (activated * up_pre).astype(jnp.bfloat16)
    expert_out = lax.dot_general(
        hidden, down_full[0], (((1,), (1,)), ((), ())), preferred_element_type=jnp.float32
    )
    slot_grad = got_grad.reshape(slot_rows, model_width)
    slot_gate = got_gate.reshape(slot_rows).astype(jnp.float32)
    grad_float = slot_grad.astype(jnp.float32)
    gate_grad_slot = jnp.sum(grad_float * expert_out, axis=1).astype(jnp.bfloat16)
    scaled_grad = (slot_gate[:, None] * grad_float).astype(jnp.bfloat16)
    hidden_grad = jnp.dot(scaled_grad, down_full[0], preferred_element_type=jnp.float32)
    pre_grad = jnp.stack([hidden_grad * up_pre * slope, hidden_grad * activated], axis=1).astype(
        jnp.bfloat16
    )
    input_grad = jnp.einsum(
        "rcf,dcf->rd", pre_grad, gate_up_full[0], preferred_element_type=jnp.float32
    )
    grad_gate_up = lax.psum_scatter(
        jnp.einsum("rd,rcf->dcf", slot_input, pre_grad, preferred_element_type=jnp.float32).astype(
            jnp.bfloat16
        ),
        ("seq", "dp"),
        scatter_dimension=0,
        tiled=True,
    ).astype(jnp.float32)
    back_input, back_gate = (
        lax.all_to_all(
            input_grad.astype(jnp.bfloat16).reshape(expert_count, capacity, model_width),
            "expert",
            split_axis=0,
            concat_axis=0,
            tiled=True,
        ),
        lax.all_to_all(
            gate_grad_slot.reshape(expert_count, capacity),
            "expert",
            split_axis=0,
            concat_axis=0,
            tiled=True,
        ),
    )
    slot_back = back_input.reshape(slot_rows, model_width)[target]
    summed = jnp.sum(
        slot_back.reshape(tok_count, top_count, model_width).astype(jnp.float32), axis=1
    )
    grad_input = summed.astype(jnp.bfloat16)
    grad_gates = back_gate.reshape(slot_rows)[target].reshape(tok_count, top_count)
    return (grad_input, grad_gates, grad_gate_up[None])


def solution(mesh):
    placed = (
        P(("expert", "seq", "dp"), None),
        P(("expert", "seq", "dp"), None),
        P(("expert", "seq", "dp"), None),
        P(("expert", "seq", "dp")),
        P(("expert", "seq", "dp"), None),
        P(("expert", "seq", "dp"), None),
        P("expert", ("seq", "dp"), None, None),
        P("expert", ("seq", "dp"), None),
    )
    return jax.shard_map(
        on_device,
        mesh=mesh,
        in_specs=placed,
        out_specs=(
            P(("expert", "seq", "dp"), None),
            P(("expert", "seq", "dp"), None),
            P("expert", ("seq", "dp"), None, None),
        ),
        check_vma=False,
    )
```

profile of v0, /device:TPU:56, one launch (start us, length us, event | category | flops | bytes accessed | tf_op | source)
XLA Modules:
  0.0 254.0 jit_solution(16477118412157919906)
XLA Ops:
  7.9 0.8 copy.24
  9.0 0.8 copy.27
  11.8 2.2 scatter_custom_fusion
  14.7 13.2 %all-to-all-start = ((bf16[32,1,16]{2,1,0:T(2,128)(2,1)}), bf16[32,1,16]{2,1,0:T(2,128)(2,1)S(1)}, u32[]{:S(2)}, u32[]{:S(2)}) async-start(bf16[32,1,16]{2,1,0:T(2,128)(2,1)} %all_to_all.25), calls=%async_computation | async-start | bytes 32768 | tf_op jit(solution)/shard_map/all_to_all | solution.py:57
  27.9 1.6 copy.29
  29.6 7.1 %scatter_custom_fusion.2 = bf16[512,2048]{1,0:T(8,128)(2,1)} fusion(s32[256]{0:T(256)S(1)} %bitcast.112, bf16[128,2048]{1,0:T(8,128)(2,1)S(1)} %copy-done, s32[1024]{0:T(1024)S(1)} %pad_clamp_fusion.1, bf16[]{:T(256)} %constant.32.clone.1), kind=kCustom, calls=%fused_computation.20 | custom fusion | bytes 2097154 | tf_op jit(solution)/shard_map/scatter | solution.py:29
  36.7 0.9 all-to-all-done
  37.6 9.1 %all-to-all-start.2 = ((bf16[32,16,2048]{2,1,0:T(8,128)(2,1)}), bf16[32,16,2048]{2,1,0:T(8,128)(2,1)S(1)}, u32[]{:S(2)}, u32[]{:S(2)}) async-start(bf16[32,16,2048]{2,1,0:T(8,128)(2,1)} %bitcast.9), calls=%async_computation.2 | async-start | bytes 4194304 | tf_op jit(solution)/shard_map/all_to_all | solution.py:43
  46.6 1.3 dynamic-slice
  48.8 10.6 %all-reduce = s32[64]{0:T(128)S(1)} all-reduce(s32[64]{0:T(128)S(1)} %dynamic-update-slice), channel_id=1, replica_groups=mesh['expert'=32,'seq'=8,'dp'=2] {'seq'}, use_global_device_ids=true, to_apply=%add | all-reduce | flops 64 | bytes 512
  59.7 2.4 fusion.4
  62.0 7.2 %scatter_custom_fusion.1 = bf16[512,2048]{1,0:T(8,128)(2,1)} fusion(s32[256]{0:T(256)S(1)} %bitcast.113, bf16[128,2048]{1,0:T(8,128)(2,1)} %fusion.4, s32[1024]{0:T(1024)S(1)} %pad_clamp_fusion.1, bf16[]{:T(256)} %constant.32.clone.1), kind=kCustom, calls=%fused_computation.22 | custom fusion | bytes 2097664 | tf_op jit(solution)/shard_map/scatter | solution.py:40
  69.2 27.1 %all-to-all-done.2 = bf16[32,16,2048]{2,1,0:T(8,128)(2,1)S(1)} async-done(((bf16[32,16,2048]{2,1,0:T(8,128)(2,1)}), bf16[32,16,2048]{2,1,0:T(8,128)(2,1)S(1)}, u32[]{:S(2)}, u32[]{:S(2)}) %all-to-all-start.2) | async-done | bytes 2097184 | tf_op jit(solution)/shard_map/all_to_all | solution.py:43
  96.3 1.4 copy-done.1
  97.6 5.9 %all-to-all-start.1 = ((bf16[32,16,2048]{2,1,0:T(8,128)(2,1)}), bf16[32,16,2048]{2,1,0:T(8,128)(2,1)S(1)}, u32[]{:S(2)}, u32[]{:S(2)}) async-start(bf16[32,16,2048]{2,1,0:T(8,128)(2,1)} %bitcast.105), calls=%async_computation.1 | async-start | bytes 4194304 | tf_op jit(solution)/shard_map/all_to_all | solution.py:50
  104.4 5.5 %fusion.2 = f32[512,2,384]{2,0,1:T(8,128)} fusion(bf16[512,2048,1]{1,0,2:T(8,128)(2,1)} %bitcast.106, bf16[1,2048,2,384]{3,1,2,0:T(8,128)(2,1)} %all-gather.8.cloned.1.call-done), kind=kOutput, calls=%fused_computation.13 | convolution fusion | flops 1610612736 | bytes 6815744 | tf_op jit(solution)/shard_map/rd,dcf->rcf/dot_general | solution.py:70
  109.9 43.3 %all-to-all-done.1 = bf16[32,16,2048]{2,1,0:T(8,128)(2,1)S(1)} async-done(((bf16[32,16,2048]{2,1,0:T(8,128)(2,1)}), bf16[32,16,2048]{2,1,0:T(8,128)(2,1)S(1)}, u32[]{:S(2)}, u32[]{:S(2)}) %all-to-all-start.1) | async-done | bytes 2097184 | tf_op jit(solution)/shard_map/all_to_all | solution.py:50
  153.3 1.8 multiply_convert_fusion
  155.0 4.0 %fusion.25 = (bf16[512,1,384]{2,0,1:T(8,128)(2,1)S(1)}, bf16[512,1,384]{2,0,1:T(8,128)(2,1)S(1)}) fusion(f32[512,2,384]{2,0,1:T(8,128)} %fusion.2, bf16[512,2048]{1,0:T(8,128)(2,1)} %bitcast.109, bf16[1,2048,384]{2,1,0:T(8,128)(2,1)} %all-gather.6.cloned.1.call-done), kind=kOutput, calls=%fused_computation.43 | convolution fusion | flops 807862272 | bytes 6029312 | tf_op jit(solution)/shard_map/dot_general | solution.py:85
  159.8 3.6 %convolution_convert_fusion = bf16[2048,2,384]{2,0,1:T(8,128)(2,1)} fusion(bf16[512,2048,1]{1,0,2:T(8,128)(2,1)S(1)} %bitcast.107, bf16[512,1,384]{2,0,1:T(8,128)(2,1)S(1)} %get-tuple-element.13, bf16[512,1,384]{2,0,1:T(8,128)(2,1)S(1)} %get-tuple-element.12), kind=kOutput, calls=%fused_computation.11 | convolution fusion | flops 1613758464 | bytes 6029312 | tf_op jit(solution)/shard_map/rd,rcf->dcf/dot_general | solution.py:93
  163.5 3.3 %fusion = bf16[512]{0:T(512)(128)(2,1)S(1)} fusion(bf16[1,2048,384]{2,1,0:T(8,128)(2,1)} %all-gather.6.cloned.1.call-done, bf16[32,16,2048]{2,1,0:T(8,128)(2,1)S(1)} %all-to-all-done.1, f32[512,2,384]{2,0,1:T(8,128)} %fusion.2), kind=kOutput, calls=%fused_computation.8 | convolution fusion | flops 809631232 | bytes 5243904 | tf_op jit(solution)/shard_map/dot_general | solution.py:77
  167.4 6.0 %all-to-all-start.4 = ((bf16[32,1,16]{2,1,0:T(2,128)(2,1)}), bf16[32,1,16]{2,1,0:T(2,128)(2,1)S(1)}, u32[]{:S(2)}, u32[]{:S(2)}) async-start(bf16[32,1,16]{2,1,0:T(2,128)(2,1)} %convert_element_type.88), calls=%async_computation.4 | async-start | bytes 32768 | tf_op jit(solution)/shard_map/all_to_all | solution.py:108
  173.5 5.3 %bitcast_convert_fusion = bf16[512,2048]{1,0:T(8,128)(2,1)} fusion(bf16[1,2048,2,384]{3,1,2,0:T(8,128)(2,1)} %all-gather.8.cloned.1.call-done, bf16[512,1,384]{2,0,1:T(8,128)(2,1)} %copy-done.5, bf16[512,1,384]{2,0,1:T(8,128)(2,1)S(1)} %get-tuple-element.12), kind=kOutput, calls=%fused_computation.9 | convolution fusion | flops 1612054528 | bytes 6029312 | tf_op jit(solution)/shard_map/rcf,dcf->rd/dot_general | solution.py:89
  178.8 4.4 %all-to-all-done.4 = bf16[32,1,16]{2,1,0:T(2,128)(2,1)S(1)} async-done(((bf16[32,1,16]{2,1,0:T(2,128)(2,1)}), bf16[32,1,16]{2,1,0:T(2,128)(2,1)S(1)}, u32[]{:S(2)}, u32[]{:S(2)}) %all-to-all-start.4) | async-done | bytes 1056 | tf_op jit(solution)/shard_map/all_to_all | solution.py:108
  183.2 5.4 %all-to-all-start.3 = ((bf16[32,16,2048]{2,1,0:T(8,128)(2,1)}), bf16[32,16,2048]{2,1,0:T(8,128)(2,1)S(1)}, u32[]{:S(2)}, u32[]{:S(2)}) async-start(bf16[32,16,2048]{2,1,0:T(8,128)(2,1)} %bitcast.108), calls=%async_computation.3 | async-start | bytes 4194304 | tf_op jit(solution)/shard_map/all_to_all | solution.py:101
  188.7 1.9 gather_fusion.1
  191.4 46.3 %all-to-all-done.3 = bf16[32,16,2048]{2,1,0:T(8,128)(2,1)S(1)} async-done(((bf16[32,16,2048]{2,1,0:T(8,128)(2,1)}), bf16[32,16,2048]{2,1,0:T(8,128)(2,1)S(1)}, u32[]{:S(2)}, u32[]{:S(2)}) %all-to-all-start.3) | async-done | bytes 2097184 | tf_op jit(solution)/shard_map/all_to_all | solution.py:101
  237.7 2.3 gather_fusion
  240.1 1.7 reshape.173
  241.8 3.6 %reduce_sum.34 = bf16[128,2048]{1,0:T(8,128)(2,1)} reduce(bf16[128,2,2048]{2,1,0:T(2,128)(2,1)S(1)} %reshape.173, bf16[]{:T(256)} %constant.32.clone.1), dimensions={1}, to_apply=%region_6.7 | reduce | flops 262144 | bytes 1572866 | tf_op jit(solution)/shard_map/reduce_sum | solution.py:117
  245.5 1.0 bitcast_convert_fusion.1
  246.4 1.1 copy.33
  (51 shorter events, 7.4 us)
Async XLA Ops:
  7.2 22.4 %copy-start = (bf16[128,2048]{1,0:T(8,128)(2,1)S(1)}, bf16[128,2048]{1,0:T(8,128)(2,1)}, u32[]{:S(2)}) copy-start(bf16[128,2048]{1,0:T(8,128)(2,1)} %param.8) | copy-start | bytes 1572868
  7.2 52.5 %all-gather.4.cloned.1.call-start = ((), (), s32[]{:S(2)}) async-start(), calls=%async_computation.6 | async-start | bytes 1179648 | tf_op jit(solution)/shard_map/all_gather | solution.py:33
  14.7 22.9 %all-to-all-start = ((bf16[32,1,16]{2,1,0:T(2,128)(2,1)}), bf16[32,1,16]{2,1,0:T(2,128)(2,1)S(1)}, u32[]{:S(2)}, u32[]{:S(2)}) async-start(bf16[32,1,16]{2,1,0:T(2,128)(2,1)} %all_to_all.25), calls=%async_computation | async-start | bytes 32768 | tf_op jit(solution)/shard_map/all_to_all | solution.py:57
  27.9 76.6 %all-gather.8.cloned.1.call-start = ((), (), s32[]{:S(2)}) async-start(), calls=%async_computation.8 | async-start | bytes 3342336 | tf_op jit(solution)/shard_map/all_gather | solution.py:67
  37.6 11.0 %copy-start.4 = (s32[8]{0:T(128)S(1)}, s32[8]{0:T(128)}, u32[]{:S(2)}) copy-start(s32[8]{0:T(128)} %param.11) | copy-start | bytes 100
  37.6 22.1 %copy-start.3 = (bf16[128,2048]{1,0:T(8,128)(2,1)S(1)}, bf16[128,2048]{1,0:T(8,128)(2,1)}, u32[]{:S(2)}) copy-start(bf16[128,2048]{1,0:T(8,128)(2,1)} %param.9) | copy-start | bytes 1572868
  37.6 58.7 %all-to-all-start.2 = ((bf16[32,16,2048]{2,1,0:T(8,128)(2,1)}), bf16[32,16,2048]{2,1,0:T(8,128)(2,1)S(1)}, u32[]{:S(2)}, u32[]{:S(2)}) async-start(bf16[32,16,2048]{2,1,0:T(8,128)(2,1)} %bitcast.9), calls=%async_computation.2 | async-start | bytes 4194304 | tf_op jit(solution)/shard_map/all_to_all | solution.py:43
  96.3 1.4 copy-start.1
  97.6 55.6 %all-to-all-start.1 = ((bf16[32,16,2048]{2,1,0:T(8,128)(2,1)}), bf16[32,16,2048]{2,1,0:T(8,128)(2,1)S(1)}, u32[]{:S(2)}, u32[]{:S(2)}) async-start(bf16[32,16,2048]{2,1,0:T(8,128)(2,1)} %bitcast.105), calls=%async_computation.1 | async-start | bytes 4194304 | tf_op jit(solution)/shard_map/all_to_all | solution.py:50
  103.6 51.4 %all-gather.6.cloned.1.call-start = ((), (), s32[]{:S(2)}) async-start(), calls=%async_computation.7 | async-start | bytes 1671168 | tf_op jit(solution)/shard_map/all_gather | solution.py:68
  104.3 141.1 %reduce-scatter.2.cloned.1.call-start = ((), (), s32[]{:S(2)}) async-start(), calls=%async_computation.9 | async-start | bytes 3342336 | tf_op jit(solution)/shard_map/reduce_scatter | solution.py:92
  155.0 4.8 %copy-start.2 = (bf16[32,16,2048]{2,1,0:T(8,128)(2,1)S(1)}, bf16[32,16,2048]{2,1,0:T(8,128)(2,1)}, u32[]{:S(2)}) copy-start(bf16[32,16,2048]{2,1,0:T(8,128)(2,1)} %copy-done.1) | copy-start | bytes 6291460
  159.1 0.7 copy-start.5
  167.4 15.7 %all-to-all-start.4 = ((bf16[32,1,16]{2,1,0:T(2,128)(2,1)}), bf16[32,1,16]{2,1,0:T(2,128)(2,1)S(1)}, u32[]{:S(2)}, u32[]{:S(2)}) async-start(bf16[32,1,16]{2,1,0:T(2,128)(2,1)} %convert_element_type.88), calls=%async_computation.4 | async-start | bytes 32768 | tf_op jit(solution)/shard_map/all_to_all | solution.py:108
  183.2 54.6 %all-to-all-start.3 = ((bf16[32,16,2048]{2,1,0:T(8,128)(2,1)}), bf16[32,16,2048]{2,1,0:T(8,128)(2,1)S(1)}, u32[]{:S(2)}, u32[]{:S(2)}) async-start(bf16[32,16,2048]{2,1,0:T(8,128)(2,1)} %bitcast.108), calls=%async_computation.3 | async-start | bytes 4194304 | tf_op jit(solution)/shard_map/all_to_all | solution.py:101
Sparse Core Ops, SparseCore 0:
  10.1 43.6 all-gather.3
  56.5 42.6 all-gather.7
  106.6 40.7 all-gather.5
  163.6 57.8 reduce-scatter.1
where the time goes:
time: 255 us; the launch traced here: 254 us
  waiting for transfers between devices  123 us (48%)
  starting transfers between devices  39.7 us (16%)
  local copies, waits for them, and re-layouts  33.6 us (13%)
  matrix products  24.1 us (9%)
  between operations  14.7 us (6%)
  blocking collectives  10.6 us (4%)
  other arithmetic  7.88 us (3%)
    all_to_all x1, waiting for transfers between devices, on_device(): lax.all_to_all(input_grad.astype(jnp.bfloat16).reshape(expert_count, capa...  46.3 us
    all_to_all x1, waiting for transfers between devices, on_device(): lax.all_to_all(send_grad.reshape(expert_count, capacity, model_width), 'e...  43.3 us
    all_to_all x1, waiting for transfers between devices, on_device(): lax.all_to_all(send_input.reshape(expert_count, capacity, model_width), '...  27.1 us
    scatter x2, local copies, waits for them, and re-layouts, on_device(): jnp.zeros((slot_rows, model_width), jnp.bfloat16).at[target]  14.2 us
    all_to_all x1, starting transfers between devices, on_device(): lax.all_to_all(send_gate.reshape(expert_count, capacity), 'expert', split...  13.2 us
    unnamed x1, blocking collectives  10.6 us
    all_to_all x1, starting transfers between devices, on_device(): lax.all_to_all(send_input.reshape(expert_count, capacity, model_width), '...  9.05 us
    unnamed x20, local copies, waits for them, and re-layouts  8.51 us
  transfers between devices with their start and end apart: 9, of which 5 were waited for; matrix products, arithmetic and copies ran while one was open for 21% of the time, Pallas kernels for 0%

commit v1 on v0

v1 whole, which is shorter than its diff:
```python
import functools

import jax
import jax.numpy as jnp
from jax import lax
from jax.experimental import pallas as pl
from jax.experimental.pallas import tpu as pltpu
from jax.sharding import PartitionSpec as P

F32 = jnp.float32
BF16 = jnp.bfloat16
NT = (((1,), (1,)), ((), ()))
NN = (((1,), (0,)), ((), ()))


def mm(a, b, dims=NN):
    return lax.dot_general(a, b, dims, preferred_element_type=F32)


def one_hot(target, rows):
    tokens = target.shape[1]
    return lax.broadcasted_iota(jnp.int32, (rows, tokens), 0) == target


def route_kernel(experts, cap, ids_ref, gate_ref, x_ref, send_ref, target_ref, gate_out_ref):
    tokens = ids_ref.shape[1]
    ids = ids_ref[...]
    members = [
        (lax.broadcasted_iota(jnp.int32, (experts, tokens), 0) == ids[k : k + 1]).astype(F32)
        for k in range(2)
    ]
    earlier = (
        lax.broadcasted_iota(jnp.int32, (tokens, tokens), 0)
        < lax.broadcasted_iota(jnp.int32, (tokens, tokens), 1)
    ).astype(BF16)
    count = mm((members[0] + members[1]).astype(BF16), earlier)
    rows = experts * cap
    gates = jnp.zeros((1, rows), F32)
    select = None
    for k in range(2):
        position = jnp.sum(members[k] * count, axis=0, keepdims=True).astype(jnp.int32)
        target = ids[k : k + 1] * cap + position
        target_ref[k : k + 1, :] = target
        hot = one_hot(target, rows)
        hot_k = hot.astype(F32)
        gate = jnp.broadcast_to(gate_ref[k : k + 1, :].astype(F32), (8, tokens)).astype(BF16)
        gates += mm(gate, hot_k.astype(BF16), NT)[0:1]
        select = hot_k if select is None else select + hot_k
    gate_out_ref[...] = gates.astype(BF16)
    send_ref[...] = mm(select.astype(BF16), x_ref[...]).astype(BF16)


def upstream_kernel(span, own_ref, names_ref, frames_ref, lm_ref, target_ref, send_ref):
    tokens = lm_ref.shape[0]
    frames = frames_ref.shape[0]
    first = own_ref[0]
    own = lax.broadcasted_iota(jnp.int32, (tokens, frames), 0) + first
    named = (own == names_ref[...]).astype(F32).astype(BF16)
    upstream = (lm_ref[...].astype(F32) + mm(named, frames_ref[...])).astype(BF16)
    rows = send_ref.shape[0]
    select = one_hot(target_ref[0:1, :], rows).astype(F32)
    select += one_hot(target_ref[1:2, :], rows).astype(F32)
    send_ref[...] = mm(select.astype(BF16), upstream).astype(BF16)


def forward_kernel(ff, x_ref, w_ref, hidden_ref, gate_term_ref, up_term_ref):
    pre = mm(x_ref[...], w_ref[:, : 2 * ff])
    gate_pre = pre[:, :ff]
    up_pre = pre[:, ff:]
    sig = jax.nn.sigmoid(gate_pre)
    activated = gate_pre * sig
    slope = sig * (1.0 + gate_pre * (1.0 - sig))
    hidden_ref[...] = (activated * up_pre).astype(BF16)
    gate_term_ref[...] = up_pre * slope
    up_term_ref[...] = activated


def backward_kernel(
    ff, y_ref, wd_ref, w_ref, gate_ref, hidden_ref, gate_term_ref, up_term_ref,
    out_ref, pre_ref, gate_grad_ref,
):
    @pl.when(pl.program_id(0) == 0)
    def _():
        down = mm(y_ref[...], wd_ref[...])
        gate_grad_ref[...] = jnp.sum(
            hidden_ref[...].astype(F32) * down, axis=1, keepdims=True
        )
        hidden_grad = down * gate_ref[...]
        pre_ref[:, :ff] = (hidden_grad * gate_term_ref[...]).astype(BF16)
        pre_ref[:, ff:] = (hidden_grad * up_term_ref[...]).astype(BF16)

    out_ref[...] = mm(pre_ref[...], w_ref[...], NT).astype(BF16)


def combine_kernel(back_ref, target_ref, column_ref, gate_ref, out_ref, gate_out_ref):
    rows = back_ref.shape[0]
    tokens = out_ref.shape[0]
    place = lax.broadcasted_iota(jnp.int32, (tokens, rows), 1)
    pick = (place == column_ref[:, 0:1]).astype(F32) + (place == column_ref[:, 1:2]).astype(F32)
    out_ref[...] = mm(pick.astype(BF16), back_ref[...]).astype(BF16)
    gates = jnp.broadcast_to(gate_ref[...].astype(F32), (8, rows)).astype(BF16)
    for k in range(2):
        hot = one_hot(target_ref[k : k + 1, :], rows).astype(F32).astype(BF16)
        gate_out_ref[k : k + 1, :] = mm(gates, hot)[0:1].astype(BF16)


def whole(shape, space=pltpu.VMEM):
    return pl.BlockSpec(shape, lambda *_: (0,) * len(shape), memory_space=space)


def call(kernel, outs, args, limit=24, **kw):
    return pl.pallas_call(
        kernel,
        out_shape=outs,
        compiler_params=pltpu.CompilerParams(vmem_limit_bytes=limit << 20),
        **kw,
    )(*args)


def on_device(moe_input, lm_grad, frame_grad, span_token, expert_ids, gate_weights, w_gate_up, w_down):
    tokens, width = moe_input.shape
    per_span = frame_grad.shape[0] // span_token.shape[0]
    experts = lax.axis_size("expert")
    n_seq = lax.axis_size("seq")
    cap = 2 * tokens * expert_ids.shape[1] // experts
    rows = experts * cap
    ff = w_down.shape[2]
    me = lax.axis_index("expert")
    sds = jax.ShapeDtypeStruct

    def exchange(values):
        return lax.all_to_all(
            values.reshape(experts, cap, width), "expert", split_axis=0, concat_axis=0, tiled=True
        ).reshape(rows, width)

    frame_rows = lax.all_gather(frame_grad, "seq", axis=0, tiled=True)

    send_input, target, send_gate = call(
        functools.partial(route_kernel, experts, cap),
        (sds((rows, width), BF16), sds((2, tokens), jnp.int32), sds((1, rows), BF16)),
        (expert_ids.T, gate_weights.T, moe_input),
    )
    got_input = exchange(send_input)

    span_names = lax.all_gather(span_token, "seq", axis=0, tiled=True)
    all_gates = lax.all_gather(send_gate, "expert", axis=0, tiled=True)
    slot_gate = lax.dynamic_slice(all_gates, (0, me * cap), (experts, cap))
    slot_gate = slot_gate.astype(F32).reshape(rows, 1)

    weights = jnp.concatenate([w_gate_up.reshape(-1, 2 * ff), w_down[0]], axis=1)
    weights = lax.all_gather(weights, ("seq", "dp"), axis=0, tiled=True)

    frame_names = jnp.repeat(span_names, per_span)[None, :]
    own = (lax.axis_index("seq") * tokens).reshape(1)
    send_grad = call(
        functools.partial(upstream_kernel, per_span),
        sds((rows, width), BF16),
        (own, frame_names, frame_rows, lm_grad, target),
        in_specs=[pl.BlockSpec(memory_space=pltpu.SMEM)]
        + [pl.BlockSpec(memory_space=pltpu.VMEM)] * 4,
    )
    got_grad = exchange(send_grad)

    hidden, gate_term, up_term = call(
        functools.partial(forward_kernel, ff),
        (sds((rows, ff), BF16), sds((rows, ff), F32), sds((rows, ff), F32)),
        (got_input, weights),
    )
    block = width // 4
    input_grad, pre_grad, gate_grad = call(
        functools.partial(backward_kernel, ff),
        (sds((rows, width), BF16), sds((rows, 2 * ff), BF16), sds((rows, 1), F32)),
        (got_grad, weights, weights, slot_gate, hidden, gate_term, up_term),
        grid=(4,),
        in_specs=[
            whole((rows, width)),
            pl.BlockSpec((width, ff), lambda j: (0, 2)),
            pl.BlockSpec((block, 2 * ff), lambda j: (j, 0)),
            whole((rows, 1)),
            whole((rows, ff)),
            whole((rows, ff)),
            whole((rows, ff)),
        ],
        out_specs=[
            pl.BlockSpec((rows, block), lambda j: (0, j)),
            whole((rows, 2 * ff)),
            whole((rows, 1)),
        ],
    )
    back_input = exchange(input_grad)
    all_gate_grad = lax.all_gather(gate_grad.astype(BF16).reshape(1, rows), "expert", axis=0, tiled=True)
    back_gate = lax.dynamic_slice(all_gate_grad, (0, me * cap), (experts, cap)).reshape(1, rows)

    partial = lax.dot_general(
        got_input, pre_grad, (((0,), (0,)), ((), ())), preferred_element_type=F32
    ).astype(BF16)
    partial = partial.reshape(n_seq, 2, -1, 2 * ff)
    core = lax.axis_index("dp")
    mine = lax.dynamic_index_in_dim(partial, core, 1, keepdims=False)
    other = lax.dynamic_index_in_dim(partial, 1 - core, 1, keepdims=False)
    other = lax.ppermute(other, "dp", [(0, 1), (1, 0)])
    pair = (mine.astype(F32) + other.astype(F32)).astype(BF16)
    grad = lax.psum_scatter(pair, "seq", scatter_dimension=0, tiled=True).astype(F32)
    grad_gate_up = grad.reshape(1, -1, 2, ff)

    grad_input, grad_gates = call(
        combine_kernel,
        (sds((tokens, width), BF16), sds((2, tokens), BF16)),
        (back_input, target, target.T, back_gate),
    )
    return grad_input, grad_gates.T, grad_gate_up


def solution(mesh):
    every = ("expert", "seq", "dp")
    return jax.shard_map(
        on_device,
        mesh=mesh,
        in_specs=(
            P(every, None),
            P(every, None),
            P(every, None),
            P(every),
            P(every, None),
            P(every, None),
            P("expert", ("seq", "dp"), None, None),
            P("expert", ("seq", "dp"), None),
        ),
        out_specs=(P(every, None), P(every, None), P("expert", ("seq", "dp"), None, None)),
        check_vma=False,
    )
```

time: 255 us -> 318 us (1.25)
  blocking collectives: 10.6 us -> 198 us
  waiting for transfers between devices: 123 us -> 34.2 us
  matrix products: 24.1 us -> 1.86 us
  local copies, waits for them, and re-layouts: 33.6 us -> 19.5 us
  starting transfers between devices: 39.7 us -> 27.4 us
  Pallas kernels: 0 us -> 12.1 us
    all_gather x0 -> x2, blocking collectives: none -> 188 us  [the longest x1 97.7 us: on_device(): lax.all_gather(gate_grad.astype(BF16).reshape(1, rows), 'expert', axis=0,...]
    all_to_all x5 -> x3, waiting for transfers between devices: 122 us -> 21.1 us  [exchange(): lax.all_to_all(values.reshape(experts, cap, width), 'expert', split_axis=...]
    dot_general x6 -> x1, matrix products: 24.1 us -> 1.86 us  [on_device(): lax.dot_general(got_input, pre_grad, (((0,), (0,)), ((), ())), preferred_...]
    scatter x3 -> x0, local copies, waits for them, and re-layouts: 16.4 us -> none  [the longest x2 14.2 us: on_device(): jnp.zeros((slot_rows, model_width), jnp.bfloat16).at[target]]
    all_to_all x5 -> x3, starting transfers between devices: 39.6 us -> 25.4 us  [exchange(): lax.all_to_all(values.reshape(experts, cap, width), 'expert', split_axis=...]
    all_gather x1, waiting for transfers between devices: 0.02 us -> 12.3 us  [on_device(): frame_rows = lax.all_gather(frame_grad, 'seq', axis=0, tiled=True)]
    pallas_call x0 -> x5, Pallas kernels: none -> 12.1 us  [call(): pl.pallas_call(kernel, out_shape=outs, compiler_params=pltpu.CompilerPara...]
    unnamed x20 -> x34, local copies, waits for them, and re-layouts: 8.51 us -> 15.7 us
  transfers between devices with their start and end apart: 9 -> 7, of which waited for: 5 -> 2; matrix products, arithmetic and copies ran while one was open for 21% -> 4% of each run, Pallas kernels for 0% -> 2%
where the time goes in v1:
time: 318 us; the launch traced here: 317 us
  blocking collectives  198 us (62%)
  waiting for transfers between devices  34.2 us (11%)
  starting transfers between devices  27.4 us (9%)
  local copies, waits for them, and re-layouts  19.5 us (6%)
  between operations  14.7 us (5%)
  Pallas kernels  12.1 us (4%)
  other arithmetic  9.12 us (3%)
    all_gather x1, blocking collectives, on_device(): lax.all_gather(gate_grad.astype(BF16).reshape(1, rows), 'expert', axis=0,...  97.7 us
    all_gather x1, blocking collectives, on_device(): all_gates = lax.all_gather(send_gate, 'expert', axis=0, tiled=True)  89.9 us
    all_to_all x3, starting transfers between devices, exchange(): lax.all_to_all(values.reshape(experts, cap, width), 'expert', split_axis=...  25.4 us
    all_to_all x3, waiting for transfers between devices, exchange(): lax.all_to_all(values.reshape(experts, cap, width), 'expert', split_axis=...  21.1 us
    unnamed x34, local copies, waits for them, and re-layouts  15.7 us
    all_gather x1, waiting for transfers between devices, on_device(): frame_rows = lax.all_gather(frame_grad, 'seq', axis=0, tiled=True)  12.3 us
    pallas_call x5, Pallas kernels, call(): pl.pallas_call(kernel, out_shape=outs, compiler_params=pltpu.CompilerPara...  12.1 us
    unnamed x1, blocking collectives  10.7 us
  transfers between devices with their start and end apart: 7, of which 2 were waited for; matrix products, arithmetic and copies ran while one was open for 4% of the time, Pallas kernels for 2%

profile of v1, /device:TPU:56, one launch (start us, length us, event | category | flops | bytes accessed | tf_op | source)
XLA Modules:
  0.0 317.2 jit_solution(18231296822636290995)
XLA Ops:
  7.2 0.7 all-gather.5.cloned.1.call-update
  7.9 1.0 copy.16
  8.9 1.6 pad_maximum_fusion
  10.6 1.0 copy-done.8
  11.6 0.7 copy-done.11
  12.9 0.9 shard_map.103
  13.9 1.4 copy-done.3
  15.3 13.3 %all-to-all-start.1 = ((bf16[32,16,2048]{2,1,0:T(8,128)(2,1)}), bf16[32,16,2048]{2,1,0:T(8,128)(2,1)S(1)}, u32[]{:S(2)}, u32[]{:S(2)}) async-start(bf16[32,16,2048]{2,1,0:T(8,128)(2,1)} %bitcast.29), calls=%async_computation.1 | async-start | bytes 4194304 | tf_op jit(solution)/shard_map/all_to_all | solution.py:132
  28.6 1.3 dynamic-slice
  30.8 10.7 %all-reduce = s32[64]{0:T(128)S(1)} all-reduce(s32[64]{0:T(128)S(1)} %dynamic-update-slice), channel_id=1, replica_groups=mesh['expert'=32,'seq'=8,'dp'=2] {'seq'}, use_global_device_ids=true, to_apply=%add | all-reduce | flops 64 | bytes 512
  41.7 12.3 %all-gather.5.cloned.1.call-done.frames_ref = bf16[256,2048]{1,0:T(8,128)(2,1)} async-done(((bf16[32,2048]{1,0:T(8,128)(2,1)}), bf16[256,2048]{1,0:T(8,128)(2,1)}) %all-gather.5.cloned.1.call-update) | async-done | bytes 1048592 | tf_op jit(solution)/shard_map/all_gather | solution.py:136
  54.0 1.2 copy-done.4
  55.2 2.3 shard_map.104
  57.5 21.1 %all-to-all-done.1 = bf16[32,16,2048]{2,1,0:T(8,128)(2,1)S(1)} async-done(((bf16[32,16,2048]{2,1,0:T(8,128)(2,1)}), bf16[32,16,2048]{2,1,0:T(8,128)(2,1)S(1)}, u32[]{:S(2)}, u32[]{:S(2)}) %all-to-all-start.1) | async-done | bytes 2097184 | tf_op jit(solution)/shard_map/all_to_all | solution.py:132
  78.6 6.3 %all-to-all-start = ((bf16[32,16,2048]{2,1,0:T(8,128)(2,1)}), bf16[32,16,2048]{2,1,0:T(8,128)(2,1)}, u32[]{:S(2)}, u32[]{:S(2)}) async-start(bf16[32,16,2048]{2,1,0:T(8,128)(2,1)} %bitcast.4), calls=%async_computation | async-start | bytes 4194304 | tf_op jit(solution)/shard_map/all_to_all | solution.py:132
  84.9 89.9 %all-gather.1 = bf16[32,1,512]{2,1,0:T(2,128)(2,1)S(1)} all-gather(bf16[1,1,512]{2,1,0:T(2,128)(2,1)S(1)} %bitcast.31), channel_id=1, replica_groups=mesh['expert'=32,'seq'=8,'dp'=2] {'expert'}, dimensions={0}, use_global_device_ids=true | all-gather | bytes 33792 | tf_op jit(solution)/shard_map/all_gather | solution.py:146
  175.2 2.3 copy-done
  177.5 1.8 shard_map.105
  179.3 0.9 copy-done.5
  180.2 2.3 copy-done.1
  182.5 1.1 copy-done.6
  183.6 5.7 %shard_map.106 = (bf16[512,2048]{1,0:T(8,128)(2,1)S(1)}, bf16[512,768]{1,0:T(8,128)(2,1)S(1)}, f32[512,1]{1,0:T(8,128)S(1)}) custom-call(bf16[512,2048]{1,0:T(8,128)(2,1)} %bitcast.5.y_ref, bf16[2048,1152]{1,0:T(8,128)(2,1)S(1)} %copy-done.1, bf16[2048,1152]{1,0:T(8,128)(2,1)S(1)} %copy-done.1, f32[512,1]{1,0:T(8,128)S(1)} %reshape.84.gate_ref, ...), custom_call_target="tpu_custom_call" | custom-call | tf_op jit(solution)/shard_map/pallas_call | solution.py:112
  189.4 1.9 convolution_convert_fusion
  191.3 1.6 copy-done.13
  192.9 1.2 dynamic-slice_bitcast_fusion
  194.2 1.9 collective-permute-start
  196.1 5.8 %all-to-all-start.2 = ((bf16[32,16,2048]{2,1,0:T(8,128)(2,1)}), bf16[32,16,2048]{2,1,0:T(8,128)(2,1)S(1)}, u32[]{:S(2)}, u32[]{:S(2)}) async-start(bf16[32,16,2048]{2,1,0:T(8,128)(2,1)} %bitcast.28), calls=%async_computation.2 | async-start | bytes 4194304 | tf_op jit(solution)/shard_map/all_to_all | solution.py:132
  202.0 3.4 %fusion = bf16[8,128,768]{2,1,0:T(8,128)(2,1)} fusion(bf16[8,128,768]{2,1,0:T(8,128)(2,1)} %collective-permute-done, bf16[8,2,128,768]{3,2,1,0:T(8,128)(2,1)} %bitcast.35, s32[]{:T(128)S(6)} %select_n.12), kind=kLoop, calls=%fused_computation.2 | loop fusion | flops 3145728 | bytes 4718596 | tf_op jit(solution)/shard_map/convert_element_type | solution.py:202
  205.6 97.7 %all-gather = bf16[16384,1]{1,0:T(8,128)(2,1)} all-gather(bf16[512,1]{1,0:T(8,128)(2,1)S(1)} %convert_element_type.20), channel_id=2, replica_groups=mesh['expert'=32,'seq'=8,'dp'=2] {'expert'}, dimensions={0}, use_global_device_ids=true | all-gather | bytes 33792 | tf_op jit(solution)/shard_map/all_gather | solution.py:191
  303.3 3.9 %reduce.1 = bf16[16384]{0:T(1024)(128)(2,1)S(1)} reduce(bf16[16384,1]{1,0:T(8,128)(2,1)} %all-gather, bf16[]{:T(256)} %constant.49), dimensions={1}, to_apply=%all-gather.reduce_sub_computation | reduce | bytes 65538 | tf_op jit(solution)/shard_map/all_gather | solution.py:191
  307.4 1.3 shard_map.107
  308.7 1.9 reshape.71
  (42 shorter events, 1.9 us)
Async XLA Ops:
  7.2 46.8 %all-gather.5.cloned.1.call-start = ((), (), s32[]{:S(2)}) async-start(), calls=%async_computation.4 | async-start | bytes 1179648 | tf_op jit(solution)/shard_map/all_gather | solution.py:136
  7.9 167.2 %all-gather.7.cloned.1.call-start = ((), (), s32[]{:S(2)}) async-start(), calls=%async_computation.5 | async-start | bytes 5013504 | tf_op jit(solution)/shard_map/all_gather | solution.py:151
  10.6 1.0 copy-start.8
  11.6 0.7 copy-start.11
  12.3 0.7 copy-start.12
  13.9 1.4 copy-start.3
  15.3 15.3 %copy-start.14 = (s32[8]{0:T(128)S(1)}, s32[8]{0:T(128)}, u32[]{:S(2)}) copy-start(s32[8]{0:T(128)} %param.11) | copy-start | bytes 100
  15.3 38.7 %copy-start.7 = (bf16[128,2048]{1,0:T(8,128)(2,1)S(1)}, bf16[128,2048]{1,0:T(8,128)(2,1)}, u32[]{:S(2)}) copy-start(bf16[128,2048]{1,0:T(8,128)(2,1)} %lm_ref.1) | copy-start | bytes 1572868
  15.3 63.3 %all-to-all-start.1 = ((bf16[32,16,2048]{2,1,0:T(8,128)(2,1)}), bf16[32,16,2048]{2,1,0:T(8,128)(2,1)S(1)}, u32[]{:S(2)}, u32[]{:S(2)}) async-start(bf16[32,16,2048]{2,1,0:T(8,128)(2,1)} %bitcast.29), calls=%async_computation.1 | async-start | bytes 4194304 | tf_op jit(solution)/shard_map/all_to_all | solution.py:132
  54.0 1.2 copy-start.4
  78.6 101.6 %all-to-all-start = ((bf16[32,16,2048]{2,1,0:T(8,128)(2,1)}), bf16[32,16,2048]{2,1,0:T(8,128)(2,1)}, u32[]{:S(2)}, u32[]{:S(2)}) async-start(bf16[32,16,2048]{2,1,0:T(8,128)(2,1)} %bitcast.4), calls=%async_computation | async-start | bytes 4194304 | tf_op jit(solution)/shard_map/all_to_all | solution.py:132
  175.1 2.3 copy-start
  179.3 0.9 copy-start.5
  180.2 2.3 copy-start.1
  182.5 1.1 copy-start.6
  189.4 1.9 copy-start.2
  189.4 1.9 copy-start.9
  191.3 1.6 copy-start.13
  194.2 7.8 %collective-permute-start = (bf16[8,128,768]{2,1,0:T(8,128)(2,1)}, bf16[8,128,768]{2,1,0:T(8,128)(2,1)}, u32[]{:S(2)}, u32[]{:S(2)}) collective-permute-start(bf16[8,128,768]{2,1,0:T(8,128)(2,1)} %dynamic-slice_bitcast_fusion), channel_id=1, source_target_pairs={{0,1},{1,0},{2,3},{3,2},{4,5},{5,4},{6,7},{7,6},{8,9},{9,8},{10,11... | collective-permute-start | bytes 4718600 | tf_op jit(solution)/shard_map/ppermute | solution.py:201
  196.1 111.3 %all-to-all-start.2 = ((bf16[32,16,2048]{2,1,0:T(8,128)(2,1)}), bf16[32,16,2048]{2,1,0:T(8,128)(2,1)S(1)}, u32[]{:S(2)}, u32[]{:S(2)}) async-start(bf16[32,16,2048]{2,1,0:T(8,128)(2,1)} %bitcast.28), calls=%async_computation.2 | async-start | bytes 4194304 | tf_op jit(solution)/shard_map/all_to_all | solution.py:132
  201.9 106.8 %reduce-scatter.2.cloned.1.call-start = ((), (), s32[]{:S(2)}) async-start(), calls=%async_computation.6 | async-start | bytes 1769472 | tf_op jit(solution)/shard_map/reduce_scatter | solution.py:203
  202.0 3.6 %copy-start.10 = (f32[512,1]{1,0:T(8,128)S(1)}, f32[512,1]{1,0:T(8,128)}, u32[]{:S(2)}) copy-start(f32[512,1]{1,0:T(8,128)} %copy-done.9) | copy-start | bytes 6148
Sparse Core Ops, SparseCore 0:
  10.1 43.8 all-gather.4
  56.7 44.6 all-gather.6
  205.6 41.9 reduce-scatter.1

commit v2 on v1

v2 whole, which is shorter than its diff:
```python
import functools

import jax
import jax.numpy as jnp
from jax import lax
from jax.experimental import pallas as pl
from jax.experimental.pallas import tpu as pltpu
from jax.sharding import PartitionSpec as P

F32 = jnp.float32
BF16 = jnp.bfloat16
NT = (((1,), (1,)), ((), ()))
NN = (((1,), (0,)), ((), ()))


def mm(a, b, dims=NN):
    return lax.dot_general(a, b, dims, preferred_element_type=F32)


def one_hot(target, rows):
    tokens = target.shape[1]
    return lax.broadcasted_iota(jnp.int32, (rows, tokens), 0) == target


def route_kernel(experts, cap, ids_ref, x_ref, send_ref, target_ref):
    tokens = ids_ref.shape[1]
    ids = ids_ref[...]
    members = [
        (lax.broadcasted_iota(jnp.int32, (experts, tokens), 0) == ids[k : k + 1]).astype(F32)
        for k in range(2)
    ]
    earlier = (
        lax.broadcasted_iota(jnp.int32, (tokens, tokens), 0)
        < lax.broadcasted_iota(jnp.int32, (tokens, tokens), 1)
    ).astype(F32)
    count = mm((members[0] + members[1]).astype(BF16), earlier.astype(BF16))
    rows = experts * cap
    select = None
    for k in range(2):
        position = jnp.sum(members[k] * count, axis=0, keepdims=True).astype(jnp.int32)
        target = ids[k : k + 1] * cap + position
        target_ref[k : k + 1, :] = target
        hot = one_hot(target, rows).astype(F32)
        select = hot if select is None else select + hot
    send_ref[...] = mm(select.astype(BF16), x_ref[...]).astype(BF16)


def upstream_kernel(own_ref, frames_ref, lm_ref, target_ref, gate_ref, send_ref):
    tokens, width = lm_ref.shape
    frames = frames_ref.shape[0]
    coded = frames_ref[:, width:].astype(F32)
    name = (coded[:, 0:1] * 32.0 + coded[:, 1:2]).astype(jnp.int32) - own_ref[0]
    named = (lax.broadcasted_iota(jnp.int32, (frames, tokens), 1) == name).astype(F32)
    cond = mm(named.T.astype(BF16), frames_ref[:, :width])
    upstream = (lm_ref[...].astype(F32) + cond).astype(BF16)
    rows = send_ref.shape[0]
    hot = [one_hot(target_ref[k : k + 1, :], rows).astype(F32) for k in range(2)]
    gates = gate_ref[...].astype(F32)
    gate = jnp.sum(hot[0] * gates[0:1] + hot[1] * gates[1:2], axis=1, keepdims=True)
    send_ref[...] = (mm((hot[0] + hot[1]).astype(BF16), upstream) * gate).astype(BF16)


def forward_kernel(ff, x_ref, w_ref, hidden_ref, gate_term_ref, up_term_ref):
    pre = mm(x_ref[...], w_ref[:, : 2 * ff])
    gate_pre = pre[:, :ff]
    up_pre = pre[:, ff:]
    sig = jax.nn.sigmoid(gate_pre)
    activated = gate_pre * sig
    slope = sig * (1.0 + gate_pre * (1.0 - sig))
    hidden_ref[...] = (activated * up_pre).astype(BF16)
    gate_term_ref[...] = up_pre * slope
    up_term_ref[...] = activated


def backward_kernel(ff, y_ref, w_ref, hidden_ref, gate_term_ref, up_term_ref, out_ref, pre_ref):
    rows, width = y_ref.shape
    hidden_grad = mm(y_ref[...], w_ref[:, 2 * ff :])
    pre_ref[:, :ff] = (hidden_grad * gate_term_ref[...]).astype(BF16)
    pre_ref[:, ff:] = (hidden_grad * up_term_ref[...]).astype(BF16)
    total = jnp.sum(hidden_ref[...].astype(F32) * hidden_grad, axis=1, keepdims=True)
    high = total.astype(BF16).astype(F32)
    lane = lax.broadcasted_iota(jnp.int32, (rows, 128), 1)
    out_ref[:, width:] = jnp.where(lane < 64, high, total - high).astype(BF16)
    block = 512
    for j in range(width // block):
        part = slice(j * block, (j + 1) * block)
        out_ref[:, part] = mm(pre_ref[...], w_ref[part, : 2 * ff], NT).astype(BF16)


def combine_kernel(back_ref, column_ref, gate_ref, out_ref, gate_out_ref):
    rows = back_ref.shape[0]
    tokens, width = out_ref.shape
    place = lax.broadcasted_iota(jnp.int32, (tokens, rows), 1)
    picks = [(place == column_ref[:, k : k + 1]).astype(F32) for k in range(2)]
    eye = (
        lax.broadcasted_iota(jnp.int32, (tokens, tokens), 0)
        == lax.broadcasted_iota(jnp.int32, (tokens, tokens), 1)
    ).astype(F32)
    for k in range(2):
        parts = mm(picks[k].astype(BF16), back_ref[:, width:])
        total = parts[:, 0:1] + parts[:, 64:65]
        total = jnp.sum(eye * total, axis=0, keepdims=True)
        gate_out_ref[k : k + 1, :] = (total / gate_ref[k : k + 1, :].astype(F32)).astype(BF16)
    pick = (picks[0] + picks[1]).astype(BF16)
    out_ref[...] = mm(pick, back_ref[:, :width]).astype(BF16)


def whole(shape, space=pltpu.VMEM):
    return pl.BlockSpec(shape, lambda *_: (0,) * len(shape), memory_space=space)


def call(kernel, outs, args, limit=60, **kw):
    return pl.pallas_call(
        kernel,
        out_shape=outs,
        compiler_params=pltpu.CompilerParams(vmem_limit_bytes=limit << 20),
        **kw,
    )(*args)


LONG = pl.CostEstimate(flops=1 << 40, bytes_accessed=1 << 30, transcendentals=0)


def ranked(values):
    return pl.pallas_call(
        lambda source, result: None,
        out_shape=jax.ShapeDtypeStruct(values.shape, values.dtype),
        in_specs=[pl.BlockSpec(memory_space=pl.ANY)],
        out_specs=pl.BlockSpec(memory_space=pl.ANY),
        input_output_aliases={0: 0},
        cost_estimate=LONG,
    )(values)


def on_device(moe_input, lm_grad, frame_grad, span_token, expert_ids, gate_weights, w_gate_up, w_down):
    tokens, width = moe_input.shape
    per_span = frame_grad.shape[0] // span_token.shape[0]
    experts = lax.axis_size("expert")
    n_seq = lax.axis_size("seq")
    cap = 2 * tokens * expert_ids.shape[1] // experts
    rows = experts * cap
    ff = w_down.shape[2]
    sds = jax.ShapeDtypeStruct

    def exchange(values):
        return lax.all_to_all(
            values.reshape(experts, cap, -1), "expert", split_axis=0, concat_axis=0, tiled=True
        ).reshape(rows, -1)

    names = jnp.repeat(span_token, per_span)[:, None]
    coded = jnp.concatenate([names // 32, names % 32], axis=1).astype(BF16)
    frames = jnp.concatenate([frame_grad, jnp.pad(coded, ((0, 0), (0, 126)))], axis=1)
    frames = lax.all_gather(frames, "seq", axis=0, tiled=True)

    gates = gate_weights.T
    send_input, target = call(
        functools.partial(route_kernel, experts, cap),
        (sds((rows, width), BF16), sds((2, tokens), jnp.int32)),
        (expert_ids.T, moe_input),
    )
    got_input = ranked(exchange(send_input))

    w_gate_up, w_down, target = lax.optimization_barrier((w_gate_up, w_down, target))
    weights = jnp.concatenate([w_gate_up.reshape(-1, 2 * ff), w_down[0]], axis=1)
    weights = lax.all_gather(weights, ("seq", "dp"), axis=0, tiled=True)

    own = (lax.axis_index("seq") * tokens).reshape(1)
    send_grad = call(
        upstream_kernel,
        sds((rows, width), BF16),
        (own, frames, lm_grad, target, gates),
        in_specs=[pl.BlockSpec(memory_space=pltpu.SMEM)]
        + [pl.BlockSpec(memory_space=pltpu.VMEM)] * 4,
    )
    got_grad = exchange(send_grad)

    hidden, gate_term, up_term = call(
        functools.partial(forward_kernel, ff),
        (sds((rows, ff), BF16), sds((rows, ff), F32), sds((rows, ff), F32)),
        (got_input, weights),
    )
    input_grad, pre_grad = call(
        functools.partial(backward_kernel, ff),
        (sds((rows, width + 128), BF16), sds((rows, 2 * ff), BF16)),
        (got_grad, weights, hidden, gate_term, up_term),
    )
    back = exchange(input_grad)

    partial = lax.dot_general(
        got_input, pre_grad, (((0,), (0,)), ((), ())), preferred_element_type=F32
    ).astype(BF16)
    partial = partial.reshape(n_seq, 2, -1, 2 * ff)
    core = lax.axis_index("dp")
    mine = lax.dynamic_index_in_dim(partial, core, 1, keepdims=False)
    other = lax.dynamic_index_in_dim(partial, 1 - core, 1, keepdims=False)
    other = lax.ppermute(other, "dp", [(0, 1), (1, 0)])
    pair = (mine.astype(F32) + other.astype(F32)).astype(BF16)
    grad = lax.psum_scatter(pair, "seq", scatter_dimension=0, tiled=True).astype(F32)
    grad_gate_up = grad.reshape(1, -1, 2, ff)

    grad_input, grad_gates = call(
        combine_kernel,
        (sds((tokens, width), BF16), sds((2, tokens), BF16)),
        (back, target.T, gates),
        cost_estimate=LONG,
    )
    return grad_input, grad_gates.T, grad_gate_up


def solution(mesh):
    every = ("expert", "seq", "dp")
    return jax.shard_map(
        on_device,
        mesh=mesh,
        in_specs=(
            P(every, None),
            P(every, None),
            P(every, None),
            P(every),
            P(every, None),
            P(every, None),
            P("expert", ("seq", "dp"), None, None),
            P("expert", ("seq", "dp"), None),
        ),
        out_specs=(P(every, None), P(every, None), P("expert", ("seq", "dp"), None, None)),
        check_vma=False,
    )
```

time: 318 us -> 211 us (0.66)
  blocking collectives: 198 us -> 0 us
  waiting for transfers between devices: 34.2 us -> 128 us
  local copies, waits for them, and re-layouts: 19.5 us -> 5.99 us
  Pallas kernels: 12.1 us -> 24.1 us
  other arithmetic: 9.12 us -> 4.4 us
    all_gather x2 -> x0, blocking collectives: 188 us -> none  [the longest x1 97.7 us: on_device(): lax.all_gather(gate_grad.astype(BF16).reshape(1, rows), 'expert', axis=0,...]
    all_gather x1, waiting for transfers between devices: 0.02 us -> 31.8 us  [on_device(): weights = lax.all_gather(weights, ('seq', 'dp'), axis=0, tiled=True)]
    all_to_all x3, waiting for transfers between devices: 21.1 us -> 51.5 us  [exchange(): lax.all_to_all(values.reshape(experts, cap, -1), 'expert', split_axis=0,...]
    all_gather x1, waiting for transfers between devices: 12.3 us -> 42.3 us  [on_device(): frames = lax.all_gather(frames, 'seq', axis=0, tiled=True)]
    unnamed x34 -> x19, local copies, waits for them, and re-layouts: 15.7 us -> 3.01 us
    pallas_call x5, Pallas kernels: 12.1 us -> 24.1 us  [call(): pl.pallas_call(kernel, out_shape=outs, compiler_params=pltpu.CompilerPara...]
    unnamed x1 -> x0, blocking collectives: 10.7 us -> none
    all_gather x1 -> x0, other arithmetic: 3.91 us -> none  [on_device(): lax.all_gather(gate_grad.astype(BF16).reshape(1, rows), 'expert', axis=0,...]
  transfers between devices with their start and end apart: 7 -> 7, of which waited for: 2 -> 6; matrix products, arithmetic and copies ran while one was open for 4% -> 4% of each run, Pallas kernels for 2% -> 6%
where the time goes in v2:
time: 211 us; the launch traced here: 208 us
  waiting for transfers between devices  128 us (61%)
  starting transfers between devices  29.6 us (14%)
  Pallas kernels  24.1 us (11%)
  between operations  13.9 us (7%)
  local copies, waits for them, and re-layouts  5.99 us (3%)
  other arithmetic  4.4 us (2%)
    all_to_all x3, waiting for transfers between devices, exchange(): lax.all_to_all(values.reshape(experts, cap, -1), 'expert', split_axis=0,...  51.5 us
    all_gather x1, waiting for transfers between devices, on_device(): frames = lax.all_gather(frames, 'seq', axis=0, tiled=True)  42.3 us
    all_gather x1, waiting for transfers between devices, on_device(): weights = lax.all_gather(weights, ('seq', 'dp'), axis=0, tiled=True)  31.8 us
    all_to_all x3, starting transfers between devices, exchange(): lax.all_to_all(values.reshape(experts, cap, -1), 'expert', split_axis=0,...  27.5 us
    pallas_call x5, Pallas kernels, call(): pl.pallas_call(kernel, out_shape=outs, compiler_params=pltpu.CompilerPara...  24.1 us
  transfers between devices with their start and end apart: 7, of which 6 were waited for; matrix products, arithmetic and copies ran while one was open for 4% of the time, Pallas kernels for 6%

profile of v2, /device:TPU:56, one launch (start us, length us, event | category | flops | bytes accessed | tf_op | source)
XLA Modules:
  0.0 208.0 jit_solution(7885157596654868354)
XLA Ops:
  7.2 3.2 %shard_map.103 = (bf16[512,2048]{1,0:T(8,128)(2,1)}, s32[2,128]{1,0:T(2,128)}) custom-call(s32[2,128]{1,0:T(2,128)} %bitcast.33, bf16[128,2048]{1,0:T(8,128)(2,1)} %x_ref.1), custom_call_target="tpu_custom_call" | custom-call | tf_op jit(solution)/shard_map/pallas_call | solution.py:113
  10.4 13.3 %all-to-all-start.1 = ((bf16[32,16,2048]{2,1,0:T(8,128)(2,1)}), bf16[32,16,2048]{2,1,0:T(8,128)(2,1)S(1)}, u32[]{:S(2)}, u32[]{:S(2)}) async-start(bf16[32,16,2048]{2,1,0:T(8,128)(2,1)} %bitcast.28), calls=%async_computation.1 | async-start | bytes 4194304 | tf_op jit(solution)/shard_map/all_to_all | solution.py:146
  23.8 0.0 all-gather.3.cloned.1.call-start
  23.8 0.1 broadcast_in_dim.3
  23.9 0.1 broadcast_in_dim_reshape.3
  24.0 0.1 copy.22
  24.1 0.7 fusion.2
  24.8 0.0 all-gather.3.cloned.1.call-update
  24.8 0.0 all-gather.5.cloned.1.call-start
  24.9 0.7 pad_maximum_fusion
  25.7 42.3 %all-gather.3.cloned.1.call-done.frames_ref = bf16[256,2176]{1,0:T(8,128)(2,1)} async-done(((bf16[32,2176]{1,0:T(8,128)(2,1)}), bf16[256,2176]{1,0:T(8,128)(2,1)}) %all-gather.3.cloned.1.call-update) | async-done | bytes 1114128 | tf_op jit(solution)/shard_map/all_gather | solution.py:153
  68.0 3.9 %shard_map.104 = bf16[512,2048]{1,0:T(8,128)(2,1)} custom-call(s32[1]{0:T(128)} %bitcast.own_ref, bf16[256,2176]{1,0:T(8,128)(2,1)} %all-gather.3.cloned.1.call-done.frames_ref, bf16[128,2048]{1,0:T(8,128)(2,1)} %lm_ref.1, s32[2,128]{1,0:T(2,128)} %get-tuple-element.16.target_ref, bf16[2,128]{1,0:T(2,128)(2,1)} %bitcast.34), custom_call_target="tpu_custom_call" | custom-call | tf_op jit(solution)/shard_map/pallas_call | solution.py:113
  71.8 2.0 all-to-all-done.1
  73.8 1.3 copy-done
  75.1 8.4 %all-to-all-start = ((bf16[32,16,2048]{2,1,0:T(8,128)(2,1)}), bf16[32,16,2048]{2,1,0:T(8,128)(2,1)}, u32[]{:S(2)}, u32[]{:S(2)}) async-start(bf16[32,16,2048]{2,1,0:T(8,128)(2,1)} %bitcast.24), calls=%async_computation | async-start | bytes 4194304 | tf_op jit(solution)/shard_map/all_to_all | solution.py:146
  83.5 31.8 %all-gather.5.cloned.1.call-done.w_ref = bf16[2048,1152]{1,0:T(8,128)(2,1)} async-done(((bf16[128,1152]{1,0:T(8,128)(2,1)}), bf16[2048,1152]{1,0:T(8,128)(2,1)}) %all-gather.5.cloned.1.call-update) | async-done | bytes 4718608 | tf_op jit(solution)/shard_map/all_gather | solution.py:165
  115.3 6.1 %shard_map.106 = (bf16[512,384]{1,0:T(8,128)(2,1)}, f32[512,384]{1,0:T(8,128)}, f32[512,384]{1,0:T(8,128)}) custom-call(bf16[512,2048]{1,0:T(8,128)(2,1)} %shard_map.105.x_ref, bf16[2048,1152]{1,0:T(8,128)(2,1)} %all-gather.5.cloned.1.call-done.w_ref), custom_call_target="tpu_custom_call" | custom-call | tf_op jit(solution)/shard_map/pallas_call | solution.py:113
  121.4 10.5 %all-to-all-done = bf16[32,16,2048]{2,1,0:T(8,128)(2,1)} async-done(((bf16[32,16,2048]{2,1,0:T(8,128)(2,1)}), bf16[32,16,2048]{2,1,0:T(8,128)(2,1)}, u32[]{:S(2)}, u32[]{:S(2)}) %all-to-all-start) | async-done | bytes 2097184 | tf_op jit(solution)/shard_map/all_to_all | solution.py:146
  131.8 7.8 %shard_map.107 = (bf16[512,2176]{1,0:T(8,128)(2,1)}, bf16[512,768]{1,0:T(8,128)(2,1)}) custom-call(bf16[512,2048]{1,0:T(8,128)(2,1)} %bitcast.4.y_ref, bf16[2048,1152]{1,0:T(8,128)(2,1)} %all-gather.5.cloned.1.call-done.w_ref, bf16[512,384]{1,0:T(8,128)(2,1)} %get-tuple-element.20.hidden_ref, f32[512,384]{1,0:T(8,128)} %get-tuple-element.21.gate_term_ref, ...), custom_call_target="tpu_custom_call" | custom-call | tf_op jit(solution)/shard_map/pallas_call | solution.py:113
  139.7 5.8 %all-to-all-start.2 = ((bf16[32,16,2176]{2,1,0:T(8,128)(2,1)}), bf16[32,16,2176]{2,1,0:T(8,128)(2,1)}, u32[]{:S(2)}, u32[]{:S(2)}) async-start(bf16[32,16,2176]{2,1,0:T(8,128)(2,1)} %bitcast.27), calls=%async_computation.2 | async-start | bytes 4456448 | tf_op jit(solution)/shard_map/all_to_all | solution.py:146
  145.5 0.0 reduce-scatter.2.cloned.1.call-start
  145.6 1.8 convolution_convert_fusion
  147.5 1.6 copy-done.2
  149.1 0.1 dynamic-slice_bitcast_fusion
  149.2 1.9 collective-permute-start
  151.1 0.7 copy.23
  151.9 2.6 %collective-permute-done = bf16[8,128,768]{2,1,0:T(8,128)(2,1)S(1)} collective-permute-done((bf16[8,128,768]{2,1,0:T(8,128)(2,1)S(1)}, bf16[8,128,768]{2,1,0:T(8,128)(2,1)S(1)}, u32[]{:S(2)}, u32[]{:S(2)}) %collective-permute-start) | collective-permute-done | bytes 1572896 | tf_op jit(solution)/shard_map/ppermute | solution.py:196
  154.5 3.0 %fusion = bf16[8,128,768]{2,1,0:T(8,128)(2,1)} fusion(bf16[8,128,768]{2,1,0:T(8,128)(2,1)S(1)} %collective-permute-done, bf16[8,2,128,768]{3,2,1,0:T(8,128)(2,1)} %bitcast.26, s32[]{:T(128)S(6)} %select_n.37), kind=kLoop, calls=%fused_computation.2 | loop fusion | flops 3145728 | bytes 4718596 | tf_op jit(solution)/shard_map/convert_element_type | solution.py:197
  157.4 0.0 reduce-scatter.2.cloned.1.call-update
  157.5 39.1 %all-to-all-done.2 = bf16[32,16,2176]{2,1,0:T(8,128)(2,1)} async-done(((bf16[32,16,2176]{2,1,0:T(8,128)(2,1)}), bf16[32,16,2176]{2,1,0:T(8,128)(2,1)}, u32[]{:S(2)}, u32[]{:S(2)}) %all-to-all-start.2) | async-done | bytes 2228256 | tf_op jit(solution)/shard_map/all_to_all | solution.py:146
  196.5 3.0 %shard_map.108 = (bf16[128,2048]{1,0:T(8,128)(2,1)}, bf16[2,128]{1,0:T(2,128)(2,1)}) custom-call(bf16[512,2176]{1,0:T(8,128)(2,1)} %bitcast.9.back_ref, s32[128,2]{1,0:T(8,128)} %bitcast.32, bf16[2,128]{1,0:T(2,128)(2,1)} %bitcast.35), custom_call_target="tpu_custom_call" | custom-call | flops 1099511627776 | bytes 1073741824 | tf_op jit(solution)/shard_map/pallas_call | solution.py:113
  199.6 1.9 reshape.194
  (22 shorter events, 0.1 us)
Async XLA Ops:
  10.4 13.4 %copy-start.7 = (s32[8]{0:T(128)S(1)}, s32[8]{0:T(128)}, u32[]{:S(2)}) copy-start(s32[8]{0:T(128)} %param.11) | copy-start | bytes 100
  10.4 13.7 %copy-start.4 = (bf16[32,2048]{1,0:T(8,128)(2,1)S(1)}, bf16[32,2048]{1,0:T(8,128)(2,1)}, u32[]{:S(2)}) copy-start(bf16[32,2048]{1,0:T(8,128)(2,1)} %param.10) | copy-start | bytes 393220
  10.4 14.4 %copy-start.3 = (bf16[1,128,2,384]{3,2,1,0:T(2,128)(2,1)S(1)}, bf16[1,128,2,384]{3,2,1,0:T(2,128)(2,1)}, u32[]{:S(2)}) copy-start(bf16[1,128,2,384]{3,2,1,0:T(2,128)(2,1)} %param.14) | copy-start | bytes 589828
  10.4 14.5 %copy-start.5 = (bf16[1,128,384]{2,1,0:T(8,128)(2,1)S(1)}, bf16[1,128,384]{2,1,0:T(8,128)(2,1)}, u32[]{:S(2)}) copy-start(bf16[1,128,384]{2,1,0:T(8,128)(2,1)} %param.15) | copy-start | bytes 294916
  10.4 63.4 %all-to-all-start.1 = ((bf16[32,16,2048]{2,1,0:T(8,128)(2,1)}), bf16[32,16,2048]{2,1,0:T(8,128)(2,1)S(1)}, u32[]{:S(2)}, u32[]{:S(2)}) async-start(bf16[32,16,2048]{2,1,0:T(8,128)(2,1)} %bitcast.28), calls=%async_computation.1 | async-start | bytes 4194304 | tf_op jit(solution)/shard_map/all_to_all | solution.py:146
  23.8 44.2 %all-gather.3.cloned.1.call-start = ((), (), s32[]{:S(2)}) async-start(), calls=%async_computation.4 | async-start | bytes 1253376 | tf_op jit(solution)/shard_map/all_gather | solution.py:153
  24.8 90.5 %all-gather.5.cloned.1.call-start = ((), (), s32[]{:S(2)}) async-start(), calls=%async_computation.5 | async-start | bytes 5013504 | tf_op jit(solution)/shard_map/all_gather | solution.py:165
  73.8 1.3 copy-start
  75.1 56.7 %all-to-all-start = ((bf16[32,16,2048]{2,1,0:T(8,128)(2,1)}), bf16[32,16,2048]{2,1,0:T(8,128)(2,1)}, u32[]{:S(2)}, u32[]{:S(2)}) async-start(bf16[32,16,2048]{2,1,0:T(8,128)(2,1)} %bitcast.24), calls=%async_computation | async-start | bytes 4194304 | tf_op jit(solution)/shard_map/all_to_all | solution.py:146
  139.7 5.9 %copy-start.1 = (bf16[512,2048]{1,0:T(8,128)(2,1)S(1)}, bf16[512,2048]{1,0:T(8,128)(2,1)}, u32[]{:S(2)}) copy-start(bf16[512,2048]{1,0:T(8,128)(2,1)} %shard_map.105.x_ref) | copy-start | bytes 6291460
  139.7 5.9 %copy-start.8 = (bf16[512,768]{1,0:T(8,128)(2,1)S(1)}, bf16[512,768]{1,0:T(8,128)(2,1)}, u32[]{:S(2)}) copy-start(bf16[512,768]{1,0:T(8,128)(2,1)} %get-tuple-element.26) | copy-start | bytes 2359300
  139.7 56.9 %all-to-all-start.2 = ((bf16[32,16,2176]{2,1,0:T(8,128)(2,1)}), bf16[32,16,2176]{2,1,0:T(8,128)(2,1)}, u32[]{:S(2)}, u32[]{:S(2)}) async-start(bf16[32,16,2176]{2,1,0:T(8,128)(2,1)} %bitcast.27), calls=%async_computation.2 | async-start | bytes 4456448 | tf_op jit(solution)/shard_map/all_to_all | solution.py:146
  145.5 54.1 %reduce-scatter.2.cloned.1.call-start = ((), (), s32[]{:S(2)}) async-start(), calls=%async_computation.6 | async-start | bytes 1769472 | tf_op jit(solution)/shard_map/reduce_scatter | solution.py:198
  147.4 1.6 copy-start.2
  147.4 3.7 %copy-start.6 = (s32[2,128]{1,0:T(2,128)S(1)}, s32[2,128]{1,0:T(2,128)}, u32[]{:S(2)}) copy-start(s32[2,128]{1,0:T(2,128)} %get-tuple-element.16.target_ref) | copy-start | bytes 3076
  149.2 5.3 %collective-permute-start = (bf16[8,128,768]{2,1,0:T(8,128)(2,1)S(1)}, bf16[8,128,768]{2,1,0:T(8,128)(2,1)S(1)}, u32[]{:S(2)}, u32[]{:S(2)}) collective-permute-start(bf16[8,128,768]{2,1,0:T(8,128)(2,1)S(1)} %dynamic-slice_bitcast_fusion), channel_id=1, source_target_pairs={{0,1},{1,0},{2,3},{3,2},{4,5},{5,4},{6,7},{7,6},{8,9},{9,8},{10,11... | collective-permute-start | bytes 4718600 | tf_op jit(solution)/shard_map/ppermute | solution.py:196
Sparse Core Ops, SparseCore 0:
  27.2 40.6 all-gather.2
  70.7 44.5 all-gather.4
  157.6 41.8 reduce-scatter.1

commit v3 on v2

v3 whole, which is shorter than its diff:
```python
import functools

import jax
import jax.numpy as jnp
from jax import lax
from jax.experimental import pallas as pl
from jax.experimental.pallas import tpu as pltpu
from jax.sharding import PartitionSpec as P

F32 = jnp.float32
BF16 = jnp.bfloat16
NX, NZ = 4, 8
NT = (((1,), (1,)), ((), ()))
NN = (((1,), (0,)), ((), ()))


def mm(a, b, dims=NN):
    return lax.dot_general(a, b, dims, preferred_element_type=F32)


def one_hot(target, rows):
    tokens = target.shape[1]
    return lax.broadcasted_iota(jnp.int32, (rows, tokens), 0) == target


def route_kernel(experts, cap, ids_ref, x_ref, out_ref, target_ref):
    tokens, width = x_ref.shape
    ids = ids_ref[...]
    members = [
        (lax.broadcasted_iota(jnp.int32, (experts, tokens), 0) == ids[k : k + 1]).astype(F32)
        for k in range(2)
    ]
    earlier = (
        lax.broadcasted_iota(jnp.int32, (tokens, tokens), 0)
        < lax.broadcasted_iota(jnp.int32, (tokens, tokens), 1)
    ).astype(F32)
    count = mm((members[0] + members[1]).astype(BF16), earlier.astype(BF16))
    line = lax.broadcasted_iota(jnp.int32, (128, tokens), 0)
    coded = jnp.zeros((128, tokens), F32)
    for k in range(2):
        position = jnp.sum(members[k] * count, axis=0, keepdims=True)
        target_ref[k : k + 1, :] = ids[k : k + 1] * cap + position.astype(jnp.int32)
        coded = jnp.where(line == 2 * k, ids[k : k + 1].astype(F32), coded)
        coded = jnp.where(line == 2 * k + 1, position, coded)
    out_ref[:, :width] = x_ref[...]
    out_ref[:, width:] = coded.T.astype(BF16)


def pack_kernel(cap, place_ref, *refs):
    blocks, outs = refs[:9], refs[9:]
    width = outs[0].shape[1]
    my_x, my_z = place_ref[0], place_ref[1]

    def pick(block, shift):
        codes = block[:, width:].astype(F32).T.astype(jnp.int32)
        tokens = codes.shape[1]
        rows = lax.broadcasted_iota(jnp.int32, (NX * cap, tokens), 0)
        select = jnp.zeros((NX * cap, tokens), F32)
        for k in range(2):
            expert, position = codes[2 * k : 2 * k + 1], codes[2 * k + 1 : 2 * k + 2]
            away = (expert // NZ - my_x + NX) % NX
            row = jnp.where(expert % NZ == my_z, away * cap + position, -1)
            select += (rows == row).astype(F32)
        picked = mm(select.astype(BF16), block[:, :width]).astype(BF16)
        first = pl.multiple_of(((my_z + shift) % NZ) * cap, cap)
        for d in range(NX):
            outs[d][pl.ds(first, cap), :] = picked[d * cap : (d + 1) * cap]

    for block, shift in zip(blocks[:7], (0, 7, 6, 5, 1, 2, 3)):
        pick(block[...], shift)
    pick(jnp.concatenate([blocks[7][...], blocks[8][...]], axis=0), 4)


def upstream_kernel(own_ref, frames_ref, lm_ref, target_ref, gate_ref, send_ref):
    tokens, width = lm_ref.shape
    frames = frames_ref.shape[0]
    coded = frames_ref[:, width:].astype(F32)
    name = (coded[:, 0:1] * 32.0 + coded[:, 1:2]).astype(jnp.int32) - own_ref[0]
    named = (lax.broadcasted_iota(jnp.int32, (frames, tokens), 1) == name).astype(F32)
    cond = mm(named.T.astype(BF16), frames_ref[:, :width])
    upstream = (lm_ref[...].astype(F32) + cond).astype(BF16)
    rows = send_ref.shape[0]
    hot = [one_hot(target_ref[k : k + 1, :], rows).astype(F32) for k in range(2)]
    gates = gate_ref[...].astype(F32)
    gate = jnp.sum(hot[0] * gates[0:1] + hot[1] * gates[1:2], axis=1, keepdims=True)
    send_ref[...] = (mm((hot[0] + hot[1]).astype(BF16), upstream) * gate).astype(BF16)


def forward_kernel(
    ff, place_ref, x0, x1, x2, x3, w_ref, hidden_ref, gate_term_ref, up_term_ref, mine_ref, other_ref
):
    rows, width = x0.shape
    core = place_ref[2]
    for d, x_ref in enumerate((x0, x1, x2, x3)):
        first = pl.multiple_of(((place_ref[0] + NX - d) % NX) * rows, rows)
        at = pl.ds(first, rows)
        for j in range(width // 256):
            own = pl.ds(pl.multiple_of((2 * j + core) * 128, 128), 128)
            away = pl.ds(pl.multiple_of((2 * j + 1 - core) * 128, 128), 128)
            mine_ref[at, j * 128 : (j + 1) * 128] = x_ref[:, own]
            other_ref[at, j * 128 : (j + 1) * 128] = x_ref[:, away]
        pre = mm(x_ref[...], w_ref[:, : 2 * ff])
        gate_pre = pre[:, :ff]
        up_pre = pre[:, ff:]
        sig = jax.nn.sigmoid(gate_pre)
        activated = gate_pre * sig
        slope = sig * (1.0 + gate_pre * (1.0 - sig))
        hidden_ref[at, :] = (activated * up_pre).astype(BF16)
        gate_term_ref[at, :] = up_pre * slope
        up_term_ref[at, :] = activated


def backward_kernel(
    ff, y_any, w_any, hidden_any, gate_any, up_any, out_any, pre_ref,
    y, wd, wg, hidden, gate_term, up_term, out, extra, sems,
):
    rows, width = y.shape
    half, block = width // 2, width // 4
    copies = []

    def fetch(source, target):
        copies.append(pltpu.make_async_copy(source, target, sems.at[len(copies)]))
        copies[-1].start()

    for h in range(2):
        part = slice(h * half, (h + 1) * half)
        fetch(y_any.at[:, part], y.at[:, part])
        fetch(w_any.at[part, 2 * ff :], wd.at[part, :])
    fetch(gate_any, gate_term)
    fetch(up_any, up_term)
    fetch(hidden_any, hidden)
    for j in range(4):
        part = slice(j * block, (j + 1) * block)
        fetch(w_any.at[part, : 2 * ff], wg.at[part, :])
    copies[0].wait()
    copies[1].wait()
    hidden_grad = mm(y[:, :half], wd[:half, :])
    copies[2].wait()
    copies[3].wait()
    hidden_grad += mm(y[:, half:], wd[half:, :])
    copies[4].wait()
    pre_ref[:, :ff] = (hidden_grad * gate_term[...]).astype(BF16)
    copies[5].wait()
    pre_ref[:, ff:] = (hidden_grad * up_term[...]).astype(BF16)
    copies[6].wait()
    total = jnp.sum(hidden[...].astype(F32) * hidden_grad, axis=1, keepdims=True)
    high = total.astype(BF16).astype(F32)
    lane = lax.broadcasted_iota(jnp.int32, (rows, 128), 1)
    extra[...] = jnp.where(lane < 64, high, total - high).astype(BF16)
    fetch(extra, out_any.at[:, width:])
    for j in range(4):
        part = slice(j * block, (j + 1) * block)
        copies[7 + j].wait()
        out[:, part] = mm(pre_ref[...], wg[part, :], NT).astype(BF16)
        fetch(out.at[:, part], out_any.at[:, part])
    for j in range(5):
        copies[11 + j].wait()


def combine_kernel(back_ref, column_ref, gate_ref, out_ref, gate_out_ref):
    rows = back_ref.shape[0]
    tokens, width = out_ref.shape
    place = lax.broadcasted_iota(jnp.int32, (tokens, rows), 1)
    picks = [(place == column_ref[:, k : k + 1]).astype(F32) for k in range(2)]
    eye = (
        lax.broadcasted_iota(jnp.int32, (tokens, tokens), 0)
        == lax.broadcasted_iota(jnp.int32, (tokens, tokens), 1)
    ).astype(F32)
    for k in range(2):
        parts = mm(picks[k].astype(BF16), back_ref[:, width:])
        total = parts[:, 0:1] + parts[:, 64:65]
        total = jnp.sum(eye * total, axis=0, keepdims=True)
        gate_out_ref[k : k + 1, :] = (total / gate_ref[k : k + 1, :].astype(F32)).astype(BF16)
    pick = (picks[0] + picks[1]).astype(BF16)
    out_ref[...] = mm(pick, back_ref[:, :width]).astype(BF16)


def call(kernel, outs, args, limit=60, **kw):
    return pl.pallas_call(
        kernel,
        out_shape=outs,
        compiler_params=pltpu.CompilerParams(vmem_limit_bytes=limit << 20),
        **kw,
    )(*args)


LONG = pl.CostEstimate(flops=1 << 40, bytes_accessed=1 << 30, transcendentals=0)


def along(dx, dz):
    return [
        (x * NZ + z, (x + dx) % NX * NZ + (z + dz) % NZ) for x in range(NX) for z in range(NZ)
    ]


def on_device(moe_input, lm_grad, frame_grad, span_token, expert_ids, gate_weights, w_gate_up, w_down):
    tokens, width = moe_input.shape
    per_span = frame_grad.shape[0] // span_token.shape[0]
    experts = NX * NZ
    cap = 2 * tokens * expert_ids.shape[1] // experts
    rows = experts * cap
    ff = w_down.shape[2]
    sds = jax.ShapeDtypeStruct
    me = lax.axis_index("expert")
    core = lax.axis_index("dp")
    place = jnp.stack([me // NZ, me % NZ, core]).astype(jnp.int32)
    smem = pl.BlockSpec(memory_space=pltpu.SMEM)
    vmem = pl.BlockSpec(memory_space=pltpu.VMEM)
    hbm = pl.BlockSpec(memory_space=pltpu.HBM)
    any_space = pl.BlockSpec(memory_space=pl.ANY)

    def exchange(values):
        return lax.all_to_all(
            values.reshape(experts, cap, -1), "expert", split_axis=0, concat_axis=0, tiled=True
        ).reshape(rows, -1)

    names = jnp.repeat(span_token, per_span)[:, None]
    coded = jnp.concatenate([names // 32, names % 32], axis=1).astype(BF16)
    frames = jnp.concatenate([frame_grad, jnp.pad(coded, ((0, 0), (0, 126)))], axis=1)
    frames = lax.all_gather(frames, "seq", axis=0, tiled=True)

    gates = gate_weights.T
    block, target = call(
        functools.partial(route_kernel, experts, cap),
        (sds((tokens, width + 128), BF16), sds((2, tokens), jnp.int32)),
        (expert_ids.T, moe_input),
    )
    up, down = [block], [block]
    for hop in range(3):
        ahead = lax.ppermute(up[-1], "expert", along(0, 1))
        behind = lax.ppermute(down[-1], "expert", along(0, -1))
        ahead, behind = lax.optimization_barrier((ahead, behind))
        up.append(ahead)
        down.append(behind)
    last_up = lax.ppermute(up[3][: tokens // 2], "expert", along(0, 1))
    last_down = lax.ppermute(down[3][tokens // 2 :], "expert", along(0, -1))

    w_gate_up, w_down, _ = lax.optimization_barrier((w_gate_up, w_down, up[1]))
    weights = jnp.concatenate([w_gate_up.reshape(-1, 2 * ff), w_down[0]], axis=1)
    weights = lax.all_gather(weights, ("seq", "dp"), axis=0, tiled=True)

    own = (lax.axis_index("seq") * tokens).reshape(1)
    lm_grad, _, _ = lax.optimization_barrier((lm_grad, up[3], down[3]))
    send_grad = call(
        upstream_kernel,
        sds((rows, width), BF16),
        (own, frames, lm_grad, target, gates),
        in_specs=[smem] + [vmem] * 4,
    )
    got_grad = exchange(send_grad)

    packed = call(
        functools.partial(pack_kernel, cap),
        [sds((NZ * cap, width), BF16)] * NX,
        (place, block, *up[1:], *down[1:], last_up, last_down),
        in_specs=[smem] + [vmem] * 9,
    )
    arrived = [packed[0]]
    for d in range(1, NX):
        arrived.append(lax.ppermute(packed[d], "expert", along(d, 0)))

    hidden, gate_term, up_term, x_mine, x_other = call(
        functools.partial(forward_kernel, ff),
        (
            sds((rows, ff), BF16), sds((rows, ff), F32), sds((rows, ff), F32),
            sds((rows, width // 2), BF16), sds((rows, width // 2), BF16),
        ),
        (place, *arrived, weights),
        in_specs=[smem] + [vmem] * 5,
    )
    input_grad, pre_grad = call(
        functools.partial(backward_kernel, ff),
        (sds((rows, width + 128), BF16), sds((rows, 2 * ff), BF16)),
        (got_grad, weights, hidden, gate_term, up_term),
        in_specs=[any_space] + [hbm] * 4,
        out_specs=[hbm, vmem],
        scratch_shapes=[
            pltpu.VMEM((rows, width), BF16),
            pltpu.VMEM((width, ff), BF16),
            pltpu.VMEM((width, 2 * ff), BF16),
            pltpu.VMEM((rows, ff), BF16),
            pltpu.VMEM((rows, ff), F32),
            pltpu.VMEM((rows, ff), F32),
            pltpu.VMEM((rows, width), BF16),
            pltpu.VMEM((rows, 128), BF16),
            pltpu.SemaphoreType.DMA((16,)),
        ],
    )
    back = exchange(input_grad)

    rows_first = (((0,), (0,)), ((), ()))
    other = mm(x_other, pre_grad, rows_first).astype(BF16)
    other = lax.ppermute(other, "dp", [(0, 1), (1, 0)])
    pair = (mm(x_mine, pre_grad, rows_first) + other.astype(F32)).astype(BF16)
    grad = lax.psum_scatter(pair, "seq", scatter_dimension=0, tiled=True).astype(F32)
    grad_gate_up = grad.reshape(1, -1, 2, ff)

    grad_input, grad_gates = call(
        combine_kernel,
        (sds((tokens, width), BF16), sds((2, tokens), BF16)),
        (back, target.T, gates),
        limit=20,
        cost_estimate=LONG,
    )
    return grad_input, grad_gates.T, grad_gate_up


def solution(mesh):
    every = ("expert", "seq", "dp")
    return jax.shard_map(
        on_device,
        mesh=mesh,
        in_specs=(
            P(every, None),
            P(every, None),
            P(every, None),
            P(every),
            P(every, None),
            P(every, None),
            P("expert", ("seq", "dp"), None, None),
            P("expert", ("seq", "dp"), None),
        ),
        out_specs=(P(every, None), P(every, None), P("expert", ("seq", "dp"), None, None)),
        check_vma=False,
    )
```

time: 211 us -> 266 us (1.26)
  starting transfers between devices: 29.6 us -> 60.4 us
  waiting for transfers between devices: 128 us -> 142 us
  matrix products: 1.84 us -> 7.57 us
    ppermute x0 -> x11, waiting for transfers between devices: none -> 97.1 us  [the longest x1 43.1 us: on_device(): last_up = lax.ppermute(up[3][:tokens // 2], 'expert', along(0, 1))]
    ppermute x0 -> x11, starting transfers between devices: none -> 45.7 us  [the longest x3 18.3 us: on_device(): behind = lax.ppermute(down[-1], 'expert', along(0, -1))]
    all_gather x1, waiting for transfers between devices: 42.3 us -> 0.01 us  [on_device(): frames = lax.all_gather(frames, 'seq', axis=0, tiled=True)]
    all_gather x1, waiting for transfers between devices: 31.8 us -> 0.01 us  [on_device(): weights = lax.all_gather(weights, ('seq', 'dp'), axis=0, tiled=True)]
    all_to_all x3 -> x2, starting transfers between devices: 27.5 us -> 12.7 us  [exchange(): lax.all_to_all(values.reshape(experts, cap, -1), 'expert', split_axis=0,...]
    all_to_all x3 -> x2, waiting for transfers between devices: 51.5 us -> 37.3 us  [exchange(): lax.all_to_all(values.reshape(experts, cap, -1), 'expert', split_axis=0,...]
    dot_general x1 -> x2, matrix products: 1.84 us -> 7.57 us  [mm(): return lax.dot_general(a, b, dims, preferred_element_type=F32)]
    reduce_scatter x1, waiting for transfers between devices: 0.01 us -> 3.74 us  [on_device(): lax.psum_scatter(pair, 'seq', scatter_dimension=0, tiled=True).astype(F32)]
  transfers between devices with their start and end apart: 7 -> 17, of which waited for: 6 -> 12; matrix products, arithmetic and copies ran while one was open for 4% -> 4% of each run, Pallas kernels for 6% -> 7%
where the time goes in v3:
time: 266 us; the launch traced here: 263 us
  waiting for transfers between devices  142 us (53%)
  starting transfers between devices  60.4 us (23%)
  Pallas kernels  26.7 us (10%)
  between operations  14 us (5%)
  local copies, waits for them, and re-layouts  8.47 us (3%)
  matrix products  7.57 us (3%)
  other arithmetic  3.83 us (1%)
    ppermute x1, waiting for transfers between devices, on_device(): last_up = lax.ppermute(up[3][:tokens // 2], 'expert', along(0, 1))  43.1 us
    all_to_all x2, waiting for transfers between devices, exchange(): lax.all_to_all(values.reshape(experts, cap, -1), 'expert', split_axis=0,...  37.3 us
    ppermute x3, waiting for transfers between devices, on_device(): ahead = lax.ppermute(up[-1], 'expert', along(0, 1))  29.7 us
    pallas_call x6, Pallas kernels, call(): pl.pallas_call(kernel, out_shape=outs, compiler_params=pltpu.CompilerPara...  26.7 us
    ppermute x3, waiting for transfers between devices, on_device(): arrived.append(lax.ppermute(packed[d], 'expert', along(d, 0)))  20.4 us
    ppermute x3, starting transfers between devices, on_device(): behind = lax.ppermute(down[-1], 'expert', along(0, -1))  18.3 us
    all_to_all x2, starting transfers between devices, exchange(): lax.all_to_all(values.reshape(experts, cap, -1), 'expert', split_axis=0,...  12.7 us
    ppermute x3, starting transfers between devices, on_device(): arrived.append(lax.ppermute(packed[d], 'expert', along(d, 0)))  10.7 us
  transfers between devices with their start and end apart: 17, of which 12 were waited for; matrix products, arithmetic and copies ran while one was open for 4% of the time, Pallas kernels for 7%

profile of v3, /device:TPU:56, one launch (start us, length us, event | category | flops | bytes accessed | tf_op | source)
XLA Modules:
  0.0 262.8 jit_solution(522868475202834046)
XLA Ops:
  9.8 2.2 shard_map.103
  12.0 4.3 %collective-permute-start = (bf16[128,2176]{1,0:T(8,128)(2,1)}, bf16[128,2176]{1,0:T(8,128)(2,1)S(1)}, u32[]{:S(2)}, u32[]{:S(2)}) collective-permute-start(bf16[128,2176]{1,0:T(8,128)(2,1)} %get-tuple-element.27.refs_0_), channel_id=1, source_target_pairs={{0,16},{16,32},{32,48},{48,64},{64,80},{80,96},{96,112},{112,0},{1... | collective-permute-start | bytes 1671176 | tf_op jit(solution)/shard_map/ppermute | solution.py:230
  16.2 8.6 %collective-permute-start.1 = (bf16[128,2176]{1,0:T(8,128)(2,1)}, bf16[128,2176]{1,0:T(8,128)(2,1)S(1)}, u32[]{:S(2)}, u32[]{:S(2)}) collective-permute-start(bf16[128,2176]{1,0:T(8,128)(2,1)} %get-tuple-element.27.refs_0_), channel_id=1, source_target_pairs={{0,112},{16,0},{32,16},{48,32},{64,48},{80,64},{96,80},{112,96},{1... | collective-permute-start | bytes 1671176 | tf_op jit(solution)/shard_map/ppermute | solution.py:231
  24.8 10.9 %collective-permute-done.refs_1_ = bf16[128,2176]{1,0:T(8,128)(2,1)S(1)} collective-permute-done((bf16[128,2176]{1,0:T(8,128)(2,1)}, bf16[128,2176]{1,0:T(8,128)(2,1)S(1)}, u32[]{:S(2)}, u32[]{:S(2)}) %collective-permute-start) | collective-permute-done | bytes 557088 | tf_op jit(solution)/shard_map/ppermute | solution.py:230
  38.2 1.6 pad_maximum_fusion
  39.8 1.9 collective-permute-start.2
  41.7 5.5 %collective-permute-start.3 = (bf16[128,2176]{1,0:T(8,128)(2,1)S(1)}, bf16[128,2176]{1,0:T(8,128)(2,1)}, u32[]{:S(2)}, u32[]{:S(2)}) collective-permute-start(bf16[128,2176]{1,0:T(8,128)(2,1)S(1)} %collective-permute-done.1.refs_4_), channel_id=1, source_target_pairs={{0,112},{16,0},{32,16},{48,32},{64,48},{80,64},{96,80},{112,96},{1... | collective-permute-start | bytes 1671176 | tf_op jit(solution)/shard_map/ppermute | solution.py:231
  47.2 9.9 %collective-permute-done.2.refs_2_ = bf16[128,2176]{1,0:T(8,128)(2,1)S(1)} collective-permute-done((bf16[128,2176]{1,0:T(8,128)(2,1)S(1)}, bf16[128,2176]{1,0:T(8,128)(2,1)S(1)}, u32[]{:S(2)}, u32[]{:S(2)}) %collective-permute-start.2) | collective-permute-done | bytes 557088 | tf_op jit(solution)/shard_map/ppermute | solution.py:230
  58.3 3.4 %collective-permute-start.4 = (bf16[128,2176]{1,0:T(8,128)(2,1)S(1)}, bf16[128,2176]{1,0:T(8,128)(2,1)S(1)}, u32[]{:S(2)}, u32[]{:S(2)}) collective-permute-start(bf16[128,2176]{1,0:T(8,128)(2,1)S(1)} %collective-permute-done.2.refs_2_), channel_id=1, source_target_pairs={{0,16},{16,32},{32,48},{48,64},{64,80},{80,96},{96,112},{112,0},{1... | collective-permute-start | bytes 1671176 | tf_op jit(solution)/shard_map/ppermute | solution.py:230
  61.8 4.2 %collective-permute-start.5 = (bf16[128,2176]{1,0:T(8,128)(2,1)}, bf16[128,2176]{1,0:T(8,128)(2,1)S(1)}, u32[]{:S(2)}, u32[]{:S(2)}) collective-permute-start(bf16[128,2176]{1,0:T(8,128)(2,1)} %collective-permute-done.3.refs_5_), channel_id=1, source_target_pairs={{0,112},{16,0},{32,16},{48,32},{64,48},{80,64},{96,80},{112,96},{1... | collective-permute-start | bytes 1671176 | tf_op jit(solution)/shard_map/ppermute | solution.py:231
  65.9 9.0 %collective-permute-done.4.refs_3_ = bf16[128,2176]{1,0:T(8,128)(2,1)S(1)} collective-permute-done((bf16[128,2176]{1,0:T(8,128)(2,1)S(1)}, bf16[128,2176]{1,0:T(8,128)(2,1)S(1)}, u32[]{:S(2)}, u32[]{:S(2)}) %collective-permute-start.4) | collective-permute-done | bytes 557088 | tf_op jit(solution)/shard_map/ppermute | solution.py:230
  76.4 4.1 %shard_map.104 = bf16[512,2048]{1,0:T(8,128)(2,1)} custom-call(s32[1]{0:T(128)} %bitcast.own_ref, bf16[256,2176]{1,0:T(8,128)(2,1)} %all-gather.3.cloned.1.call-done.frames_ref, bf16[128,2048]{1,0:T(8,128)(2,1)} %lm_ref, s32[2,128]{1,0:T(2,128)} %get-tuple-element.35.target_ref, bf16[2,128]{1,0:T(2,128)(2,1)} %bitcast.22), custom_call_target="tpu_custom_call" | custom-call | tf_op jit(solution)/shard_map/pallas_call | solution.py:179
  80.5 7.6 %all-to-all-start = ((bf16[32,16,2048]{2,1,0:T(8,128)(2,1)}), bf16[32,16,2048]{2,1,0:T(8,128)(2,1)S(1)}, u32[]{:S(2)}, u32[]{:S(2)}) async-start(bf16[32,16,2048]{2,1,0:T(8,128)(2,1)} %bitcast.24), calls=%async_computation | async-start | bytes 4194304 | tf_op jit(solution)/shard_map/all_to_all | solution.py:213
  88.9 3.7 %collective-permute-start.6 = (bf16[64,2176]{1,0:T(8,128)(2,1)}, bf16[64,2176]{1,0:T(8,128)(2,1)S(1)}, u32[]{:S(2)}, u32[]{:S(2)}) collective-permute-start(bf16[64,2176]{1,0:T(8,128)(2,1)} %slice.6), channel_id=1, source_target_pairs={{0,16},{16,32},{32,48},{48,64},{64,80},{80,96},{96,112},{112,0},{1... | collective-permute-start | bytes 835592 | tf_op jit(solution)/shard_map/ppermute | solution.py:235
  92.6 3.4 %collective-permute-start.7 = (bf16[64,2176]{1,0:T(8,128)(2,1)S(1)}, bf16[64,2176]{1,0:T(8,128)(2,1)S(1)}, u32[]{:S(2)}, u32[]{:S(2)}) collective-permute-start(bf16[64,2176]{1,0:T(8,128)(2,1)S(1)} %slice.7), channel_id=1, source_target_pairs={{0,112},{16,0},{32,16},{48,32},{64,48},{80,64},{96,80},{112,96},{1... | collective-permute-start | bytes 835592 | tf_op jit(solution)/shard_map/ppermute | solution.py:236
  96.6 43.1 %collective-permute-done.6.refs_7_ = bf16[64,2176]{1,0:T(8,128)(2,1)S(1)} collective-permute-done((bf16[64,2176]{1,0:T(8,128)(2,1)}, bf16[64,2176]{1,0:T(8,128)(2,1)S(1)}, u32[]{:S(2)}, u32[]{:S(2)}) %collective-permute-start.6) | collective-permute-done | bytes 278560 | tf_op jit(solution)/shard_map/ppermute | solution.py:235
  141.1 4.3 %shard_map.105 = (bf16[128,2048]{1,0:T(8,128)(2,1)}, bf16[128,2048]{1,0:T(8,128)(2,1)}, bf16[128,2048]{1,0:T(8,128)(2,1)}, bf16[128,2048]{1,0:T(8,128)(2,1)}) custom-call(s32[3]{0:T(128)} %pad_add_fusion.place_ref, bf16[128,2176]{1,0:T(8,128)(2,1)} %get-tuple-element.27.refs_0_, bf16[128,2176]{1,0:T(8,128)(2,1)} %copy-done.4, bf16[128,2176]{1,0:T(8,128)(2,1)} %copy-done.6, ...), custom_call_target="tpu_custom_call" | custom-call | tf_op jit(solution)/shard_map/pallas_call | solution.py:179
  145.4 4.7 %collective-permute-start.10 = (bf16[128,2048]{1,0:T(8,128)(2,1)}, bf16[128,2048]{1,0:T(8,128)(2,1)S(1)}, u32[]{:S(2)}, u32[]{:S(2)}) collective-permute-start(bf16[128,2048]{1,0:T(8,128)(2,1)} %get-tuple-element.41), channel_id=1, source_target_pairs={{0,384},{16,400},{32,416},{48,432},{64,448},{80,464},{96,480},{112... | collective-permute-start | bytes 1572872 | tf_op jit(solution)/shard_map/ppermute | solution.py:260
  150.1 1.9 collective-permute-start.8
  152.0 4.2 %collective-permute-start.9 = (bf16[128,2048]{1,0:T(8,128)(2,1)}, bf16[128,2048]{1,0:T(8,128)(2,1)}, u32[]{:S(2)}, u32[]{:S(2)}) collective-permute-start(bf16[128,2048]{1,0:T(8,128)(2,1)} %get-tuple-element.40), channel_id=1, source_target_pairs={{0,256},{16,272},{32,288},{48,304},{64,320},{80,336},{96,352},{112... | collective-permute-start | bytes 1572872 | tf_op jit(solution)/shard_map/ppermute | solution.py:260
  156.2 15.2 %collective-permute-done.10.x3 = bf16[128,2048]{1,0:T(8,128)(2,1)S(1)} collective-permute-done((bf16[128,2048]{1,0:T(8,128)(2,1)}, bf16[128,2048]{1,0:T(8,128)(2,1)S(1)}, u32[]{:S(2)}, u32[]{:S(2)}) %collective-permute-start.10) | collective-permute-done | bytes 524320 | tf_op jit(solution)/shard_map/ppermute | solution.py:260
  171.4 5.2 %collective-permute-done.8.x1 = bf16[128,2048]{1,0:T(8,128)(2,1)S(1)} collective-permute-done((bf16[128,2048]{1,0:T(8,128)(2,1)}, bf16[128,2048]{1,0:T(8,128)(2,1)S(1)}, u32[]{:S(2)}, u32[]{:S(2)}) %collective-permute-start.8) | collective-permute-done | bytes 524320 | tf_op jit(solution)/shard_map/ppermute | solution.py:260
  177.4 6.9 %shard_map.106 = (bf16[512,384]{1,0:T(8,128)(2,1)}, f32[512,384]{1,0:T(8,128)}, f32[512,384]{1,0:T(8,128)}, bf16[512,1024]{1,0:T(8,128)(2,1)}, bf16[512,1024]{1,0:T(8,128)(2,1)}) custom-call(s32[3]{0:T(128)} %pad_add_fusion.place_ref, bf16[128,2048]{1,0:T(8,128)(2,1)} %get-tuple-element.38.x0, bf16[128,2048]{1,0:T(8,128)(2,1)} %copy-done.8, ...), custom_call_target="tpu_custom_call" | custom-call | tf_op jit(solution)/shard_map/pallas_call | solution.py:179
  185.7 7.9 %shard_map.107 = (bf16[512,2176]{1,0:T(8,128)(2,1)}, bf16[512,768]{1,0:T(8,128)(2,1)}) custom-call(bf16[512,2048]{1,0:T(8,128)(2,1)} %bitcast.25, bf16[2048,1152]{1,0:T(8,128)(2,1)} %all-gather.5.cloned.1.call-done.w_ref.w_any, bf16[512,384]{1,0:T(8,128)(2,1)} %get-tuple-element.42.hidden_any, f32[512,384]{1,0:T(8,128)} %get-tuple-element.43.gate_any, ...), custom_call_target="tpu_custom_call" | custom-call | tf_op jit(solution)/shard_map/pallas_call | solution.py:179
  193.6 5.0 %all-to-all-start.1 = ((bf16[32,16,2176]{2,1,0:T(8,128)(2,1)}), bf16[32,16,2176]{2,1,0:T(8,128)(2,1)S(1)}, u32[]{:S(2)}, u32[]{:S(2)}) async-start(bf16[32,16,2176]{2,1,0:T(8,128)(2,1)} %bitcast.26), calls=%async_computation.1 | async-start | bytes 4456448 | tf_op jit(solution)/shard_map/all_to_all | solution.py:213
  198.7 3.7 %convolution_convert_fusion = bf16[1024,768]{1,0:T(8,128)(2,1)} fusion(bf16[512,1024]{1,0:T(8,128)(2,1)} %get-tuple-element.50, bf16[512,768]{1,0:T(8,128)(2,1)} %get-tuple-element.49), kind=kOutput, calls=%fused_computation.1 | convolution fusion | flops 806092800 | bytes 3407872 | tf_op jit(solution)/shard_map/dot_general | solution.py:18
  202.4 1.9 collective-permute-start.11
  204.5 3.6 %collective-permute-done.11 = bf16[1024,768]{1,0:T(8,128)(2,1)} collective-permute-done((bf16[1024,768]{1,0:T(8,128)(2,1)}, bf16[1024,768]{1,0:T(8,128)(2,1)}, u32[]{:S(2)}, u32[]{:S(2)}) %collective-permute-start.11) | collective-permute-done | bytes 1572896 | tf_op jit(solution)/shard_map/ppermute | solution.py:293
  208.1 3.9 %add_convert_fusion = bf16[1024,768]{1,0:T(8,128)(2,1)} fusion(bf16[1024,768]{1,0:T(8,128)(2,1)} %collective-permute-done.11, bf16[512,1024]{1,0:T(8,128)(2,1)S(1)} %copy-done.12, bf16[512,768]{1,0:T(8,128)(2,1)} %get-tuple-element.49), kind=kOutput, calls=%fused_computation | convolution fusion | flops 807665664 | bytes 4980736 | tf_op jit(solution)/shard_map/dot_general | solution.py:18
  212.0 37.3 %all-to-all-done.1 = bf16[32,16,2176]{2,1,0:T(8,128)(2,1)S(1)} async-done(((bf16[32,16,2176]{2,1,0:T(8,128)(2,1)}), bf16[32,16,2176]{2,1,0:T(8,128)(2,1)S(1)}, u32[]{:S(2)}, u32[]{:S(2)}) %all-to-all-start.1) | async-done | bytes 2228256 | tf_op jit(solution)/shard_map/all_to_all | solution.py:213
  250.6 3.7 %reduce-scatter.2.cloned.1.call-done = bf16[128,768]{1,0:T(8,128)(2,1)} async-done(((bf16[1024,768]{1,0:T(8,128)(2,1)}), bf16[128,768]{1,0:T(8,128)(2,1)}) %reduce-scatter.2.cloned.1.call-update) | async-done | bytes 196624 | tf_op jit(solution)/shard_map/reduce_scatter | solution.py:295
  254.3 1.9 reshape.179
  (52 shorter events, 14.3 us)
Async XLA Ops:
  7.2 69.2 %all-gather.3.cloned.1.call-start = ((), (), s32[]{:S(2)}) async-start(), calls=%async_computation.3 | async-start | bytes 1253376 | tf_op jit(solution)/shard_map/all_gather | solution.py:220
  9.8 166.8 %all-gather.5.cloned.1.call-start = ((), (), s32[]{:S(2)}) async-start(), calls=%async_computation.4 | async-start | bytes 5013504 | tf_op jit(solution)/shard_map/all_gather | solution.py:240
  12.0 23.8 %collective-permute-start = (bf16[128,2176]{1,0:T(8,128)(2,1)}, bf16[128,2176]{1,0:T(8,128)(2,1)S(1)}, u32[]{:S(2)}, u32[]{:S(2)}) collective-permute-start(bf16[128,2176]{1,0:T(8,128)(2,1)} %get-tuple-element.27.refs_0_), channel_id=1, source_target_pairs={{0,16},{16,32},{32,48},{48,64},{64,80},{80,96},{96,112},{112,0},{1... | collective-permute-start | bytes 1671176 | tf_op jit(solution)/shard_map/ppermute | solution.py:230
  16.2 20.8 %collective-permute-start.1 = (bf16[128,2176]{1,0:T(8,128)(2,1)}, bf16[128,2176]{1,0:T(8,128)(2,1)S(1)}, u32[]{:S(2)}, u32[]{:S(2)}) collective-permute-start(bf16[128,2176]{1,0:T(8,128)(2,1)} %get-tuple-element.27.refs_0_), channel_id=1, source_target_pairs={{0,112},{16,0},{32,16},{48,32},{64,48},{80,64},{96,80},{112,96},{1... | collective-permute-start | bytes 1671176 | tf_op jit(solution)/shard_map/ppermute | solution.py:231
  35.7 44.8 %copy-start.4 = (bf16[128,2176]{1,0:T(8,128)(2,1)}, bf16[128,2176]{1,0:T(8,128)(2,1)S(1)}, u32[]{:S(2)}) copy-start(bf16[128,2176]{1,0:T(8,128)(2,1)S(1)} %collective-permute-done.refs_1_) | copy-start | bytes 1671172
  37.0 43.5 %copy-start.5 = (bf16[128,2176]{1,0:T(8,128)(2,1)}, bf16[128,2176]{1,0:T(8,128)(2,1)S(1)}, u32[]{:S(2)}) copy-start(bf16[128,2176]{1,0:T(8,128)(2,1)S(1)} %collective-permute-done.1.refs_4_) | copy-start | bytes 1671172
  39.8 17.3 %collective-permute-start.2 = (bf16[128,2176]{1,0:T(8,128)(2,1)S(1)}, bf16[128,2176]{1,0:T(8,128)(2,1)S(1)}, u32[]{:S(2)}, u32[]{:S(2)}) collective-permute-start(bf16[128,2176]{1,0:T(8,128)(2,1)S(1)} %collective-permute-done.refs_1_), channel_id=1, source_target_pairs={{0,16},{16,32},{32,48},{48,64},{64,80},{80,96},{96,112},{112,0},{1... | collective-permute-start | bytes 1671176 | tf_op jit(solution)/shard_map/ppermute | solution.py:230
  41.7 16.6 %collective-permute-start.3 = (bf16[128,2176]{1,0:T(8,128)(2,1)S(1)}, bf16[128,2176]{1,0:T(8,128)(2,1)}, u32[]{:S(2)}, u32[]{:S(2)}) collective-permute-start(bf16[128,2176]{1,0:T(8,128)(2,1)S(1)} %collective-permute-done.1.refs_4_), channel_id=1, source_target_pairs={{0,112},{16,0},{32,16},{48,32},{64,48},{80,64},{96,80},{112,96},{1... | collective-permute-start | bytes 1671176 | tf_op jit(solution)/shard_map/ppermute | solution.py:231
  57.1 23.4 %copy-start.6 = (bf16[128,2176]{1,0:T(8,128)(2,1)}, bf16[128,2176]{1,0:T(8,128)(2,1)S(1)}, u32[]{:S(2)}) copy-start(bf16[128,2176]{1,0:T(8,128)(2,1)S(1)} %collective-permute-done.2.refs_2_) | copy-start | bytes 1671172
  58.3 16.6 %collective-permute-start.4 = (bf16[128,2176]{1,0:T(8,128)(2,1)S(1)}, bf16[128,2176]{1,0:T(8,128)(2,1)S(1)}, u32[]{:S(2)}, u32[]{:S(2)}) collective-permute-start(bf16[128,2176]{1,0:T(8,128)(2,1)S(1)} %collective-permute-done.2.refs_2_), channel_id=1, source_target_pairs={{0,16},{16,32},{32,48},{48,64},{64,80},{80,96},{96,112},{112,0},{1... | collective-permute-start | bytes 1671176 | tf_op jit(solution)/shard_map/ppermute | solution.py:230
  61.8 14.6 %collective-permute-start.5 = (bf16[128,2176]{1,0:T(8,128)(2,1)}, bf16[128,2176]{1,0:T(8,128)(2,1)S(1)}, u32[]{:S(2)}, u32[]{:S(2)}) collective-permute-start(bf16[128,2176]{1,0:T(8,128)(2,1)} %collective-permute-done.3.refs_5_), channel_id=1, source_target_pairs={{0,112},{16,0},{32,16},{48,32},{64,48},{80,64},{96,80},{112,96},{1... | collective-permute-start | bytes 1671176 | tf_op jit(solution)/shard_map/ppermute | solution.py:231
  74.9 13.2 %copy-start.2 = (bf16[128,2176]{1,0:T(8,128)(2,1)}, bf16[128,2176]{1,0:T(8,128)(2,1)S(1)}, u32[]{:S(2)}) copy-start(bf16[128,2176]{1,0:T(8,128)(2,1)S(1)} %collective-permute-done.4.refs_3_) | copy-start | bytes 1671172
  76.4 12.5 %copy-start.3 = (bf16[128,2176]{1,0:T(8,128)(2,1)}, bf16[128,2176]{1,0:T(8,128)(2,1)S(1)}, u32[]{:S(2)}) copy-start(bf16[128,2176]{1,0:T(8,128)(2,1)S(1)} %collective-permute-done.5.refs_6_) | copy-start | bytes 1671172
  80.5 103.8 %all-to-all-start = ((bf16[32,16,2048]{2,1,0:T(8,128)(2,1)}), bf16[32,16,2048]{2,1,0:T(8,128)(2,1)S(1)}, u32[]{:S(2)}, u32[]{:S(2)}) async-start(bf16[32,16,2048]{2,1,0:T(8,128)(2,1)} %bitcast.24), calls=%async_computation | async-start | bytes 4194304 | tf_op jit(solution)/shard_map/all_to_all | solution.py:213
  88.9 50.7 %collective-permute-start.6 = (bf16[64,2176]{1,0:T(8,128)(2,1)}, bf16[64,2176]{1,0:T(8,128)(2,1)S(1)}, u32[]{:S(2)}, u32[]{:S(2)}) collective-permute-start(bf16[64,2176]{1,0:T(8,128)(2,1)} %slice.6), channel_id=1, source_target_pairs={{0,16},{16,32},{32,48},{48,64},{64,80},{80,96},{96,112},{112,0},{1... | collective-permute-start | bytes 835592 | tf_op jit(solution)/shard_map/ppermute | solution.py:235
  92.6 47.0 %collective-permute-start.7 = (bf16[64,2176]{1,0:T(8,128)(2,1)S(1)}, bf16[64,2176]{1,0:T(8,128)(2,1)S(1)}, u32[]{:S(2)}, u32[]{:S(2)}) collective-permute-start(bf16[64,2176]{1,0:T(8,128)(2,1)S(1)} %slice.7), channel_id=1, source_target_pairs={{0,112},{16,0},{32,16},{48,32},{64,48},{80,64},{96,80},{112,96},{1... | collective-permute-start | bytes 835592 | tf_op jit(solution)/shard_map/ppermute | solution.py:236
  139.6 0.7 copy-start.9
  140.4 0.7 copy-start.10
  145.4 26.0 %collective-permute-start.10 = (bf16[128,2048]{1,0:T(8,128)(2,1)}, bf16[128,2048]{1,0:T(8,128)(2,1)S(1)}, u32[]{:S(2)}, u32[]{:S(2)}) collective-permute-start(bf16[128,2048]{1,0:T(8,128)(2,1)} %get-tuple-element.41), channel_id=1, source_target_pairs={{0,384},{16,400},{32,416},{48,432},{64,448},{80,464},{96,480},{112... | collective-permute-start | bytes 1572872 | tf_op jit(solution)/shard_map/ppermute | solution.py:260
  150.1 26.5 %collective-permute-start.8 = (bf16[128,2048]{1,0:T(8,128)(2,1)}, bf16[128,2048]{1,0:T(8,128)(2,1)S(1)}, u32[]{:S(2)}, u32[]{:S(2)}) collective-permute-start(bf16[128,2048]{1,0:T(8,128)(2,1)} %get-tuple-element.39), channel_id=1, source_target_pairs={{0,128},{16,144},{32,160},{48,176},{64,192},{80,208},{96,224},{112... | collective-permute-start | bytes 1572872 | tf_op jit(solution)/shard_map/ppermute | solution.py:260
  152.0 24.6 %collective-permute-start.9 = (bf16[128,2048]{1,0:T(8,128)(2,1)}, bf16[128,2048]{1,0:T(8,128)(2,1)}, u32[]{:S(2)}, u32[]{:S(2)}) collective-permute-start(bf16[128,2048]{1,0:T(8,128)(2,1)} %get-tuple-element.40), channel_id=1, source_target_pairs={{0,256},{16,272},{32,288},{48,304},{64,320},{80,336},{96,352},{112... | collective-permute-start | bytes 1572872 | tf_op jit(solution)/shard_map/ppermute | solution.py:260
  171.4 5.2 %copy-start.7 = (bf16[128,2048]{1,0:T(8,128)(2,1)}, bf16[128,2048]{1,0:T(8,128)(2,1)S(1)}, u32[]{:S(2)}) copy-start(bf16[128,2048]{1,0:T(8,128)(2,1)S(1)} %collective-permute-done.10.x3) | copy-start | bytes 1572868
  176.6 0.8 copy-start.8
  184.3 1.4 copy-start.1
  193.6 55.6 %all-to-all-start.1 = ((bf16[32,16,2176]{2,1,0:T(8,128)(2,1)}), bf16[32,16,2176]{2,1,0:T(8,128)(2,1)S(1)}, u32[]{:S(2)}, u32[]{:S(2)}) async-start(bf16[32,16,2176]{2,1,0:T(8,128)(2,1)} %bitcast.26), calls=%async_computation.1 | async-start | bytes 4456448 | tf_op jit(solution)/shard_map/all_to_all | solution.py:213
  198.7 55.7 %reduce-scatter.2.cloned.1.call-start = ((), (), s32[]{:S(2)}) async-start(), calls=%async_computation.5 | async-start | bytes 1769472 | tf_op jit(solution)/shard_map/reduce_scatter | solution.py:295
  198.7 5.7 %copy-start.11 = (s32[2,128]{1,0:T(2,128)S(1)}, s32[2,128]{1,0:T(2,128)}, u32[]{:S(2)}) copy-start(s32[2,128]{1,0:T(2,128)} %get-tuple-element.35.target_ref) | copy-start | bytes 3076
  198.7 9.4 %copy-start.12 = (bf16[512,1024]{1,0:T(8,128)(2,1)S(1)}, bf16[512,1024]{1,0:T(8,128)(2,1)}, u32[]{:S(2)}) copy-start(bf16[512,1024]{1,0:T(8,128)(2,1)} %get-tuple-element.48) | copy-start | bytes 3145732
  202.4 5.6 %collective-permute-start.11 = (bf16[1024,768]{1,0:T(8,128)(2,1)}, bf16[1024,768]{1,0:T(8,128)(2,1)}, u32[]{:S(2)}, u32[]{:S(2)}) collective-permute-start(bf16[1024,768]{1,0:T(8,128)(2,1)} %convolution_convert_fusion), channel_id=1, source_target_pairs={{0,1},{1,0},{2,3},{3,2},{4,5},{5,4},{6,7},{7,6},{8,9},{9,8},{10,11... | collective-permute-start | bytes 4718600 | tf_op jit(solution)/shard_map/ppermute | solution.py:293
  208.1 41.2 %copy-start = (bf16[128,2]{0,1:T(2,128)(2,1)S(1)}, bf16[128,2]{0,1:T(2,128)(2,1)}, u32[]{:S(2)}) copy-start(bf16[128,2]{0,1:T(2,128)(2,1)} %param.13) | copy-start | bytes 1540
Sparse Core Ops, SparseCore 0:
  10.7 44.0 all-gather.2
  57.4 44.7 all-gather.4
  212.1 42.2 reduce-scatter.1

commit v4 on v2

v4 whole, which is shorter than its diff:
```python
import functools

import jax
import jax.numpy as jnp
from jax import lax
from jax.experimental import pallas as pl
from jax.experimental.pallas import tpu as pltpu
from jax.sharding import PartitionSpec as P

F32 = jnp.float32
BF16 = jnp.bfloat16
NT = (((1,), (1,)), ((), ()))
NN = (((1,), (0,)), ((), ()))
TN = (((0,), (0,)), ((), ()))


def mm(a, b, dims=NN):
    return lax.dot_general(a, b, dims, preferred_element_type=F32)


def one_hot(target, rows):
    tokens = target.shape[1]
    return lax.broadcasted_iota(jnp.int32, (rows, tokens), 0) == target


def route_kernel(experts, cap, ids_ref, x_any, send_any, target_ref, x, send, sems):
    load = pltpu.make_async_copy(x_any, x, sems.at[0])
    load.start()
    tokens = ids_ref.shape[1]
    ids = ids_ref[...]
    members = [
        (lax.broadcasted_iota(jnp.int32, (experts, tokens), 0) == ids[k : k + 1]).astype(F32)
        for k in range(2)
    ]
    earlier = (
        lax.broadcasted_iota(jnp.int32, (tokens, tokens), 0)
        < lax.broadcasted_iota(jnp.int32, (tokens, tokens), 1)
    ).astype(F32)
    count = mm((members[0] + members[1]).astype(BF16), earlier.astype(BF16))
    rows = experts * cap
    targets = []
    for k in range(2):
        position = jnp.sum(members[k] * count, axis=0, keepdims=True).astype(jnp.int32)
        targets.append(ids[k : k + 1] * cap + position)
        target_ref[k : k + 1, :] = targets[k]
    load.wait()
    block = rows // 4
    stores = []
    for j in range(4):
        part = slice(j * block, (j + 1) * block)
        select = sum(one_hot(t - j * block, block).astype(F32) for t in targets)
        send[part, :] = mm(select.astype(BF16), x[...]).astype(BF16)
        stores.append(pltpu.make_async_copy(send.at[part, :], send_any.at[part, :], sems.at[1 + j]))
        stores[j].start()
    for store in stores:
        store.wait()


def upstream_kernel(own_ref, names_ref, frames_ref, lm_ref, target_ref, gate_ref, send_ref):
    tokens = lm_ref.shape[0]
    frames = frames_ref.shape[0]
    own = lax.broadcasted_iota(jnp.int32, (tokens, frames), 0) + own_ref[0]
    named = (own == names_ref[...]).astype(F32)
    cond = mm(named.astype(BF16), frames_ref[...])
    upstream = (lm_ref[...].astype(F32) + cond).astype(BF16)
    rows = send_ref.shape[0]
    hot = [one_hot(target_ref[k : k + 1, :], rows).astype(F32) for k in range(2)]
    gates = gate_ref[...].astype(F32)
    gate = jnp.sum(hot[0] * gates[0:1] + hot[1] * gates[1:2], axis=1, keepdims=True)
    send_ref[...] = (mm((hot[0] + hot[1]).astype(BF16), upstream) * gate).astype(BF16)


def forward_kernel(
    ff, n_seq, place_ref, x_ref, w_ref, hidden_ref, gate_term_ref, up_term_ref, mine_ref, other_ref
):
    seq, core = place_ref[0], place_ref[1]
    for j in range(n_seq):
        owner = (seq + j) % n_seq
        own = pl.ds(pl.multiple_of((2 * owner + core) * 128, 128), 128)
        away = pl.ds(pl.multiple_of((2 * owner + 1 - core) * 128, 128), 128)
        mine_ref[:, j * 128 : (j + 1) * 128] = x_ref[:, own]
        other_ref[:, j * 128 : (j + 1) * 128] = x_ref[:, away]
    pre = mm(x_ref[...], w_ref[:, : 2 * ff])
    gate_pre = pre[:, :ff]
    up_pre = pre[:, ff:]
    sig = jax.nn.sigmoid(gate_pre)
    activated = gate_pre * sig
    slope = sig * (1.0 + gate_pre * (1.0 - sig))
    hidden_ref[...] = (activated * up_pre).astype(BF16)
    gate_term_ref[...] = up_pre * slope
    up_term_ref[...] = activated


def backward_kernel(
    ff, y_any, w_any, hidden_any, gate_any, up_any, out_any, pre_ref,
    y, wd, wg, hidden, gate_term, up_term, out, extra, sems,
):
    rows, width = y.shape
    half, block = width // 2, width // 4
    copies = []

    def fetch(source, target):
        copies.append(pltpu.make_async_copy(source, target, sems.at[len(copies)]))
        copies[-1].start()

    for h in range(2):
        part = slice(h * half, (h + 1) * half)
        fetch(y_any.at[:, part], y.at[:, part])
        fetch(w_any.at[part, 2 * ff :], wd.at[part, :])
    copies[0].wait()
    copies[1].wait()
    fetch(gate_any, gate_term)
    fetch(up_any, up_term)
    fetch(hidden_any, hidden)
    hidden_grad = mm(y[:, :half], wd[:half, :])
    copies[2].wait()
    copies[3].wait()
    for j in range(4):
        part = slice(j * block, (j + 1) * block)
        fetch(w_any.at[part, : 2 * ff], wg.at[part, :])
    hidden_grad += mm(y[:, half:], wd[half:, :])
    copies[4].wait()
    pre_ref[:, :ff] = (hidden_grad * gate_term[...]).astype(BF16)
    copies[5].wait()
    pre_ref[:, ff:] = (hidden_grad * up_term[...]).astype(BF16)
    copies[6].wait()
    total = jnp.sum(hidden[...].astype(F32) * hidden_grad, axis=1, keepdims=True)
    high = total.astype(BF16).astype(F32)
    lane = lax.broadcasted_iota(jnp.int32, (rows, 128), 1)
    extra[...] = jnp.where(lane < 64, high, total - high).astype(BF16)
    fetch(extra, out_any.at[:, width:])
    for j in range(4):
        part = slice(j * block, (j + 1) * block)
        copies[7 + j].wait()
        out[:, part] = mm(pre_ref[...], wg[part, :], NT).astype(BF16)
        fetch(out.at[:, part], out_any.at[:, part])
    for j in range(5):
        copies[11 + j].wait()


def away_kernel(x_ref, pre_ref, out_ref):
    out_ref[...] = mm(x_ref[...], pre_ref[...], TN).astype(BF16)


def near_kernel(x_any, pre_any, other_any, *refs):
    count = len(refs) - 4
    outs, (x, pre, other, sems) = refs[:count], refs[count:]
    rows = x.shape[1] // count
    copies = [pltpu.make_async_copy(pre_any, pre, sems.at[0])]
    copies[0].start()
    loads = []
    for j in range(count):
        part = slice(j * rows, (j + 1) * rows)
        loads.append(
            (
                pltpu.make_async_copy(x_any.at[:, part], x.at[:, part], sems.at[1 + 2 * j]),
                pltpu.make_async_copy(other_any.at[part, :], other.at[part, :], sems.at[2 + 2 * j]),
            )
        )
        for load in loads[j]:
            load.start()
    copies[0].wait()
    stores = []
    for j in range(count):
        part = slice(j * rows, (j + 1) * rows)
        for load in loads[j]:
            load.wait()
        both = mm(x[:, part], pre[...], TN) + other[part, :].astype(F32)
        other[part, :] = both.astype(BF16)
        stores.append(
            pltpu.make_async_copy(other.at[part, :], outs[j], sems.at[1 + 2 * count + j])
        )
        stores[j].start()
    for store in stores:
        store.wait()


def total_kernel(*refs):
    total = refs[0][...].astype(F32)
    for ref in refs[1:-1]:
        total += ref[...].astype(F32)
    ff = total.shape[1] // 2
    refs[-1][:, 0, :] = total[:, :ff]
    refs[-1][:, 1, :] = total[:, ff:]


def combine_kernel(back_any, column_ref, gate_ref, out_ref, gate_out_ref, back, sems):
    rows = back.shape[0]
    tokens, width = out_ref.shape
    block = rows // 4
    loads = []
    for j in range(4):
        part = slice(j * block, (j + 1) * block)
        loads.append(pltpu.make_async_copy(back_any.at[part, :], back.at[part, :], sems.at[j]))
        loads[j].start()
    place = lax.broadcasted_iota(jnp.int32, (tokens, rows), 1)
    picks = [(place == column_ref[:, k : k + 1]).astype(F32) for k in range(2)]
    pick = (picks[0] + picks[1]).astype(BF16)
    total = None
    for j in range(4):
        part = slice(j * block, (j + 1) * block)
        loads[j].wait()
        term = mm(pick[:, part], back[part, :width])
        total = term if total is None else total + term
    out_ref[...] = total.astype(BF16)
    eye = (
        lax.broadcasted_iota(jnp.int32, (tokens, tokens), 0)
        == lax.broadcasted_iota(jnp.int32, (tokens, tokens), 1)
    ).astype(F32)
    for k in range(2):
        parts = mm(picks[k].astype(BF16), back[:, width:])
        gate = jnp.sum(eye * (parts[:, 0:1] + parts[:, 64:65]), axis=0, keepdims=True)
        gate_out_ref[k : k + 1, :] = (gate / gate_ref[k : k + 1, :].astype(F32)).astype(BF16)


def call(kernel, outs, args, limit=60, **kw):
    return pl.pallas_call(
        kernel,
        out_shape=outs,
        compiler_params=pltpu.CompilerParams(vmem_limit_bytes=limit << 20),
        **kw,
    )(*args)


LONG = pl.CostEstimate(flops=1 << 40, bytes_accessed=1 << 30, transcendentals=0)


def ranked(values):
    return pl.pallas_call(
        lambda source, result: None,
        out_shape=jax.ShapeDtypeStruct(values.shape, values.dtype),
        in_specs=[pl.BlockSpec(memory_space=pl.ANY)],
        out_specs=pl.BlockSpec(memory_space=pl.ANY),
        input_output_aliases={0: 0},
        compiler_params=pltpu.CompilerParams(vmem_limit_bytes=1 << 20),
        cost_estimate=LONG,
    )(values)


def on_device(moe_input, lm_grad, frame_grad, span_token, expert_ids, gate_weights, w_gate_up, w_down):
    tokens, width = moe_input.shape
    per_span = frame_grad.shape[0] // span_token.shape[0]
    experts = lax.axis_size("expert")
    n_seq = lax.axis_size("seq")
    cap = 2 * tokens * expert_ids.shape[1] // experts
    rows = experts * cap
    ff = w_down.shape[2]
    sds = jax.ShapeDtypeStruct
    any_space = pl.BlockSpec(memory_space=pl.ANY)
    vmem = pl.BlockSpec(memory_space=pltpu.VMEM)
    smem = pl.BlockSpec(memory_space=pltpu.SMEM)

    def exchange(values):
        return lax.all_to_all(
            values.reshape(experts, cap, -1), "expert", split_axis=0, concat_axis=0, tiled=True
        ).reshape(rows, -1)

    seq = lax.axis_index("seq")
    place = jnp.stack([seq, lax.axis_index("dp")]).astype(jnp.int32)
    frames = lax.all_gather(frame_grad, "seq", axis=0, tiled=True)

    gates = gate_weights.T
    send_input, target = call(
        functools.partial(route_kernel, experts, cap),
        (sds((rows, width), BF16), sds((2, tokens), jnp.int32)),
        (expert_ids.T, moe_input),
        in_specs=[vmem, any_space],
        out_specs=[any_space, vmem],
        scratch_shapes=[
            pltpu.VMEM((tokens, width), BF16),
            pltpu.VMEM((rows, width), BF16),
            pltpu.SemaphoreType.DMA((5,)),
        ],
    )
    got_input = ranked(exchange(send_input))

    w_gate_up, w_down, target = lax.optimization_barrier((w_gate_up, w_down, target))
    weights = jnp.concatenate([w_gate_up.reshape(-1, 2 * ff), w_down[0]], axis=1)
    weights = lax.all_gather(weights, ("seq", "dp"), axis=0, tiled=True)

    span_token, _ = lax.optimization_barrier((span_token, target))
    names = lax.all_gather(span_token, "seq", axis=0, tiled=True)
    names = jnp.repeat(names, per_span)[None, :]
    send_grad = call(
        upstream_kernel,
        sds((rows, width), BF16),
        ((seq * tokens).reshape(1), names, frames, lm_grad, target, gates),
        in_specs=[smem] + [vmem] * 5,
        cost_estimate=LONG,
    )
    got_grad = exchange(send_grad)

    hidden, gate_term, up_term, x_mine, x_other = call(
        functools.partial(forward_kernel, ff, n_seq),
        (
            sds((rows, ff), BF16), sds((rows, ff), F32), sds((rows, ff), F32),
            sds((rows, width // 2), BF16), sds((rows, width // 2), BF16),
        ),
        (place, got_input, weights),
        in_specs=[smem, vmem, vmem],
    )
    input_grad, pre_grad = call(
        functools.partial(backward_kernel, ff),
        (sds((rows, width + 128), BF16), sds((rows, 2 * ff), BF16)),
        (got_grad, weights, hidden, gate_term, up_term),
        limit=60,
        in_specs=[any_space] * 5,
        out_specs=[any_space, pl.BlockSpec(memory_space=pltpu.VMEM)],
        scratch_shapes=[
            pltpu.VMEM((rows, width), BF16),
            pltpu.VMEM((width, ff), BF16),
            pltpu.VMEM((width, 2 * ff), BF16),
            pltpu.VMEM((rows, ff), BF16),
            pltpu.VMEM((rows, ff), F32),
            pltpu.VMEM((rows, ff), F32),
            pltpu.VMEM((rows, width), BF16),
            pltpu.VMEM((rows, 128), BF16),
            pltpu.SemaphoreType.DMA((16,)),
        ],
    )
    back = exchange(input_grad)

    other = call(
        away_kernel,
        sds((width // 2, 2 * ff), BF16),
        (x_other, pre_grad),
        grid=(4,),
        in_specs=[
            pl.BlockSpec((rows, width // 8), lambda j: (0, j)),
            pl.BlockSpec((rows, 2 * ff), lambda j: (0, 0)),
        ],
        out_specs=pl.BlockSpec((width // 8, 2 * ff), lambda j: (j, 0)),
    )
    other = lax.ppermute(other, "dp", [(0, 1), (1, 0)])
    sums = call(
        near_kernel,
        [sds((width // 2 // n_seq, 2 * ff), BF16)] * n_seq,
        (x_mine, pre_grad, other),
        in_specs=[any_space] * 3,
        out_specs=[any_space] * n_seq,
        scratch_shapes=[
            pltpu.VMEM((rows, width // 2), BF16),
            pltpu.VMEM((rows, 2 * ff), BF16),
            pltpu.VMEM((width // 2, 2 * ff), BF16),
            pltpu.SemaphoreType.DMA((1 + 3 * n_seq,)),
        ],
    )
    shares = [sums[0]]
    for d in range(1, n_seq):
        pairs = [(i, (i + d) % n_seq) for i in range(n_seq)]
        shares.append(lax.ppermute(sums[d], "seq", pairs))
    grad_gate_up = call(
        total_kernel, sds((width // 2 // n_seq, 2, ff), F32), shares, limit=20
    )[None]

    grad_input, grad_gates = call(
        combine_kernel,
        (sds((tokens, width), BF16), sds((2, tokens), BF16)),
        (back, target.T, gates),
        limit=20,
        in_specs=[any_space, vmem, vmem],
        out_specs=[vmem, vmem],
        scratch_shapes=[
            pltpu.VMEM((rows, width + 128), BF16),
            pltpu.SemaphoreType.DMA((4,)),
        ],
        cost_estimate=LONG,
    )
    return grad_input, grad_gates.T, grad_gate_up


def solution(mesh):
    every = ("expert", "seq", "dp")
    return jax.shard_map(
        on_device,
        mesh=mesh,
        in_specs=(
            P(every, None),
            P(every, None),
            P(every, None),
            P(every),
            P(every, None),
            P(every, None),
            P("expert", ("seq", "dp"), None, None),
            P("expert", ("seq", "dp"), None),
        ),
        out_specs=(P(every, None), P(every, None), P("expert", ("seq", "dp"), None, None)),
        check_vma=False,
    )
```

time: 211 us -> 228 us (1.081)
  starting transfers between devices: 29.6 us -> 54.9 us
  waiting for transfers between devices: 128 us -> 103 us
  Pallas kernels: 24.1 us -> 35.8 us
  blocking collectives: 0 us -> 10.6 us
  other arithmetic: 4.4 us -> 1.41 us
    all_gather x1, waiting for transfers between devices: 42.3 us -> 13.5 us  [on_device(): frames = lax.all_gather(frame_grad, 'seq', axis=0, tiled=True)]
    ppermute x0 -> x7, starting transfers between devices: none -> 26.9 us  [on_device(): shares.append(lax.ppermute(sums[d], 'seq', pairs))]
    ppermute x0 -> x7, waiting for transfers between devices: none -> 24.3 us  [on_device(): shares.append(lax.ppermute(sums[d], 'seq', pairs))]
    all_gather x1, waiting for transfers between devices: 31.8 us -> 19.7 us  [on_device(): weights = lax.all_gather(weights, ('seq', 'dp'), axis=0, tiled=True)]
    pallas_call x5 -> x8, Pallas kernels: 24.1 us -> 35.8 us  [call(): pl.pallas_call(kernel, out_shape=outs, compiler_params=pltpu.CompilerPara...]
    all_to_all x3, waiting for transfers between devices: 51.5 us -> 40.9 us  [exchange(): lax.all_to_all(values.reshape(experts, cap, -1), 'expert', split_axis=0,...]
    unnamed x0 -> x1, blocking collectives: none -> 10.6 us
    convert_element_type x1 -> x0, other arithmetic: 2.96 us -> none  [on_device(): pair = (mine.astype(F32) + other.astype(F32)).astype(BF16)]
  transfers between devices with their start and end apart: 7 -> 13, of which waited for: 6 -> 10; matrix products, arithmetic and copies ran while one was open for 4% -> 2% of each run, Pallas kernels for 6% -> 12%
where the time goes in v4:
time: 228 us; the launch traced here: 225 us
  waiting for transfers between devices  103 us (45%)
  starting transfers between devices  54.9 us (24%)
  Pallas kernels  35.8 us (16%)
  between operations  14.9 us (7%)
  blocking collectives  10.6 us (5%)
  local copies, waits for them, and re-layouts  4.54 us (2%)
    all_to_all x3, waiting for transfers between devices, exchange(): lax.all_to_all(values.reshape(experts, cap, -1), 'expert', split_axis=0,...  40.9 us
    pallas_call x8, Pallas kernels, call(): pl.pallas_call(kernel, out_shape=outs, compiler_params=pltpu.CompilerPara...  35.8 us
    ppermute x7, starting transfers between devices, on_device(): shares.append(lax.ppermute(sums[d], 'seq', pairs))  26.9 us
    all_to_all x3, starting transfers between devices, exchange(): lax.all_to_all(values.reshape(experts, cap, -1), 'expert', split_axis=0,...  25.8 us
    ppermute x7, waiting for transfers between devices, on_device(): shares.append(lax.ppermute(sums[d], 'seq', pairs))  24.3 us
    all_gather x1, waiting for transfers between devices, on_device(): weights = lax.all_gather(weights, ('seq', 'dp'), axis=0, tiled=True)  19.7 us
    all_gather x1, waiting for transfers between devices, on_device(): frames = lax.all_gather(frame_grad, 'seq', axis=0, tiled=True)  13.5 us
    unnamed x1, blocking collectives  10.6 us
  transfers between devices with their start and end apart: 13, of which 10 were waited for; matrix products, arithmetic and copies ran while one was open for 2% of the time, Pallas kernels for 12%

profile of v4, /device:TPU:56, one launch (start us, length us, event | category | flops | bytes accessed | tf_op | source)
XLA Modules:
  0.0 224.9 jit_solution(15575819913294004589)
XLA Ops:
  7.9 4.0 %shard_map.103 = (bf16[512,2048]{1,0:T(8,128)(2,1)}, s32[2,128]{1,0:T(2,128)}) custom-call(s32[2,128]{1,0:T(2,128)} %bitcast.30, bf16[128,2048]{1,0:T(8,128)(2,1)} %x_any.1), custom_call_target="tpu_custom_call" | custom-call | tf_op jit(solution)/shard_map/pallas_call | solution.py:217
  12.0 13.4 %all-to-all-start.1 = ((bf16[32,16,2048]{2,1,0:T(8,128)(2,1)}), bf16[32,16,2048]{2,1,0:T(8,128)(2,1)}, u32[]{:S(2)}, u32[]{:S(2)}) async-start(bf16[32,16,2048]{2,1,0:T(8,128)(2,1)} %bitcast.24), calls=%async_computation.1 | async-start | bytes 4194304 | tf_op jit(solution)/shard_map/all_to_all | solution.py:254
  26.3 1.3 dynamic-slice
  28.5 10.6 %all-reduce = s32[64]{0:T(128)S(1)} all-reduce(s32[64]{0:T(128)S(1)} %dynamic-update-slice), channel_id=1, replica_groups=mesh['expert'=32,'seq'=8,'dp'=2] {'seq'}, use_global_device_ids=true, to_apply=%add | all-reduce | flops 64 | bytes 512
  40.5 13.5 %all-gather.3.cloned.1.call-done.frames_ref = bf16[256,2048]{1,0:T(8,128)(2,1)} async-done(((bf16[32,2048]{1,0:T(8,128)(2,1)}), bf16[256,2048]{1,0:T(8,128)(2,1)}) %all-gather.3.cloned.1.call-update) | async-done | bytes 1048592 | tf_op jit(solution)/shard_map/all_gather | solution.py:260
  54.0 3.6 %shard_map.104 = bf16[512,2048]{1,0:T(8,128)(2,1)} custom-call(s32[1]{0:T(128)} %bitcast.own_ref, s32[1,256]{1,0:T(1,128)} %broadcast_in_dim_reshape.3.names_ref, bf16[256,2048]{1,0:T(8,128)(2,1)} %all-gather.3.cloned.1.call-done.frames_ref, bf16[128,2048]{1,0:T(8,128)(2,1)} %lm_ref.1, s32[2,128]{1,0:T(2,128)} %get-tuple-element.27.target_ref, ...), custom_call_target="tpu_custom_call" | custom-call | flops 1099511627776 | bytes 1073741824 | tf_op jit(solution)/shard_map/pallas_call | solution.py:217
  57.6 17.8 %all-to-all-done.1 = bf16[32,16,2048]{2,1,0:T(8,128)(2,1)} async-done(((bf16[32,16,2048]{2,1,0:T(8,128)(2,1)}), bf16[32,16,2048]{2,1,0:T(8,128)(2,1)}, u32[]{:S(2)}, u32[]{:S(2)}) %all-to-all-start.1) | async-done | bytes 2097184 | tf_op jit(solution)/shard_map/all_to_all | solution.py:254
  75.4 6.3 %all-to-all-start = ((bf16[32,16,2048]{2,1,0:T(8,128)(2,1)}), bf16[32,16,2048]{2,1,0:T(8,128)(2,1)}, u32[]{:S(2)}, u32[]{:S(2)}) async-start(bf16[32,16,2048]{2,1,0:T(8,128)(2,1)} %bitcast.25), calls=%async_computation | async-start | bytes 4194304 | tf_op jit(solution)/shard_map/all_to_all | solution.py:254
  81.7 19.7 %all-gather.5.cloned.1.call-done.w_ref.w_any = bf16[2048,1152]{1,0:T(8,128)(2,1)} async-done(((bf16[128,1152]{1,0:T(8,128)(2,1)}), bf16[2048,1152]{1,0:T(8,128)(2,1)}) %all-gather.5.cloned.1.call-update) | async-done | bytes 4718608 | tf_op jit(solution)/shard_map/all_gather | solution.py:279
  101.4 6.9 %shard_map.106 = (bf16[512,384]{1,0:T(8,128)(2,1)}, f32[512,384]{1,0:T(8,128)}, f32[512,384]{1,0:T(8,128)}, bf16[512,1024]{1,0:T(8,128)(2,1)}, bf16[512,1024]{1,0:T(8,128)(2,1)}) custom-call(s32[2]{0:T(128)} %pad_add_fusion.place_ref, bf16[512,2048]{1,0:T(8,128)(2,1)} %shard_map.105.x_ref, bf16[2048,1152]{1,0:T(8,128)(2,1)} %all-gather.5.cloned.1.call-done.w_ref.w_any), custom_call_target="tpu_custom_call" | custom-call | tf_op jit(solution)/shard_map/pallas_call | solution.py:217
  108.4 23.1 %all-to-all-done = bf16[32,16,2048]{2,1,0:T(8,128)(2,1)} async-done(((bf16[32,16,2048]{2,1,0:T(8,128)(2,1)}), bf16[32,16,2048]{2,1,0:T(8,128)(2,1)}, u32[]{:S(2)}, u32[]{:S(2)}) %all-to-all-start) | async-done | bytes 2097184 | tf_op jit(solution)/shard_map/all_to_all | solution.py:254
  131.4 7.8 %shard_map.107 = (bf16[512,2176]{1,0:T(8,128)(2,1)}, bf16[512,768]{1,0:T(8,128)(2,1)}) custom-call(bf16[512,2048]{1,0:T(8,128)(2,1)} %bitcast.5.y_any, bf16[2048,1152]{1,0:T(8,128)(2,1)} %all-gather.5.cloned.1.call-done.w_ref.w_any, bf16[512,384]{1,0:T(8,128)(2,1)} %get-tuple-element.32.hidden_any, f32[512,384]{1,0:T(8,128)} %get-tuple-element.33.gate_any, ...), custom_call_target="tpu_custom_call" | custom-call | tf_op jit(solution)/shard_map/pallas_call | solution.py:217
  139.3 6.1 %all-to-all-start.2 = ((bf16[32,16,2176]{2,1,0:T(8,128)(2,1)}), bf16[32,16,2176]{2,1,0:T(8,128)(2,1)S(1)}, u32[]{:S(2)}, u32[]{:S(2)}) async-start(bf16[32,16,2176]{2,1,0:T(8,128)(2,1)} %bitcast.23), calls=%async_computation.2 | async-start | bytes 4456448 | tf_op jit(solution)/shard_map/all_to_all | solution.py:254
  145.4 4.5 %shard_map.109 = bf16[1024,768]{1,0:T(8,128)(2,1)} custom-call(bf16[512,1024]{1,0:T(8,128)(2,1)} %get-tuple-element.40.x_ref, bf16[512,768]{1,0:T(8,128)(2,1)} %get-tuple-element.39.pre_ref.pre_any), custom_call_target="tpu_custom_call" | custom-call | tf_op jit(solution)/shard_map/pallas_call | solution.py:217
  150.0 2.0 collective-permute-start
  152.0 3.6 %collective-permute-done.other_any = bf16[1024,768]{1,0:T(8,128)(2,1)S(1)} collective-permute-done((bf16[1024,768]{1,0:T(8,128)(2,1)}, bf16[1024,768]{1,0:T(8,128)(2,1)S(1)}, u32[]{:S(2)}, u32[]{:S(2)}) %collective-permute-start) | collective-permute-done | bytes 1572896 | tf_op jit(solution)/shard_map/ppermute | solution.py:334
  155.6 1.2 copy-done.2
  156.8 4.8 %shard_map.110 = (bf16[128,768]{1,0:T(8,128)(2,1)}, bf16[128,768]{1,0:T(8,128)(2,1)}, bf16[128,768]{1,0:T(8,128)(2,1)}, bf16[128,768]{1,0:T(8,128)(2,1)}, bf16[1...) custom-call(bf16[512,1024]{1,0:T(8,128)(2,1)} %get-tuple-element.38.x_any, ...), custom_call_target="tpu_custom_call" | custom-call | tf_op jit(solution)/shard_map/pallas_call | solution.py:217
  161.6 1.9 collective-permute-start.1
  163.6 4.2 %collective-permute-start.2 = (bf16[128,768]{1,0:T(8,128)(2,1)}, bf16[128,768]{1,0:T(8,128)(2,1)S(1)}, u32[]{:S(2)}, u32[]{:S(2)}) collective-permute-start(bf16[128,768]{1,0:T(8,128)(2,1)} %get-tuple-element.43), channel_id=1, source_target_pairs={{0,4},{2,6},{4,8},{6,10},{8,12},{10,14},{12,0},{14,2},{1,5},{3,7},... | collective-permute-start | bytes 589832 | tf_op jit(solution)/shard_map/ppermute | solution.py:351
  167.8 5.8 %collective-permute-start.3 = (bf16[128,768]{1,0:T(8,128)(2,1)}, bf16[128,768]{1,0:T(8,128)(2,1)S(1)}, u32[]{:S(2)}, u32[]{:S(2)}) collective-permute-start(bf16[128,768]{1,0:T(8,128)(2,1)} %get-tuple-element.44), channel_id=1, source_target_pairs={{0,6},{2,8},{4,10},{6,12},{8,14},{10,0},{12,2},{14,4},{1,7},{3,9},... | collective-permute-start | bytes 589832 | tf_op jit(solution)/shard_map/ppermute | solution.py:351
  173.6 2.9 %collective-permute-start.4 = (bf16[128,768]{1,0:T(8,128)(2,1)}, bf16[128,768]{1,0:T(8,128)(2,1)S(1)}, u32[]{:S(2)}, u32[]{:S(2)}) collective-permute-start(bf16[128,768]{1,0:T(8,128)(2,1)} %get-tuple-element.45), channel_id=1, source_target_pairs={{0,8},{2,10},{4,12},{6,14},{8,0},{10,2},{12,4},{14,6},{1,9},{3,11}... | collective-permute-start | bytes 589832 | tf_op jit(solution)/shard_map/ppermute | solution.py:351
  176.6 4.8 %collective-permute-start.5 = (bf16[128,768]{1,0:T(8,128)(2,1)}, bf16[128,768]{1,0:T(8,128)(2,1)S(1)}, u32[]{:S(2)}, u32[]{:S(2)}) collective-permute-start(bf16[128,768]{1,0:T(8,128)(2,1)} %get-tuple-element.46), channel_id=1, source_target_pairs={{0,10},{2,12},{4,14},{6,0},{8,2},{10,4},{12,6},{14,8},{1,11},{3,13... | collective-permute-start | bytes 589832 | tf_op jit(solution)/shard_map/ppermute | solution.py:351
  181.4 5.3 %collective-permute-start.6 = (bf16[128,768]{1,0:T(8,128)(2,1)}, bf16[128,768]{1,0:T(8,128)(2,1)S(1)}, u32[]{:S(2)}, u32[]{:S(2)}) collective-permute-start(bf16[128,768]{1,0:T(8,128)(2,1)} %get-tuple-element.47), channel_id=1, source_target_pairs={{0,12},{2,14},{4,0},{6,2},{8,4},{10,6},{12,8},{14,10},{1,13},{3,15... | collective-permute-start | bytes 589832 | tf_op jit(solution)/shard_map/ppermute | solution.py:351
  186.7 1.9 collective-permute-start.7
  188.7 3.8 %collective-permute-done.3.refs_3_ = bf16[128,768]{1,0:T(8,128)(2,1)S(1)} collective-permute-done((bf16[128,768]{1,0:T(8,128)(2,1)}, bf16[128,768]{1,0:T(8,128)(2,1)S(1)}, u32[]{:S(2)}, u32[]{:S(2)}) %collective-permute-start.3) | collective-permute-done | bytes 196640 | tf_op jit(solution)/shard_map/ppermute | solution.py:351
  193.3 11.1 %collective-permute-done.5.refs_5_ = bf16[128,768]{1,0:T(8,128)(2,1)S(1)} collective-permute-done((bf16[128,768]{1,0:T(8,128)(2,1)}, bf16[128,768]{1,0:T(8,128)(2,1)S(1)}, u32[]{:S(2)}, u32[]{:S(2)}) %collective-permute-start.5) | collective-permute-done | bytes 196640 | tf_op jit(solution)/shard_map/ppermute | solution.py:351
  204.4 3.6 %collective-permute-done.6.refs_6_ = bf16[128,768]{1,0:T(8,128)(2,1)S(1)} collective-permute-done((bf16[128,768]{1,0:T(8,128)(2,1)}, bf16[128,768]{1,0:T(8,128)(2,1)S(1)}, u32[]{:S(2)}, u32[]{:S(2)}) %collective-permute-start.6) | collective-permute-done | bytes 196640 | tf_op jit(solution)/shard_map/ppermute | solution.py:351
  208.0 5.0 %collective-permute-done.7.refs_7_ = bf16[128,768]{1,0:T(8,128)(2,1)} collective-permute-done((bf16[128,768]{1,0:T(8,128)(2,1)}, bf16[128,768]{1,0:T(8,128)(2,1)}, u32[]{:S(2)}, u32[]{:S(2)}) %collective-permute-start.7) | collective-permute-done | bytes 196640 | tf_op jit(solution)/shard_map/ppermute | solution.py:351
  213.1 0.9 copy-done
  214.0 2.0 shard_map.111
  216.0 2.1 shard_map.108
  (29 shorter events, 4.1 us)
Async XLA Ops:
  7.2 46.9 %all-gather.3.cloned.1.call-start = ((), (), s32[]{:S(2)}) async-start(), calls=%async_computation.3 | async-start | bytes 1179648 | tf_op jit(solution)/shard_map/all_gather | solution.py:260
  11.9 13.5 %copy-start.3 = (bf16[1,128,2,384]{3,2,1,0:T(2,128)(2,1)S(1)}, bf16[1,128,2,384]{3,2,1,0:T(2,128)(2,1)}, u32[]{:S(2)}) copy-start(bf16[1,128,2,384]{3,2,1,0:T(2,128)(2,1)} %param.14) | copy-start | bytes 589828
  11.9 13.6 %copy-start.4 = (bf16[1,128,384]{2,1,0:T(8,128)(2,1)S(1)}, bf16[1,128,384]{2,1,0:T(8,128)(2,1)}, u32[]{:S(2)}) copy-start(bf16[1,128,384]{2,1,0:T(8,128)(2,1)} %param.15) | copy-start | bytes 294916
  11.9 16.3 %copy-start.6 = (s32[8]{0:T(128)S(1)}, s32[8]{0:T(128)}, u32[]{:S(2)}) copy-start(s32[8]{0:T(128)} %param.11) | copy-start | bytes 100
  12.0 63.5 %all-to-all-start.1 = ((bf16[32,16,2048]{2,1,0:T(8,128)(2,1)}), bf16[32,16,2048]{2,1,0:T(8,128)(2,1)}, u32[]{:S(2)}, u32[]{:S(2)}) async-start(bf16[32,16,2048]{2,1,0:T(8,128)(2,1)} %bitcast.24), calls=%async_computation.1 | async-start | bytes 4194304 | tf_op jit(solution)/shard_map/all_to_all | solution.py:254
  25.4 76.0 %all-gather.5.cloned.1.call-start = ((), (), s32[]{:S(2)}) async-start(), calls=%async_computation.4 | async-start | bytes 5013504 | tf_op jit(solution)/shard_map/all_gather | solution.py:279
  75.4 56.0 %all-to-all-start = ((bf16[32,16,2048]{2,1,0:T(8,128)(2,1)}), bf16[32,16,2048]{2,1,0:T(8,128)(2,1)}, u32[]{:S(2)}, u32[]{:S(2)}) async-start(bf16[32,16,2048]{2,1,0:T(8,128)(2,1)} %bitcast.25), calls=%async_computation | async-start | bytes 4194304 | tf_op jit(solution)/shard_map/all_to_all | solution.py:254
  139.3 76.7 %all-to-all-start.2 = ((bf16[32,16,2176]{2,1,0:T(8,128)(2,1)}), bf16[32,16,2176]{2,1,0:T(8,128)(2,1)S(1)}, u32[]{:S(2)}, u32[]{:S(2)}) async-start(bf16[32,16,2176]{2,1,0:T(8,128)(2,1)} %bitcast.23), calls=%async_computation.2 | async-start | bytes 4456448 | tf_op jit(solution)/shard_map/all_to_all | solution.py:254
  150.0 38.6 %copy-start.5 = (s32[2,128]{1,0:T(2,128)S(1)}, s32[2,128]{1,0:T(2,128)}, u32[]{:S(2)}) copy-start(s32[2,128]{1,0:T(2,128)} %get-tuple-element.27.target_ref) | copy-start | bytes 3076
  150.0 5.6 %collective-permute-start = (bf16[1024,768]{1,0:T(8,128)(2,1)}, bf16[1024,768]{1,0:T(8,128)(2,1)S(1)}, u32[]{:S(2)}, u32[]{:S(2)}) collective-permute-start(bf16[1024,768]{1,0:T(8,128)(2,1)} %shard_map.109), channel_id=1, source_target_pairs={{0,1},{1,0},{2,3},{3,2},{4,5},{5,4},{6,7},{7,6},{8,9},{9,8},{10,11... | collective-permute-start | bytes 4718600 | tf_op jit(solution)/shard_map/ppermute | solution.py:334
  155.6 1.2 copy-start.2
  156.8 59.2 %copy-start.1 = (bf16[128,2]{0,1:T(2,128)(2,1)S(1)}, bf16[128,2]{0,1:T(2,128)(2,1)}, u32[]{:S(2)}) copy-start(bf16[128,2]{0,1:T(2,128)(2,1)} %param.13) | copy-start | bytes 1540
  161.6 19.8 %collective-permute-start.1 = (bf16[128,768]{1,0:T(8,128)(2,1)}, bf16[128,768]{1,0:T(8,128)(2,1)S(1)}, u32[]{:S(2)}, u32[]{:S(2)}) collective-permute-start(bf16[128,768]{1,0:T(8,128)(2,1)} %get-tuple-element.42), channel_id=1, source_target_pairs={{0,2},{2,4},{4,6},{6,8},{8,10},{10,12},{12,14},{14,0},{1,3},{3,5},... | collective-permute-start | bytes 589832 | tf_op jit(solution)/shard_map/ppermute | solution.py:351
  163.6 23.1 %collective-permute-start.2 = (bf16[128,768]{1,0:T(8,128)(2,1)}, bf16[128,768]{1,0:T(8,128)(2,1)S(1)}, u32[]{:S(2)}, u32[]{:S(2)}) collective-permute-start(bf16[128,768]{1,0:T(8,128)(2,1)} %get-tuple-element.43), channel_id=1, source_target_pairs={{0,4},{2,6},{4,8},{6,10},{8,12},{10,14},{12,0},{14,2},{1,5},{3,7},... | collective-permute-start | bytes 589832 | tf_op jit(solution)/shard_map/ppermute | solution.py:351
  167.8 24.8 %collective-permute-start.3 = (bf16[128,768]{1,0:T(8,128)(2,1)}, bf16[128,768]{1,0:T(8,128)(2,1)S(1)}, u32[]{:S(2)}, u32[]{:S(2)}) collective-permute-start(bf16[128,768]{1,0:T(8,128)(2,1)} %get-tuple-element.44), channel_id=1, source_target_pairs={{0,6},{2,8},{4,10},{6,12},{8,14},{10,0},{12,2},{14,4},{1,7},{3,9},... | collective-permute-start | bytes 589832 | tf_op jit(solution)/shard_map/ppermute | solution.py:351
  173.6 19.7 %collective-permute-start.4 = (bf16[128,768]{1,0:T(8,128)(2,1)}, bf16[128,768]{1,0:T(8,128)(2,1)S(1)}, u32[]{:S(2)}, u32[]{:S(2)}) collective-permute-start(bf16[128,768]{1,0:T(8,128)(2,1)} %get-tuple-element.45), channel_id=1, source_target_pairs={{0,8},{2,10},{4,12},{6,14},{8,0},{10,2},{12,4},{14,6},{1,9},{3,11}... | collective-permute-start | bytes 589832 | tf_op jit(solution)/shard_map/ppermute | solution.py:351
  176.6 27.9 %collective-permute-start.5 = (bf16[128,768]{1,0:T(8,128)(2,1)}, bf16[128,768]{1,0:T(8,128)(2,1)S(1)}, u32[]{:S(2)}, u32[]{:S(2)}) collective-permute-start(bf16[128,768]{1,0:T(8,128)(2,1)} %get-tuple-element.46), channel_id=1, source_target_pairs={{0,10},{2,12},{4,14},{6,0},{8,2},{10,4},{12,6},{14,8},{1,11},{3,13... | collective-permute-start | bytes 589832 | tf_op jit(solution)/shard_map/ppermute | solution.py:351
  181.4 26.6 %collective-permute-start.6 = (bf16[128,768]{1,0:T(8,128)(2,1)}, bf16[128,768]{1,0:T(8,128)(2,1)S(1)}, u32[]{:S(2)}, u32[]{:S(2)}) collective-permute-start(bf16[128,768]{1,0:T(8,128)(2,1)} %get-tuple-element.47), channel_id=1, source_target_pairs={{0,12},{2,14},{4,0},{6,2},{8,4},{10,6},{12,8},{14,10},{1,13},{3,15... | collective-permute-start | bytes 589832 | tf_op jit(solution)/shard_map/ppermute | solution.py:351
  186.7 26.4 %collective-permute-start.7 = (bf16[128,768]{1,0:T(8,128)(2,1)}, bf16[128,768]{1,0:T(8,128)(2,1)}, u32[]{:S(2)}, u32[]{:S(2)}) collective-permute-start(bf16[128,768]{1,0:T(8,128)(2,1)} %get-tuple-element.48), channel_id=1, source_target_pairs={{0,14},{2,0},{4,2},{6,4},{8,6},{10,8},{12,10},{14,12},{1,15},{3,1}... | collective-permute-start | bytes 589832 | tf_op jit(solution)/shard_map/ppermute | solution.py:351
  213.1 0.9 copy-start
Sparse Core Ops, SparseCore 0:
  10.1 43.8 all-gather.2
  56.7 44.6 all-gather.4

commit v5 on v2

v5 whole, which is shorter than its diff:
```python
import functools

import jax
import jax.numpy as jnp
from jax import lax
from jax.experimental import pallas as pl
from jax.experimental.pallas import tpu as pltpu
from jax.sharding import PartitionSpec as P

F32 = jnp.float32
BF16 = jnp.bfloat16
NT = (((1,), (1,)), ((), ()))
NN = (((1,), (0,)), ((), ()))
TN = (((0,), (0,)), ((), ()))


def mm(a, b, dims=NN):
    return lax.dot_general(a, b, dims, preferred_element_type=F32)


def one_hot(target, rows):
    tokens = target.shape[1]
    return lax.broadcasted_iota(jnp.int32, (rows, tokens), 0) == target


def route_kernel(experts, cap, ids_ref, x_any, send_any, target_ref, x, send, sems):
    load = pltpu.make_async_copy(x_any, x, sems.at[0])
    load.start()
    tokens, width = x.shape
    ids = ids_ref[...]
    members = [
        (lax.broadcasted_iota(jnp.int32, (experts, tokens), 0) == ids[k : k + 1]).astype(F32)
        for k in range(2)
    ]
    earlier = (
        lax.broadcasted_iota(jnp.int32, (tokens, tokens), 0)
        < lax.broadcasted_iota(jnp.int32, (tokens, tokens), 1)
    ).astype(F32)
    count = mm((members[0] + members[1]).astype(BF16), earlier.astype(BF16))
    half = experts * cap // 2
    sub = cap // 2
    targets = []
    for k in range(2):
        position = jnp.sum(members[k] * count, axis=0, keepdims=True).astype(jnp.int32)
        low = jnp.where(position < sub, position, position + (half - sub))
        targets.append(ids[k : k + 1] * sub + low)
        target_ref[k : k + 1, :] = targets[k]
    load.wait()
    block = half // 2
    stores = []
    for j in range(4):
        select = sum(one_hot(t - j * block, block).astype(F32) for t in targets)
        to = (slice(j % 2 * block, (j % 2 + 1) * block), slice(j // 2 * width, (j // 2 + 1) * width))
        send[to] = mm(select.astype(BF16), x[...]).astype(BF16)
        stores.append(pltpu.make_async_copy(send.at[to], send_any.at[to], sems.at[1 + j]))
        stores[j].start()
    for store in stores:
        store.wait()


def upstream_kernel(own_ref, names_ref, frames_ref, lm_ref, target_ref, gate_ref, send_ref):
    tokens = lm_ref.shape[0]
    frames = frames_ref.shape[0]
    own = lax.broadcasted_iota(jnp.int32, (tokens, frames), 0) + own_ref[0]
    named = (own == names_ref[...]).astype(F32)
    cond = mm(named.astype(BF16), frames_ref[...])
    upstream = (lm_ref[...].astype(F32) + cond).astype(BF16)
    half, width = send_ref.shape[0], lm_ref.shape[1]
    hot = [one_hot(target_ref[k : k + 1, :], 2 * half).astype(F32) for k in range(2)]
    gates = gate_ref[...].astype(F32)
    gate = jnp.sum(hot[0] * gates[0:1] + hot[1] * gates[1:2], axis=1, keepdims=True)
    scaled = (mm((hot[0] + hot[1]).astype(BF16), upstream) * gate).astype(BF16)
    send_ref[:, :width] = scaled[:half]
    send_ref[:, width:] = scaled[half:]


def forward_kernel(
    ff, place_ref, x_ref, w_ref, hidden_ref, gate_term_ref, up_term_ref, columns_ref, *keep
):
    half, width = x_ref.shape[0], x_ref.shape[1] // 2
    core = place_ref[1]
    for i in range(2):
        at = slice(i * half, (i + 1) * half)
        for j in range(width // 256):
            own = pl.ds(pl.multiple_of(i * width + (2 * j + core) * 128, 128), 128)
            away = pl.ds(pl.multiple_of(i * width + (2 * j + 1 - core) * 128, 128), 128)
            columns_ref[at, j * 128 : (j + 1) * 128] = x_ref[:, away]
            columns_ref[at, width // 2 + j * 128 : width // 2 + (j + 1) * 128] = x_ref[:, own]
        pre = mm(x_ref[:, i * width : (i + 1) * width], w_ref[:, : 2 * ff])
        gate_pre = pre[:, :ff]
        up_pre = pre[:, ff:]
        sig = jax.nn.sigmoid(gate_pre)
        activated = gate_pre * sig
        slope = sig * (1.0 + gate_pre * (1.0 - sig))
        hidden_ref[at, :] = (activated * up_pre).astype(BF16)
        gate_term_ref[at, :] = up_pre * slope
        up_term_ref[at, :] = activated
    for ref in keep:
        ref[...] = w_ref[...]


def backward_kernel(
    ff, y_any, w_any, hidden_any, gate_any, up_any, out_any, pre_any,
    y, wd, wg, hidden, gate_term, up_term, out, pre, sems,
):
    half, width = y_any.shape[0], y_any.shape[1] // 2
    chunk = width // 4
    copies = []

    def fetch(source, target):
        copies.append(pltpu.make_async_copy(source, target, sems.at[len(copies)]))
        copies[-1].start()

    for c in range(4):
        part = slice(c * chunk, (c + 1) * chunk)
        fetch(w_any.at[part, 2 * ff :], wd.at[part, :])
        for i in range(2):
            begin = i * width + c * chunk
            fetch(y_any.at[:, begin : begin + chunk], y.at[i * half : (i + 1) * half, part])
    hidden_grad = None
    for c in range(4):
        part = slice(c * chunk, (c + 1) * chunk)
        for n in range(3):
            copies[3 * c + n].wait()
        if c == 0:
            fetch(gate_any, gate_term)
            fetch(up_any, up_term)
            fetch(hidden_any, hidden)
        if c == 1:
            for j in range(4):
                to = slice(j * chunk, (j + 1) * chunk)
                fetch(w_any.at[to, : 2 * ff], wg.at[to, :])
        term = mm(y[:, part], wd[part, :])
        hidden_grad = term if hidden_grad is None else hidden_grad + term
    for n in range(12, 19):
        copies[n].wait()
    extra = jnp.zeros((half, 128), F32)
    lane = lax.broadcasted_iota(jnp.int32, (half, 128), 1)
    for i in range(2):
        at = slice(i * half, (i + 1) * half)
        grad = hidden_grad[at]
        pre[at, :ff] = (grad * gate_term[at, :]).astype(BF16)
        pre[at, ff:] = (grad * up_term[at, :]).astype(BF16)
        total = jnp.sum(hidden[at, :].astype(F32) * grad, axis=1, keepdims=True)
        high = total.astype(BF16).astype(F32)
        extra = jnp.where(lane // 64 == i, jnp.where(lane % 64 < 32, high, total - high), extra)
    out[:, 2 * width :] = extra.astype(BF16)
    fetch(out.at[:, 2 * width :], out_any.at[:, 2 * width :])
    for j in range(4):
        grads = mm(pre[...], wg[j * chunk : (j + 1) * chunk, :], NT).astype(BF16)
        for i in range(2):
            to = slice(i * width + j * chunk, i * width + (j + 1) * chunk)
            out[:, to] = grads[i * half : (i + 1) * half]
            fetch(out.at[:, to], out_any.at[:, to])
    fetch(pre, pre_any)
    for copy in copies[19:]:
        copy.wait()

def combine_kernel(back_any, column_ref, gate_ref, out_ref, gate_out_ref, back, sems):
    half = back.shape[0]
    tokens, width = out_ref.shape
    loads = []
    for i, part in enumerate((slice(0, width), slice(width, 2 * width + 128))):
        loads.append(pltpu.make_async_copy(back_any.at[:, part], back.at[:, part], sems.at[i]))
        loads[i].start()
    place = lax.broadcasted_iota(jnp.int32, (tokens, 2 * half), 1)
    picks = [(place == column_ref[:, k : k + 1]).astype(F32) for k in range(2)]
    pick = (picks[0] + picks[1]).astype(BF16)
    loads[0].wait()
    total = mm(pick[:, :half], back[:, :width])
    loads[1].wait()
    total += mm(pick[:, half:], back[:, width : 2 * width])
    out_ref[...] = total.astype(BF16)
    eye = (
        lax.broadcasted_iota(jnp.int32, (tokens, tokens), 0)
        == lax.broadcasted_iota(jnp.int32, (tokens, tokens), 1)
    ).astype(F32)
    for k in range(2):
        first = mm(picks[k][:, :half].astype(BF16), back[:, 2 * width :])
        second = mm(picks[k][:, half:].astype(BF16), back[:, 2 * width :])
        parts = first[:, 0:1] + first[:, 32:33] + second[:, 64:65] + second[:, 96:97]
        gate = jnp.sum(eye * parts, axis=0, keepdims=True)
        gate_out_ref[k : k + 1, :] = (gate / gate_ref[k : k + 1, :].astype(F32)).astype(BF16)


def call(kernel, outs, args, limit=60, **kw):
    return pl.pallas_call(
        kernel,
        out_shape=outs,
        compiler_params=pltpu.CompilerParams(vmem_limit_bytes=limit << 20),
        **kw,
    )(*args)


LONG = pl.CostEstimate(flops=1 << 40, bytes_accessed=1 << 30, transcendentals=0)


def ranked(values):
    return pl.pallas_call(
        lambda source, result: None,
        out_shape=jax.ShapeDtypeStruct(values.shape, values.dtype),
        in_specs=[pl.BlockSpec(memory_space=pl.ANY)],
        out_specs=pl.BlockSpec(memory_space=pl.ANY),
        input_output_aliases={0: 0},
        compiler_params=pltpu.CompilerParams(vmem_limit_bytes=1 << 20),
        cost_estimate=LONG,
    )(values)


def on_device(moe_input, lm_grad, frame_grad, span_token, expert_ids, gate_weights, w_gate_up, w_down):
    tokens, width = moe_input.shape
    per_span = frame_grad.shape[0] // span_token.shape[0]
    experts = lax.axis_size("expert")
    cap = 2 * tokens * expert_ids.shape[1] // experts
    rows = experts * cap
    half = rows // 2
    ff = w_down.shape[2]
    sds = jax.ShapeDtypeStruct
    any_space = pl.BlockSpec(memory_space=pl.ANY)
    vmem = pl.BlockSpec(memory_space=pltpu.VMEM)
    smem = pl.BlockSpec(memory_space=pltpu.SMEM)

    def exchange(values):
        return lax.all_to_all(
            values.reshape(experts, cap // 2, -1), "expert", split_axis=0, concat_axis=0, tiled=True
        ).reshape(half, -1)

    seq = lax.axis_index("seq")
    place = jnp.stack([seq, lax.axis_index("dp")]).astype(jnp.int32)
    frames = lax.all_gather(frame_grad, "seq", axis=0, tiled=True)

    gates = gate_weights.T
    send_input, target = call(
        functools.partial(route_kernel, experts, cap),
        (sds((half, 2 * width), BF16), sds((2, tokens), jnp.int32)),
        (expert_ids.T, moe_input),
        in_specs=[vmem, any_space],
        out_specs=[any_space, vmem],
        scratch_shapes=[
            pltpu.VMEM((tokens, width), BF16),
            pltpu.VMEM((half, 2 * width), BF16),
            pltpu.SemaphoreType.DMA((5,)),
        ],
    )
    got_input = ranked(exchange(send_input))

    w_gate_up, w_down, target = lax.optimization_barrier((w_gate_up, w_down, target))
    weights = jnp.concatenate([w_gate_up.reshape(-1, 2 * ff), w_down[0]], axis=1)
    weights = lax.all_gather(weights, ("seq", "dp"), axis=0, tiled=True)

    span_token, _ = lax.optimization_barrier((span_token, target))
    names = lax.all_gather(span_token, "seq", axis=0, tiled=True)
    names = jnp.repeat(names, per_span)[None, :]
    send_grad = call(
        upstream_kernel,
        sds((half, 2 * width), BF16),
        ((seq * tokens).reshape(1), names, frames, lm_grad, target, gates),
        in_specs=[smem] + [vmem] * 5,
        cost_estimate=LONG,
    )
    got_grad = exchange(send_grad)

    hidden, gate_term, up_term, columns = call(
        functools.partial(forward_kernel, ff),
        (
            sds((rows, ff), BF16), sds((rows, ff), F32), sds((rows, ff), F32),
            sds((rows, width), BF16),
        ),
        (place, got_input, weights),
        limit=60,
        in_specs=[smem, vmem, vmem],
    )
    input_grad, pre_grad = call(
        functools.partial(backward_kernel, ff),
        (sds((half, 2 * width + 128), BF16), sds((rows, 2 * ff), BF16)),
        (got_grad, weights, hidden, gate_term, up_term),
        in_specs=[any_space] * 5,
        out_specs=[any_space] * 2,
        scratch_shapes=[
            pltpu.VMEM((rows, width), BF16),
            pltpu.VMEM((width, ff), BF16),
            pltpu.VMEM((width, 2 * ff), BF16),
            pltpu.VMEM((rows, ff), BF16),
            pltpu.VMEM((rows, ff), F32),
            pltpu.VMEM((rows, ff), F32),
            pltpu.VMEM((half, 2 * width + 128), BF16),
            pltpu.VMEM((rows, 2 * ff), BF16),
            pltpu.SemaphoreType.DMA((29,)),
        ],
    )
    back = exchange(input_grad)

    partial = mm(columns, pre_grad, TN).astype(BF16)
    other = lax.ppermute(partial[: width // 2], "dp", [(0, 1), (1, 0)])
    pair = (partial[width // 2 :].astype(F32) + other.astype(F32)).astype(BF16)
    grad = lax.psum_scatter(pair, "seq", scatter_dimension=0, tiled=True).astype(F32)
    grad_gate_up = grad.reshape(1, -1, 2, ff)

    grad_input, grad_gates = call(
        combine_kernel,
        (sds((tokens, width), BF16), sds((2, tokens), BF16)),
        (back, target.T, gates),
        limit=20,
        in_specs=[any_space, vmem, vmem],
        out_specs=[vmem, vmem],
        scratch_shapes=[
            pltpu.VMEM((half, 2 * width + 128), BF16),
            pltpu.SemaphoreType.DMA((2,)),
        ],
        cost_estimate=LONG,
    )
    return grad_input, grad_gates.T, grad_gate_up


def solution(mesh):
    every = ("expert", "seq", "dp")
    return jax.shard_map(
        on_device,
        mesh=mesh,
        in_specs=(
            P(every, None),
            P(every, None),
            P(every, None),
            P(every),
            P(every, None),
            P(every, None),
            P("expert", ("seq", "dp"), None, None),
            P("expert", ("seq", "dp"), None),
        ),
        out_specs=(P(every, None), P(every, None), P("expert", ("seq", "dp"), None, None)),
        check_vma=False,
    )
```

time: 211 us -> 213 us (level)
  blocking collectives: 0 us -> 10.6 us
  waiting for transfers between devices: 128 us -> 119 us
    all_gather x1, waiting for transfers between devices: 42.3 us -> 13.6 us  [on_device(): frames = lax.all_gather(frame_grad, 'seq', axis=0, tiled=True)]
    all_to_all x3, waiting for transfers between devices: 51.5 us -> 76.8 us  [exchange(): lax.all_to_all(values.reshape(experts, cap // 2, -1), 'expert', split_axi...]
    all_gather x1, waiting for transfers between devices: 31.8 us -> 19.8 us  [on_device(): weights = lax.all_gather(weights, ('seq', 'dp'), axis=0, tiled=True)]
    unnamed x0 -> x1, blocking collectives: none -> 10.6 us
    reduce_scatter x1, waiting for transfers between devices: 0.01 us -> 4.43 us  [on_device(): lax.psum_scatter(pair, 'seq', scatter_dimension=0, tiled=True).astype(F32)]
  transfers between devices with their start and end apart: 7 -> 7, of which waited for: 6 -> 7; matrix products, arithmetic and copies ran while one was open for 4% -> 6% of each run, Pallas kernels for 6% -> 8%
where the time goes in v5:
time: 213 us; the launch traced here: 210 us
  waiting for transfers between devices  119 us (56%)
  starting transfers between devices  28 us (13%)
  Pallas kernels  23 us (11%)
  between operations  14.6 us (7%)
  blocking collectives  10.6 us (5%)
  local copies, waits for them, and re-layouts  6.54 us (3%)
  other arithmetic  4.89 us (2%)
  matrix products  3.43 us (2%)
    all_to_all x3, waiting for transfers between devices, exchange(): lax.all_to_all(values.reshape(experts, cap // 2, -1), 'expert', split_axi...  76.8 us
    all_to_all x3, starting transfers between devices, exchange(): lax.all_to_all(values.reshape(experts, cap // 2, -1), 'expert', split_axi...  26 us
    pallas_call x5, Pallas kernels, call(): pl.pallas_call(kernel, out_shape=outs, compiler_params=pltpu.CompilerPara...  23 us
    all_gather x1, waiting for transfers between devices, on_device(): weights = lax.all_gather(weights, ('seq', 'dp'), axis=0, tiled=True)  19.8 us
    all_gather x1, waiting for transfers between devices, on_device(): frames = lax.all_gather(frame_grad, 'seq', axis=0, tiled=True)  13.6 us
    unnamed x1, blocking collectives  10.6 us
    reduce_scatter x1, waiting for transfers between devices, on_device(): lax.psum_scatter(pair, 'seq', scatter_dimension=0, tiled=True).astype(F32)  4.43 us
  transfers between devices with their start and end apart: 7, of which 7 were waited for; matrix products, arithmetic and copies ran while one was open for 6% of the time, Pallas kernels for 8%

profile of v5, /device:TPU:56, one launch (start us, length us, event | category | flops | bytes accessed | tf_op | source)
XLA Modules:
  0.0 210.0 jit_solution(5608983057926463006)
XLA Ops:
  7.2 0.7 all-gather.3.cloned.1.call-update
  7.9 4.0 %shard_map.103 = (bf16[256,4096]{1,0:T(8,128)(2,1)}, s32[2,128]{1,0:T(2,128)}) custom-call(s32[2,128]{1,0:T(2,128)} %bitcast.30, bf16[128,2048]{1,0:T(8,128)(2,1)} %x_any.1), custom_call_target="tpu_custom_call" | custom-call | tf_op jit(solution)/shard_map/pallas_call | solution.py:187
  11.9 13.4 %all-to-all-start.1 = ((bf16[32,8,4096]{2,1,0:T(8,128)(2,1)}), bf16[32,8,4096]{2,1,0:T(8,128)(2,1)}, u32[]{:S(2)}, u32[]{:S(2)}) async-start(bf16[32,8,4096]{2,1,0:T(8,128)(2,1)} %bitcast.25), calls=%async_computation.1 | async-start | bytes 4194304 | tf_op jit(solution)/shard_map/all_to_all | solution.py:224
  25.4 0.0 all-gather.5.cloned.1.call-start
  25.5 0.7 pad_maximum_fusion
  26.3 1.3 dynamic-slice
  28.2 0.2 dynamic-update-slice
  28.4 10.6 %all-reduce = s32[64]{0:T(128)S(1)} all-reduce(s32[64]{0:T(128)S(1)} %dynamic-update-slice), channel_id=1, replica_groups=mesh['expert'=32,'seq'=8,'dp'=2] {'seq'}, use_global_device_ids=true, to_apply=%add | all-reduce | flops 64 | bytes 512
  39.1 0.1 broadcast_in_dim.3
  39.1 0.7 broadcast_in_dim_reshape.3.names_ref
  39.8 0.7 pad_add_fusion.place_ref
  40.5 13.6 %all-gather.3.cloned.1.call-done.frames_ref = bf16[256,2048]{1,0:T(8,128)(2,1)} async-done(((bf16[32,2048]{1,0:T(8,128)(2,1)}), bf16[256,2048]{1,0:T(8,128)(2,1)}) %all-gather.3.cloned.1.call-update) | async-done | bytes 1048592 | tf_op jit(solution)/shard_map/all_gather | solution.py:230
  54.1 3.6 %shard_map.104 = bf16[256,4096]{1,0:T(8,128)(2,1)} custom-call(s32[1]{0:T(128)} %bitcast.own_ref, s32[1,256]{1,0:T(1,128)} %broadcast_in_dim_reshape.3.names_ref, bf16[256,2048]{1,0:T(8,128)(2,1)} %all-gather.3.cloned.1.call-done.frames_ref, bf16[128,2048]{1,0:T(8,128)(2,1)} %lm_ref.1, s32[2,128]{1,0:T(2,128)} %get-tuple-element.18.target_ref, ...), custom_call_target="tpu_custom_call" | custom-call | flops 1099511627776 | bytes 1073741824 | tf_op jit(solution)/shard_map/pallas_call | solution.py:187
  57.7 17.7 %all-to-all-done.1 = bf16[32,8,4096]{2,1,0:T(8,128)(2,1)} async-done(((bf16[32,8,4096]{2,1,0:T(8,128)(2,1)}), bf16[32,8,4096]{2,1,0:T(8,128)(2,1)}, u32[]{:S(2)}, u32[]{:S(2)}) %all-to-all-start.1) | async-done | bytes 2097184 | tf_op jit(solution)/shard_map/all_to_all | solution.py:224
  75.4 6.3 %all-to-all-start = ((bf16[32,8,4096]{2,1,0:T(8,128)(2,1)}), bf16[32,8,4096]{2,1,0:T(8,128)(2,1)}, u32[]{:S(2)}, u32[]{:S(2)}) async-start(bf16[32,8,4096]{2,1,0:T(8,128)(2,1)} %bitcast.26), calls=%async_computation | async-start | bytes 4194304 | tf_op jit(solution)/shard_map/all_to_all | solution.py:224
  81.7 19.8 %all-gather.5.cloned.1.call-done.w_ref.w_any = bf16[2048,1152]{1,0:T(8,128)(2,1)} async-done(((bf16[128,1152]{1,0:T(8,128)(2,1)}), bf16[2048,1152]{1,0:T(8,128)(2,1)}) %all-gather.5.cloned.1.call-update) | async-done | bytes 4718608 | tf_op jit(solution)/shard_map/all_gather | solution.py:249
  101.5 7.0 %shard_map.106 = (bf16[512,384]{1,0:T(8,128)(2,1)}, f32[512,384]{1,0:T(8,128)}, f32[512,384]{1,0:T(8,128)}, bf16[512,2048]{1,0:T(8,128)(2,1)}) custom-call(s32[2]{0:T(128)} %pad_add_fusion.place_ref, bf16[256,4096]{1,0:T(8,128)(2,1)} %shard_map.105.x_ref, bf16[2048,1152]{1,0:T(8,128)(2,1)} %all-gather.5.cloned.1.call-done.w_ref.w_any), custom_call_target="tpu_custom_call" | custom-call | tf_op jit(solution)/shard_map/pallas_call | solution.py:187
  108.4 23.0 %all-to-all-done = bf16[32,8,4096]{2,1,0:T(8,128)(2,1)} async-done(((bf16[32,8,4096]{2,1,0:T(8,128)(2,1)}), bf16[32,8,4096]{2,1,0:T(8,128)(2,1)}, u32[]{:S(2)}, u32[]{:S(2)}) %all-to-all-start) | async-done | bytes 2097184 | tf_op jit(solution)/shard_map/all_to_all | solution.py:224
  131.4 6.8 %shard_map.107 = (bf16[256,4224]{1,0:T(8,128)(2,1)}, bf16[512,768]{1,0:T(8,128)(2,1)}) custom-call(bf16[256,4096]{1,0:T(8,128)(2,1)} %bitcast.5.y_any, bf16[2048,1152]{1,0:T(8,128)(2,1)} %all-gather.5.cloned.1.call-done.w_ref.w_any, bf16[512,384]{1,0:T(8,128)(2,1)} %get-tuple-element.23.hidden_any, f32[512,384]{1,0:T(8,128)} %get-tuple-element.24.gate_any, ...), custom_call_target="tpu_custom_call" | custom-call | tf_op jit(solution)/shard_map/pallas_call | solution.py:187
  138.3 6.3 %all-to-all-start.2 = ((bf16[32,8,4224]{2,1,0:T(8,128)(2,1)}), bf16[32,8,4224]{2,1,0:T(8,128)(2,1)S(1)}, u32[]{:S(2)}, u32[]{:S(2)}) async-start(bf16[32,8,4224]{2,1,0:T(8,128)(2,1)} %bitcast.24), calls=%async_computation.2 | async-start | bytes 4325376 | tf_op jit(solution)/shard_map/all_to_all | solution.py:224
  144.5 0.0 reduce-scatter.2.cloned.1.call-start
  144.6 3.4 %convolution_convert_fusion = bf16[2048,768]{1,0:T(8,128)(2,1)S(1)} fusion(bf16[512,2048]{1,0:T(8,128)(2,1)} %get-tuple-element.29, bf16[512,768]{1,0:T(8,128)(2,1)S(1)} %copy-done.5), kind=kOutput, calls=%fused_computation | convolution fusion | flops 1612185600 | bytes 6029312 | tf_op jit(solution)/shard_map/dot_general | solution.py:18
  148.0 1.4 slice.9
  149.5 0.8 copy-done.1
  150.3 1.9 collective-permute-start
  152.2 0.1 copy.13
  152.3 3.6 %collective-permute-done = bf16[1024,768]{1,0:T(8,128)(2,1)} collective-permute-done((bf16[1024,768]{1,0:T(8,128)(2,1)}, bf16[1024,768]{1,0:T(8,128)(2,1)}, u32[]{:S(2)}, u32[]{:S(2)}) %collective-permute-start) | collective-permute-done | bytes 1572896 | tf_op jit(solution)/shard_map/ppermute | solution.py:294
  155.9 3.5 %add_convert_fusion = bf16[1024,768]{1,0:T(8,128)(2,1)} fusion(bf16[1024,768]{1,0:T(8,128)(2,1)} %collective-permute-done, bf16[2048,768]{1,0:T(8,128)(2,1)} %copy-done.1), kind=kLoop, calls=%fused_computation.1 | loop fusion | flops 3145728 | bytes 4718592 | tf_op jit(solution)/shard_map/convert_element_type | solution.py:295
  159.4 36.1 %all-to-all-done.2 = bf16[32,8,4224]{2,1,0:T(8,128)(2,1)S(1)} async-done(((bf16[32,8,4224]{2,1,0:T(8,128)(2,1)}), bf16[32,8,4224]{2,1,0:T(8,128)(2,1)S(1)}, u32[]{:S(2)}, u32[]{:S(2)}) %all-to-all-start.2) | async-done | bytes 2162720 | tf_op jit(solution)/shard_map/all_to_all | solution.py:224
  195.5 1.6 shard_map.108
  197.1 4.4 %reduce-scatter.2.cloned.1.call-done = bf16[128,768]{1,0:T(8,128)(2,1)} async-done(((bf16[1024,768]{1,0:T(8,128)(2,1)}), bf16[128,768]{1,0:T(8,128)(2,1)}) %reduce-scatter.2.cloned.1.call-update) | async-done | bytes 196624 | tf_op jit(solution)/shard_map/reduce_scatter | solution.py:296
  201.6 1.9 reshape.47
  (19 shorter events, 0.1 us)
Async XLA Ops:
  7.2 46.9 %all-gather.3.cloned.1.call-start = ((), (), s32[]{:S(2)}) async-start(), calls=%async_computation.4 | async-start | bytes 1179648 | tf_op jit(solution)/shard_map/all_gather | solution.py:230
  11.9 13.5 %copy-start.2 = (bf16[1,128,2,384]{3,2,1,0:T(2,128)(2,1)S(1)}, bf16[1,128,2,384]{3,2,1,0:T(2,128)(2,1)}, u32[]{:S(2)}) copy-start(bf16[1,128,2,384]{3,2,1,0:T(2,128)(2,1)} %param.14) | copy-start | bytes 589828
  11.9 13.6 %copy-start.3 = (bf16[1,128,384]{2,1,0:T(8,128)(2,1)S(1)}, bf16[1,128,384]{2,1,0:T(8,128)(2,1)}, u32[]{:S(2)}) copy-start(bf16[1,128,384]{2,1,0:T(8,128)(2,1)} %param.15) | copy-start | bytes 294916
  11.9 16.3 %copy-start.6 = (s32[8]{0:T(128)S(1)}, s32[8]{0:T(128)}, u32[]{:S(2)}) copy-start(s32[8]{0:T(128)} %param.11) | copy-start | bytes 100
  11.9 63.5 %all-to-all-start.1 = ((bf16[32,8,4096]{2,1,0:T(8,128)(2,1)}), bf16[32,8,4096]{2,1,0:T(8,128)(2,1)}, u32[]{:S(2)}, u32[]{:S(2)}) async-start(bf16[32,8,4096]{2,1,0:T(8,128)(2,1)} %bitcast.25), calls=%async_computation.1 | async-start | bytes 4194304 | tf_op jit(solution)/shard_map/all_to_all | solution.py:224
  25.4 76.1 %all-gather.5.cloned.1.call-start = ((), (), s32[]{:S(2)}) async-start(), calls=%async_computation.5 | async-start | bytes 5013504 | tf_op jit(solution)/shard_map/all_gather | solution.py:249
  75.4 56.0 %all-to-all-start = ((bf16[32,8,4096]{2,1,0:T(8,128)(2,1)}), bf16[32,8,4096]{2,1,0:T(8,128)(2,1)}, u32[]{:S(2)}, u32[]{:S(2)}) async-start(bf16[32,8,4096]{2,1,0:T(8,128)(2,1)} %bitcast.26), calls=%async_computation | async-start | bytes 4194304 | tf_op jit(solution)/shard_map/all_to_all | solution.py:224
  138.2 6.3 %copy-start.5 = (bf16[512,768]{1,0:T(8,128)(2,1)S(1)}, bf16[512,768]{1,0:T(8,128)(2,1)}, u32[]{:S(2)}) copy-start(bf16[512,768]{1,0:T(8,128)(2,1)} %get-tuple-element.30) | copy-start | bytes 2359300
  138.3 57.3 %all-to-all-start.2 = ((bf16[32,8,4224]{2,1,0:T(8,128)(2,1)}), bf16[32,8,4224]{2,1,0:T(8,128)(2,1)S(1)}, u32[]{:S(2)}, u32[]{:S(2)}) async-start(bf16[32,8,4224]{2,1,0:T(8,128)(2,1)} %bitcast.24), calls=%async_computation.2 | async-start | bytes 4325376 | tf_op jit(solution)/shard_map/all_to_all | solution.py:224
  144.5 57.0 %reduce-scatter.2.cloned.1.call-start = ((), (), s32[]{:S(2)}) async-start(), calls=%async_computation.6 | async-start | bytes 1769472 | tf_op jit(solution)/shard_map/reduce_scatter | solution.py:296
  148.0 2.2 %copy-start.1 = (bf16[2048,768]{1,0:T(8,128)(2,1)}, bf16[2048,768]{1,0:T(8,128)(2,1)S(1)}, u32[]{:S(2)}) copy-start(bf16[2048,768]{1,0:T(8,128)(2,1)S(1)} %convolution_convert_fusion) | copy-start | bytes 9437188
  148.0 4.2 %copy-start.4 = (s32[2,128]{1,0:T(2,128)S(1)}, s32[2,128]{1,0:T(2,128)}, u32[]{:S(2)}) copy-start(s32[2,128]{1,0:T(2,128)} %get-tuple-element.18.target_ref) | copy-start | bytes 3076
  150.3 5.6 %collective-permute-start = (bf16[1024,768]{1,0:T(8,128)(2,1)}, bf16[1024,768]{1,0:T(8,128)(2,1)}, u32[]{:S(2)}, u32[]{:S(2)}) collective-permute-start(bf16[1024,768]{1,0:T(8,128)(2,1)} %slice.9), channel_id=1, source_target_pairs={{0,1},{1,0},{2,3},{3,2},{4,5},{5,4},{6,7},{7,6},{8,9},{9,8},{10,11... | collective-permute-start | bytes 4718600 | tf_op jit(solution)/shard_map/ppermute | solution.py:294
  152.3 43.2 %copy-start = (bf16[128,2]{0,1:T(2,128)(2,1)S(1)}, bf16[128,2]{0,1:T(2,128)(2,1)}, u32[]{:S(2)}) copy-start(bf16[128,2]{0,1:T(2,128)(2,1)} %param.13) | copy-start | bytes 1540
Sparse Core Ops, SparseCore 0:
  10.1 43.9 all-gather.2
  56.8 44.6 all-gather.4
  159.6 41.9 reduce-scatter.1

commit v6 on v5

--- a/solution.py
+++ b/solution.py
@@ -75,7 +75,7 @@
 
 
 def forward_kernel(
-    ff, place_ref, x_ref, w_ref, hidden_ref, gate_term_ref, up_term_ref, columns_ref, *keep
+    ff, place_ref, x_ref, w_ref, hidden_ref, gate_term_ref, up_term_ref, mine_ref, other_ref
 ):
     half, width = x_ref.shape[0], x_ref.shape[1] // 2
     core = place_ref[1]
@@ -84,8 +84,8 @@
         for j in range(width // 256):
             own = pl.ds(pl.multiple_of(i * width + (2 * j + core) * 128, 128), 128)
             away = pl.ds(pl.multiple_of(i * width + (2 * j + 1 - core) * 128, 128), 128)
-            columns_ref[at, j * 128 : (j + 1) * 128] = x_ref[:, away]
-            columns_ref[at, width // 2 + j * 128 : width // 2 + (j + 1) * 128] = x_ref[:, own]
+            mine_ref[at, j * 128 : (j + 1) * 128] = x_ref[:, own]
+            other_ref[at, j * 128 : (j + 1) * 128] = x_ref[:, away]
         pre = mm(x_ref[:, i * width : (i + 1) * width], w_ref[:, : 2 * ff])
         gate_pre = pre[:, :ff]
         up_pre = pre[:, ff:]
@@ -95,8 +95,6 @@
         hidden_ref[at, :] = (activated * up_pre).astype(BF16)
         gate_term_ref[at, :] = up_pre * slope
         up_term_ref[at, :] = activated
-    for ref in keep:
-        ref[...] = w_ref[...]
 
 
 def backward_kernel(
@@ -260,16 +258,19 @@
     )
     got_grad = exchange(send_grad)
 
-    hidden, gate_term, up_term, columns = call(
+    hidden, gate_term, up_term, x_mine, x_other = call(
         functools.partial(forward_kernel, ff),
         (
             sds((rows, ff), BF16), sds((rows, ff), F32), sds((rows, ff), F32),
-            sds((rows, width), BF16),
+            sds((rows, width // 2), BF16), sds((rows, width // 2), BF16),
         ),
         (place, got_input, weights),
         limit=60,
         in_specs=[smem, vmem, vmem],
     )
+    swap = [(0, 1), (1, 0)]
+    x_other = lax.ppermute(x_other, "dp", swap)
+    hidden, x_other = lax.optimization_barrier((hidden, x_other))
     input_grad, pre_grad = call(
         functools.partial(backward_kernel, ff),
         (sds((half, 2 * width + 128), BF16), sds((rows, 2 * ff), BF16)),
@@ -290,9 +291,8 @@
     )
     back = exchange(input_grad)
 
-    partial = mm(columns, pre_grad, TN).astype(BF16)
-    other = lax.ppermute(partial[: width // 2], "dp", [(0, 1), (1, 0)])
-    pair = (partial[width // 2 :].astype(F32) + other.astype(F32)).astype(BF16)
+    pre_other = lax.ppermute(pre_grad, "dp", swap)
+    pair = (mm(x_mine, pre_grad, TN) + mm(x_other, pre_other, TN)).astype(BF16)
     grad = lax.psum_scatter(pair, "seq", scatter_dimension=0, tiled=True).astype(F32)
     grad_gate_up = grad.reshape(1, -1, 2, ff)
 

time: 213 us -> 207 us (0.972); the launches traced: 210 us -> 207 us
  other arithmetic: 4.89 us -> 1.35 us
  matrix products: 3.43 us -> 5.85 us
  local copies, waits for them, and re-layouts: 6.54 us -> 4.31 us
    all_to_all x3, waiting for transfers between devices: 76.8 us -> 37.8 us  [exchange(): lax.all_to_all(values.reshape(experts, cap // 2, -1), 'expert', split_axi...]
    reduce_scatter x1, waiting for transfers between devices: 4.43 us -> 42 us  [on_device(): lax.psum_scatter(pair, 'seq', scatter_dimension=0, tiled=True).astype(F32)]
    convert_element_type x1 -> x0, other arithmetic: 3.51 us -> none  [on_device(): pair = (partial[width // 2:].astype(F32) + other.astype(F32)).astype(BF16)]
    dot_general x1 -> x2, matrix products: 3.43 us -> 5.85 us  [mm(): return lax.dot_general(a, b, dims, preferred_element_type=F32)]
    ppermute x1 -> x2, starting transfers between devices: 1.91 us -> 4.05 us  [the longest x1 2.13 us: on_device(): x_other = lax.ppermute(x_other, 'dp', swap)]
  transfers between devices with their start and end apart: 7 -> 8, of which waited for: 7 -> 7; matrix products, arithmetic and copies ran while one was open for 6% -> 6% of each run, Pallas kernels for 8% -> 7%
where the time goes in v6:
time: 207 us
  waiting for transfers between devices  117 us (57%)
  starting transfers between devices  30.1 us (15%)
  Pallas kernels  23.1 us (11%)
  between operations  14.6 us (7%)
  blocking collectives  10.7 us (5%)
  matrix products  5.85 us (3%)
  local copies, waits for them, and re-layouts  4.31 us (2%)
    reduce_scatter x1, waiting for transfers between devices, on_device(): lax.psum_scatter(pair, 'seq', scatter_dimension=0, tiled=True).astype(F32)  42 us
    all_to_all x3, waiting for transfers between devices, exchange(): lax.all_to_all(values.reshape(experts, cap // 2, -1), 'expert', split_axi...  37.8 us
    all_to_all x3, starting transfers between devices, exchange(): lax.all_to_all(values.reshape(experts, cap // 2, -1), 'expert', split_axi...  26 us
    pallas_call x5, Pallas kernels, call(): pl.pallas_call(kernel, out_shape=outs, compiler_params=pltpu.CompilerPara...  23.1 us
    all_gather x1, waiting for transfers between devices, on_device(): weights = lax.all_gather(weights, ('seq', 'dp'), axis=0, tiled=True)  19.8 us
    all_gather x1, waiting for transfers between devices, on_device(): frames = lax.all_gather(frame_grad, 'seq', axis=0, tiled=True)  13.6 us
    unnamed x1, blocking collectives  10.7 us
    dot_general x2, matrix products, mm(): return lax.dot_general(a, b, dims, preferred_element_type=F32)  5.85 us
  transfers between devices with their start and end apart: 8, of which 7 were waited for; matrix products, arithmetic and copies ran while one was open for 6% of the time, Pallas kernels for 7%

profile of v6, /device:TPU:56, one launch (start us, length us, event | category | flops | bytes accessed | tf_op | source)
XLA Modules:
  0.0 206.6 jit_solution(14628798975270864418)
XLA Ops:
  7.2 0.0 all-gather.3.cloned.1.call-start
  7.2 0.7 all-gather.3.cloned.1.call-update
  7.9 3.9 %shard_map.103 = (bf16[256,4096]{1,0:T(8,128)(2,1)}, s32[2,128]{1,0:T(2,128)}) custom-call(s32[2,128]{1,0:T(2,128)} %bitcast.32, bf16[128,2048]{1,0:T(8,128)(2,1)} %x_any.1), custom_call_target="tpu_custom_call" | custom-call | tf_op jit(solution)/shard_map/pallas_call | solution.py:185
  11.9 13.4 %all-to-all-start.1 = ((bf16[32,8,4096]{2,1,0:T(8,128)(2,1)}), bf16[32,8,4096]{2,1,0:T(8,128)(2,1)}, u32[]{:S(2)}, u32[]{:S(2)}) async-start(bf16[32,8,4096]{2,1,0:T(8,128)(2,1)} %bitcast.27), calls=%async_computation.1 | async-start | bytes 4194304 | tf_op jit(solution)/shard_map/all_to_all | solution.py:222
  25.3 0.0 all-gather.5.cloned.1.call-start
  25.4 0.7 pad_maximum_fusion
  26.2 1.3 dynamic-slice
  28.1 0.2 dynamic-update-slice
  28.4 10.7 %all-reduce = s32[64]{0:T(128)S(1)} all-reduce(s32[64]{0:T(128)S(1)} %dynamic-update-slice), channel_id=1, replica_groups=mesh['expert'=32,'seq'=8,'dp'=2] {'seq'}, use_global_device_ids=true, to_apply=%add | all-reduce | flops 64 | bytes 512
  39.1 0.1 broadcast_in_dim.3
  39.2 0.7 broadcast_in_dim_reshape.3.names_ref
  39.8 0.6 pad_add_fusion.place_ref
  40.4 13.6 %all-gather.3.cloned.1.call-done.frames_ref = bf16[256,2048]{1,0:T(8,128)(2,1)} async-done(((bf16[32,2048]{1,0:T(8,128)(2,1)}), bf16[256,2048]{1,0:T(8,128)(2,1)}) %all-gather.3.cloned.1.call-update) | async-done | bytes 1048592 | tf_op jit(solution)/shard_map/all_gather | solution.py:228
  54.0 3.6 %shard_map.104 = bf16[256,4096]{1,0:T(8,128)(2,1)} custom-call(s32[1]{0:T(128)} %bitcast.own_ref, s32[1,256]{1,0:T(1,128)} %broadcast_in_dim_reshape.3.names_ref, bf16[256,2048]{1,0:T(8,128)(2,1)} %all-gather.3.cloned.1.call-done.frames_ref, bf16[128,2048]{1,0:T(8,128)(2,1)} %lm_ref.1, s32[2,128]{1,0:T(2,128)} %get-tuple-element.21.target_ref, ...), custom_call_target="tpu_custom_call" | custom-call | flops 1099511627776 | bytes 1073741824 | tf_op jit(solution)/shard_map/pallas_call | solution.py:185
  57.6 17.7 %all-to-all-done.1 = bf16[32,8,4096]{2,1,0:T(8,128)(2,1)} async-done(((bf16[32,8,4096]{2,1,0:T(8,128)(2,1)}), bf16[32,8,4096]{2,1,0:T(8,128)(2,1)}, u32[]{:S(2)}, u32[]{:S(2)}) %all-to-all-start.1) | async-done | bytes 2097184 | tf_op jit(solution)/shard_map/all_to_all | solution.py:222
  75.4 6.3 %all-to-all-start = ((bf16[32,8,4096]{2,1,0:T(8,128)(2,1)}), bf16[32,8,4096]{2,1,0:T(8,128)(2,1)}, u32[]{:S(2)}, u32[]{:S(2)}) async-start(bf16[32,8,4096]{2,1,0:T(8,128)(2,1)} %bitcast.28), calls=%async_computation | async-start | bytes 4194304 | tf_op jit(solution)/shard_map/all_to_all | solution.py:222
  81.6 19.8 %all-gather.5.cloned.1.call-done.w_ref.w_any = bf16[2048,1152]{1,0:T(8,128)(2,1)} async-done(((bf16[128,1152]{1,0:T(8,128)(2,1)}), bf16[2048,1152]{1,0:T(8,128)(2,1)}) %all-gather.5.cloned.1.call-update) | async-done | bytes 4718608 | tf_op jit(solution)/shard_map/all_gather | solution.py:247
  101.4 7.0 %shard_map.106 = (bf16[512,384]{1,0:T(8,128)(2,1)}, f32[512,384]{1,0:T(8,128)}, f32[512,384]{1,0:T(8,128)}, bf16[512,1024]{1,0:T(8,128)(2,1)}, bf16[512,1024]{1,0:T(8,128)(2,1)}) custom-call(s32[2]{0:T(128)} %pad_add_fusion.place_ref, bf16[256,4096]{1,0:T(8,128)(2,1)} %shard_map.105.x_ref, bf16[2048,1152]{1,0:T(8,128)(2,1)} %all-gather.5.cloned.1.call-done.w_ref.w_any), custom_call_target="tpu_custom_call" | custom-call | tf_op jit(solution)/shard_map/pallas_call | solution.py:185
  108.4 2.1 %collective-permute-start = (bf16[512,1024]{1,0:T(8,128)(2,1)}, bf16[512,1024]{1,0:T(8,128)(2,1)}, u32[]{:S(2)}, u32[]{:S(2)}) collective-permute-start(bf16[512,1024]{1,0:T(8,128)(2,1)} %get-tuple-element.27), channel_id=1, source_target_pairs={{0,1},{1,0},{2,3},{3,2},{4,5},{5,4},{6,7},{7,6},{8,9},{9,8},{10,11... | collective-permute-start | bytes 3145736 | tf_op jit(solution)/shard_map/ppermute | solution.py:272
  110.5 2.7 %collective-permute-done = bf16[512,1024]{1,0:T(8,128)(2,1)} collective-permute-done((bf16[512,1024]{1,0:T(8,128)(2,1)}, bf16[512,1024]{1,0:T(8,128)(2,1)}, u32[]{:S(2)}, u32[]{:S(2)}) %collective-permute-start) | collective-permute-done | bytes 1048608 | tf_op jit(solution)/shard_map/ppermute | solution.py:272
  113.3 18.1 %all-to-all-done = bf16[32,8,4096]{2,1,0:T(8,128)(2,1)} async-done(((bf16[32,8,4096]{2,1,0:T(8,128)(2,1)}), bf16[32,8,4096]{2,1,0:T(8,128)(2,1)}, u32[]{:S(2)}, u32[]{:S(2)}) %all-to-all-start) | async-done | bytes 2097184 | tf_op jit(solution)/shard_map/all_to_all | solution.py:222
  131.4 6.9 %shard_map.107 = (bf16[256,4224]{1,0:T(8,128)(2,1)}, bf16[512,768]{1,0:T(8,128)(2,1)}) custom-call(bf16[256,4096]{1,0:T(8,128)(2,1)} %bitcast.5.y_any, bf16[2048,1152]{1,0:T(8,128)(2,1)} %all-gather.5.cloned.1.call-done.w_ref.w_any, bf16[512,384]{1,0:T(8,128)(2,1)} %get-tuple-element.28.hidden_any, f32[512,384]{1,0:T(8,128)} %get-tuple-element.29.gate_any, ...), custom_call_target="tpu_custom_call" | custom-call | tf_op jit(solution)/shard_map/pallas_call | solution.py:185
  138.3 1.9 collective-permute-start.1
  140.2 6.3 %all-to-all-start.2 = ((bf16[32,8,4224]{2,1,0:T(8,128)(2,1)}), bf16[32,8,4224]{2,1,0:T(8,128)(2,1)S(1)}, u32[]{:S(2)}, u32[]{:S(2)}) async-start(bf16[32,8,4224]{2,1,0:T(8,128)(2,1)} %bitcast.26), calls=%async_computation.2 | async-start | bytes 4325376 | tf_op jit(solution)/shard_map/all_to_all | solution.py:222
  146.5 0.0 reduce-scatter.2.cloned.1.call-start
  146.6 2.2 %fusion = f32[1024,768]{1,0:T(8,128)S(1)} fusion(bf16[512,1024]{1,0:T(8,128)(2,1)S(1)} %copy-done.1, bf16[512,768]{1,0:T(8,128)(2,1)} %get-tuple-element.35), kind=kOutput, calls=%fused_computation.3 | convolution fusion | flops 805306368 | bytes 4980736 | tf_op jit(solution)/shard_map/dot_general | solution.py:18
  148.8 3.7 %add_convert_fusion = bf16[1024,768]{1,0:T(8,128)(2,1)} fusion(f32[1024,768]{1,0:T(8,128)S(1)} %fusion, bf16[512,1024]{1,0:T(8,128)(2,1)} %collective-permute-done, bf16[512,768]{1,0:T(8,128)(2,1)} %collective-permute-done.1), kind=kOutput, calls=%fused_computation | convolution fusion | flops 806879232 | bytes 6553600 | tf_op jit(solution)/shard_map/dot_general | solution.py:18
  152.5 0.1 copy.13
  152.6 42.0 %reduce-scatter.2.cloned.1.call-done = bf16[128,768]{1,0:T(8,128)(2,1)} async-done(((bf16[1024,768]{1,0:T(8,128)(2,1)}), bf16[128,768]{1,0:T(8,128)(2,1)}) %reduce-scatter.2.cloned.1.call-update) | async-done | bytes 196624 | tf_op jit(solution)/shard_map/reduce_scatter | solution.py:296
  194.6 1.9 reshape.47
  196.5 2.0 all-to-all-done.2
  198.4 1.6 shard_map.108
  (18 shorter events, 0.1 us)
Async XLA Ops:
  7.2 46.8 %all-gather.3.cloned.1.call-start = ((), (), s32[]{:S(2)}) async-start(), calls=%async_computation.4 | async-start | bytes 1179648 | tf_op jit(solution)/shard_map/all_gather | solution.py:228
  11.8 13.5 %copy-start.2 = (bf16[1,128,2,384]{3,2,1,0:T(2,128)(2,1)S(1)}, bf16[1,128,2,384]{3,2,1,0:T(2,128)(2,1)}, u32[]{:S(2)}) copy-start(bf16[1,128,2,384]{3,2,1,0:T(2,128)(2,1)} %param.14) | copy-start | bytes 589828
  11.9 13.6 %copy-start.3 = (bf16[1,128,384]{2,1,0:T(8,128)(2,1)S(1)}, bf16[1,128,384]{2,1,0:T(8,128)(2,1)}, u32[]{:S(2)}) copy-start(bf16[1,128,384]{2,1,0:T(8,128)(2,1)} %param.15) | copy-start | bytes 294916
  11.9 16.3 %copy-start.5 = (s32[8]{0:T(128)S(1)}, s32[8]{0:T(128)}, u32[]{:S(2)}) copy-start(s32[8]{0:T(128)} %param.11) | copy-start | bytes 100
  11.9 63.5 %all-to-all-start.1 = ((bf16[32,8,4096]{2,1,0:T(8,128)(2,1)}), bf16[32,8,4096]{2,1,0:T(8,128)(2,1)}, u32[]{:S(2)}, u32[]{:S(2)}) async-start(bf16[32,8,4096]{2,1,0:T(8,128)(2,1)} %bitcast.27), calls=%async_computation.1 | async-start | bytes 4194304 | tf_op jit(solution)/shard_map/all_to_all | solution.py:222
  25.3 76.1 %all-gather.5.cloned.1.call-start = ((), (), s32[]{:S(2)}) async-start(), calls=%async_computation.5 | async-start | bytes 5013504 | tf_op jit(solution)/shard_map/all_gather | solution.py:247
  75.4 56.0 %all-to-all-start = ((bf16[32,8,4096]{2,1,0:T(8,128)(2,1)}), bf16[32,8,4096]{2,1,0:T(8,128)(2,1)}, u32[]{:S(2)}, u32[]{:S(2)}) async-start(bf16[32,8,4096]{2,1,0:T(8,128)(2,1)} %bitcast.28), calls=%async_computation | async-start | bytes 4194304 | tf_op jit(solution)/shard_map/all_to_all | solution.py:222
  108.4 4.9 %collective-permute-start = (bf16[512,1024]{1,0:T(8,128)(2,1)}, bf16[512,1024]{1,0:T(8,128)(2,1)}, u32[]{:S(2)}, u32[]{:S(2)}) collective-permute-start(bf16[512,1024]{1,0:T(8,128)(2,1)} %get-tuple-element.27), channel_id=1, source_target_pairs={{0,1},{1,0},{2,3},{3,2},{4,5},{5,4},{6,7},{7,6},{8,9},{9,8},{10,11... | collective-permute-start | bytes 3145736 | tf_op jit(solution)/shard_map/ppermute | solution.py:272
  138.3 10.5 %collective-permute-start.1 = (bf16[512,768]{1,0:T(8,128)(2,1)}, bf16[512,768]{1,0:T(8,128)(2,1)}, u32[]{:S(2)}, u32[]{:S(2)}) collective-permute-start(bf16[512,768]{1,0:T(8,128)(2,1)} %get-tuple-element.35), channel_id=1, source_target_pairs={{0,1},{1,0},{2,3},{3,2},{4,5},{5,4},{6,7},{7,6},{8,9},{9,8},{10,11... | collective-permute-start | bytes 2359304 | tf_op jit(solution)/shard_map/ppermute | solution.py:294
  140.2 6.3 %copy-start.1 = (bf16[512,1024]{1,0:T(8,128)(2,1)S(1)}, bf16[512,1024]{1,0:T(8,128)(2,1)}, u32[]{:S(2)}) copy-start(bf16[512,1024]{1,0:T(8,128)(2,1)} %get-tuple-element.34) | copy-start | bytes 3145732
  140.2 58.2 %all-to-all-start.2 = ((bf16[32,8,4224]{2,1,0:T(8,128)(2,1)}), bf16[32,8,4224]{2,1,0:T(8,128)(2,1)S(1)}, u32[]{:S(2)}, u32[]{:S(2)}) async-start(bf16[32,8,4224]{2,1,0:T(8,128)(2,1)} %bitcast.26), calls=%async_computation.2 | async-start | bytes 4325376 | tf_op jit(solution)/shard_map/all_to_all | solution.py:222
  146.5 48.1 %reduce-scatter.2.cloned.1.call-start = ((), (), s32[]{:S(2)}) async-start(), calls=%async_computation.6 | async-start | bytes 1769472 | tf_op jit(solution)/shard_map/reduce_scatter | solution.py:296
  148.7 3.7 %copy-start.4 = (s32[2,128]{1,0:T(2,128)S(1)}, s32[2,128]{1,0:T(2,128)}, u32[]{:S(2)}) copy-start(s32[2,128]{1,0:T(2,128)} %get-tuple-element.21.target_ref) | copy-start | bytes 3076
  152.4 46.0 %copy-start = (bf16[128,2]{0,1:T(2,128)(2,1)S(1)}, bf16[128,2]{0,1:T(2,128)(2,1)}, u32[]{:S(2)}) copy-start(bf16[128,2]{0,1:T(2,128)(2,1)} %param.13) | copy-start | bytes 1540
Sparse Core Ops, SparseCore 0:
  10.1 43.8 all-gather.2
  56.7 44.6 all-gather.4
  152.6 41.9 reduce-scatter.1

commit v7 on v6

--- a/solution.py
+++ b/solution.py
@@ -23,19 +23,22 @@
     return lax.broadcasted_iota(jnp.int32, (rows, tokens), 0) == target
 
 
-def route_kernel(experts, cap, ids_ref, x_any, send_any, target_ref, x, send, sems):
-    load = pltpu.make_async_copy(x_any, x, sems.at[0])
+def route_kernel(experts, cap, ids_any, x_any, send_any, target_any, ids_ref, x, send, target, sems):
+    names = pltpu.make_async_copy(ids_any, ids_ref, sems.at[0])
+    load = pltpu.make_async_copy(x_any, x, sems.at[1])
+    names.start()
     load.start()
     tokens, width = x.shape
+    earlier = (
+        lax.broadcasted_iota(jnp.int32, (tokens, tokens), 0)
+        < lax.broadcasted_iota(jnp.int32, (tokens, tokens), 1)
+    ).astype(F32)
+    names.wait()
     ids = ids_ref[...]
     members = [
         (lax.broadcasted_iota(jnp.int32, (experts, tokens), 0) == ids[k : k + 1]).astype(F32)
         for k in range(2)
     ]
-    earlier = (
-        lax.broadcasted_iota(jnp.int32, (tokens, tokens), 0)
-        < lax.broadcasted_iota(jnp.int32, (tokens, tokens), 1)
-    ).astype(F32)
     count = mm((members[0] + members[1]).astype(BF16), earlier.astype(BF16))
     half = experts * cap // 2
     sub = cap // 2
@@ -44,16 +47,17 @@
         position = jnp.sum(members[k] * count, axis=0, keepdims=True).astype(jnp.int32)
         low = jnp.where(position < sub, position, position + (half - sub))
         targets.append(ids[k : k + 1] * sub + low)
-        target_ref[k : k + 1, :] = targets[k]
+        target[k : k + 1, :] = targets[k]
+    stores = [pltpu.make_async_copy(target, target_any, sems.at[2])]
+    stores[0].start()
     load.wait()
     block = half // 2
-    stores = []
     for j in range(4):
         select = sum(one_hot(t - j * block, block).astype(F32) for t in targets)
         to = (slice(j % 2 * block, (j % 2 + 1) * block), slice(j // 2 * width, (j // 2 + 1) * width))
         send[to] = mm(select.astype(BF16), x[...]).astype(BF16)
-        stores.append(pltpu.make_async_copy(send.at[to], send_any.at[to], sems.at[1 + j]))
-        stores[j].start()
+        stores.append(pltpu.make_async_copy(send.at[to], send_any.at[to], sems.at[3 + j]))
+        stores[-1].start()
     for store in stores:
         store.wait()
 
@@ -143,6 +147,7 @@
         high = total.astype(BF16).astype(F32)
         extra = jnp.where(lane // 64 == i, jnp.where(lane % 64 < 32, high, total - high), extra)
     out[:, 2 * width :] = extra.astype(BF16)
+    fetch(pre, pre_any)
     fetch(out.at[:, 2 * width :], out_any.at[:, 2 * width :])
     for j in range(4):
         grads = mm(pre[...], wg[j * chunk : (j + 1) * chunk, :], NT).astype(BF16)
@@ -150,7 +155,6 @@
             to = slice(i * width + j * chunk, i * width + (j + 1) * chunk)
             out[:, to] = grads[i * half : (i + 1) * half]
             fetch(out.at[:, to], out_any.at[:, to])
-    fetch(pre, pre_any)
     for copy in copies[19:]:
         copy.wait()
 
@@ -232,12 +236,14 @@
         functools.partial(route_kernel, experts, cap),
         (sds((half, 2 * width), BF16), sds((2, tokens), jnp.int32)),
         (expert_ids.T, moe_input),
-        in_specs=[vmem, any_space],
-        out_specs=[any_space, vmem],
+        in_specs=[any_space] * 2,
+        out_specs=[any_space] * 2,
         scratch_shapes=[
+            pltpu.VMEM((2, tokens), jnp.int32),
             pltpu.VMEM((tokens, width), BF16),
             pltpu.VMEM((half, 2 * width), BF16),
-            pltpu.SemaphoreType.DMA((5,)),
+            pltpu.VMEM((2, tokens), jnp.int32),
+            pltpu.SemaphoreType.DMA((7,)),
         ],
     )
     got_input = ranked(exchange(send_input))

time: 207 us -> 206 us (level)
    all_to_all x3, waiting for transfers between devices: 37.8 us -> 35.3 us  [exchange(): lax.all_to_all(values.reshape(experts, cap // 2, -1), 'expert', split_axi...]
where the time goes in v7:
time: 206 us; the launch traced here: 205 us
  waiting for transfers between devices  117 us (57%)
  starting transfers between devices  30.1 us (15%)
  Pallas kernels  21.6 us (10%)
  between operations  14.6 us (7%)
  blocking collectives  10.7 us (5%)
  matrix products  5.85 us (3%)
  local copies, waits for them, and re-layouts  4.31 us (2%)
    reduce_scatter x1, waiting for transfers between devices, on_device(): lax.psum_scatter(pair, 'seq', scatter_dimension=0, tiled=True).astype(F32)  42 us
    all_to_all x3, waiting for transfers between devices, exchange(): lax.all_to_all(values.reshape(experts, cap // 2, -1), 'expert', split_axi...  35.3 us
    all_to_all x3, starting transfers between devices, exchange(): lax.all_to_all(values.reshape(experts, cap // 2, -1), 'expert', split_axi...  26 us
    pallas_call x5, Pallas kernels, call(): pl.pallas_call(kernel, out_shape=outs, compiler_params=pltpu.CompilerPara...  21.6 us
    all_gather x1, waiting for transfers between devices, on_device(): weights = lax.all_gather(weights, ('seq', 'dp'), axis=0, tiled=True)  21 us
    all_gather x1, waiting for transfers between devices, on_device(): frames = lax.all_gather(frame_grad, 'seq', axis=0, tiled=True)  14.8 us
    unnamed x1, blocking collectives  10.7 us
    dot_general x2, matrix products, mm(): return lax.dot_general(a, b, dims, preferred_element_type=F32)  5.85 us
  transfers between devices with their start and end apart: 8, of which 7 were waited for; matrix products, arithmetic and copies ran while one was open for 6% of the time, Pallas kernels for 7%

profile of v7, /device:TPU:56, one launch (start us, length us, event | category | flops | bytes accessed | tf_op | source)
XLA Modules:
  0.0 205.1 jit_solution(16010929845886523476)
XLA Ops:
  7.2 0.0 all-gather.3.cloned.1.call-start
  7.2 0.7 all-gather.3.cloned.1.call-update
  7.9 2.8 %shard_map.103 = (bf16[256,4096]{1,0:T(8,128)(2,1)}, s32[2,128]{1,0:T(2,128)}) custom-call(s32[2,128]{1,0:T(2,128)} %bitcast.32, bf16[128,2048]{1,0:T(8,128)(2,1)} %x_any.1), custom_call_target="tpu_custom_call" | custom-call | tf_op jit(solution)/shard_map/pallas_call | solution.py:189
  10.7 13.4 %all-to-all-start.1 = ((bf16[32,8,4096]{2,1,0:T(8,128)(2,1)}), bf16[32,8,4096]{2,1,0:T(8,128)(2,1)}, u32[]{:S(2)}, u32[]{:S(2)}) async-start(bf16[32,8,4096]{2,1,0:T(8,128)(2,1)} %bitcast.27), calls=%async_computation.1 | async-start | bytes 4194304 | tf_op jit(solution)/shard_map/all_to_all | solution.py:226
  24.2 0.0 all-gather.5.cloned.1.call-start
  24.3 0.7 pad_maximum_fusion
  25.0 1.3 dynamic-slice
  27.0 0.2 dynamic-update-slice
  27.2 10.7 %all-reduce = s32[64]{0:T(128)S(1)} all-reduce(s32[64]{0:T(128)S(1)} %dynamic-update-slice), channel_id=1, replica_groups=mesh['expert'=32,'seq'=8,'dp'=2] {'seq'}, use_global_device_ids=true, to_apply=%add | all-reduce | flops 64 | bytes 512
  37.9 0.1 broadcast_in_dim.3
  38.0 0.7 broadcast_in_dim_reshape.3.names_ref
  38.7 0.6 pad_add_fusion.place_ref
  39.3 14.8 %all-gather.3.cloned.1.call-done.frames_ref = bf16[256,2048]{1,0:T(8,128)(2,1)} async-done(((bf16[32,2048]{1,0:T(8,128)(2,1)}), bf16[256,2048]{1,0:T(8,128)(2,1)}) %all-gather.3.cloned.1.call-update) | async-done | bytes 1048592 | tf_op jit(solution)/shard_map/all_gather | solution.py:232
  54.1 3.6 %shard_map.104 = bf16[256,4096]{1,0:T(8,128)(2,1)} custom-call(s32[1]{0:T(128)} %bitcast.own_ref, s32[1,256]{1,0:T(1,128)} %broadcast_in_dim_reshape.3.names_ref, bf16[256,2048]{1,0:T(8,128)(2,1)} %all-gather.3.cloned.1.call-done.frames_ref, bf16[128,2048]{1,0:T(8,128)(2,1)} %lm_ref.1, s32[2,128]{1,0:T(2,128)} %get-tuple-element.21.target_ref, ...), custom_call_target="tpu_custom_call" | custom-call | flops 1099511627776 | bytes 1073741824 | tf_op jit(solution)/shard_map/pallas_call | solution.py:189
  57.7 16.4 %all-to-all-done.1 = bf16[32,8,4096]{2,1,0:T(8,128)(2,1)} async-done(((bf16[32,8,4096]{2,1,0:T(8,128)(2,1)}), bf16[32,8,4096]{2,1,0:T(8,128)(2,1)}, u32[]{:S(2)}, u32[]{:S(2)}) %all-to-all-start.1) | async-done | bytes 2097184 | tf_op jit(solution)/shard_map/all_to_all | solution.py:226
  74.2 6.3 %all-to-all-start = ((bf16[32,8,4096]{2,1,0:T(8,128)(2,1)}), bf16[32,8,4096]{2,1,0:T(8,128)(2,1)}, u32[]{:S(2)}, u32[]{:S(2)}) async-start(bf16[32,8,4096]{2,1,0:T(8,128)(2,1)} %bitcast.28), calls=%async_computation | async-start | bytes 4194304 | tf_op jit(solution)/shard_map/all_to_all | solution.py:226
  80.4 21.0 %all-gather.5.cloned.1.call-done.w_ref.w_any = bf16[2048,1152]{1,0:T(8,128)(2,1)} async-done(((bf16[128,1152]{1,0:T(8,128)(2,1)}), bf16[2048,1152]{1,0:T(8,128)(2,1)}) %all-gather.5.cloned.1.call-update) | async-done | bytes 4718608 | tf_op jit(solution)/shard_map/all_gather | solution.py:253
  101.4 7.0 %shard_map.106 = (bf16[512,384]{1,0:T(8,128)(2,1)}, f32[512,384]{1,0:T(8,128)}, f32[512,384]{1,0:T(8,128)}, bf16[512,1024]{1,0:T(8,128)(2,1)}, bf16[512,1024]{1,0:T(8,128)(2,1)}) custom-call(s32[2]{0:T(128)} %pad_add_fusion.place_ref, bf16[256,4096]{1,0:T(8,128)(2,1)} %shard_map.105.x_ref, bf16[2048,1152]{1,0:T(8,128)(2,1)} %all-gather.5.cloned.1.call-done.w_ref.w_any), custom_call_target="tpu_custom_call" | custom-call | tf_op jit(solution)/shard_map/pallas_call | solution.py:189
  108.4 2.1 %collective-permute-start = (bf16[512,1024]{1,0:T(8,128)(2,1)}, bf16[512,1024]{1,0:T(8,128)(2,1)}, u32[]{:S(2)}, u32[]{:S(2)}) collective-permute-start(bf16[512,1024]{1,0:T(8,128)(2,1)} %get-tuple-element.27), channel_id=1, source_target_pairs={{0,1},{1,0},{2,3},{3,2},{4,5},{5,4},{6,7},{7,6},{8,9},{9,8},{10,11... | collective-permute-start | bytes 3145736 | tf_op jit(solution)/shard_map/ppermute | solution.py:278
  110.6 2.7 %collective-permute-done = bf16[512,1024]{1,0:T(8,128)(2,1)} collective-permute-done((bf16[512,1024]{1,0:T(8,128)(2,1)}, bf16[512,1024]{1,0:T(8,128)(2,1)}, u32[]{:S(2)}, u32[]{:S(2)}) %collective-permute-start) | collective-permute-done | bytes 1048608 | tf_op jit(solution)/shard_map/ppermute | solution.py:278
  113.3 16.9 %all-to-all-done = bf16[32,8,4096]{2,1,0:T(8,128)(2,1)} async-done(((bf16[32,8,4096]{2,1,0:T(8,128)(2,1)}), bf16[32,8,4096]{2,1,0:T(8,128)(2,1)}, u32[]{:S(2)}, u32[]{:S(2)}) %all-to-all-start) | async-done | bytes 2097184 | tf_op jit(solution)/shard_map/all_to_all | solution.py:226
  130.2 6.6 %shard_map.107 = (bf16[256,4224]{1,0:T(8,128)(2,1)}, bf16[512,768]{1,0:T(8,128)(2,1)}) custom-call(bf16[256,4096]{1,0:T(8,128)(2,1)} %bitcast.5.y_any, bf16[2048,1152]{1,0:T(8,128)(2,1)} %all-gather.5.cloned.1.call-done.w_ref.w_any, bf16[512,384]{1,0:T(8,128)(2,1)} %get-tuple-element.28.hidden_any, f32[512,384]{1,0:T(8,128)} %get-tuple-element.29.gate_any, ...), custom_call_target="tpu_custom_call" | custom-call | tf_op jit(solution)/shard_map/pallas_call | solution.py:189
  136.8 1.9 collective-permute-start.1
  138.7 6.3 %all-to-all-start.2 = ((bf16[32,8,4224]{2,1,0:T(8,128)(2,1)}), bf16[32,8,4224]{2,1,0:T(8,128)(2,1)S(1)}, u32[]{:S(2)}, u32[]{:S(2)}) async-start(bf16[32,8,4224]{2,1,0:T(8,128)(2,1)} %bitcast.26), calls=%async_computation.2 | async-start | bytes 4325376 | tf_op jit(solution)/shard_map/all_to_all | solution.py:226
  145.0 0.0 reduce-scatter.2.cloned.1.call-start
  145.1 2.2 %fusion = f32[1024,768]{1,0:T(8,128)S(1)} fusion(bf16[512,1024]{1,0:T(8,128)(2,1)S(1)} %copy-done.1, bf16[512,768]{1,0:T(8,128)(2,1)} %get-tuple-element.35), kind=kOutput, calls=%fused_computation.3 | convolution fusion | flops 805306368 | bytes 4980736 | tf_op jit(solution)/shard_map/dot_general | solution.py:18
  147.3 3.7 %add_convert_fusion = bf16[1024,768]{1,0:T(8,128)(2,1)} fusion(f32[1024,768]{1,0:T(8,128)S(1)} %fusion, bf16[512,1024]{1,0:T(8,128)(2,1)} %collective-permute-done, bf16[512,768]{1,0:T(8,128)(2,1)} %collective-permute-done.1), kind=kOutput, calls=%fused_computation | convolution fusion | flops 806879232 | bytes 6553600 | tf_op jit(solution)/shard_map/dot_general | solution.py:18
  151.0 0.1 copy.13
  151.1 42.0 %reduce-scatter.2.cloned.1.call-done = bf16[128,768]{1,0:T(8,128)(2,1)} async-done(((bf16[1024,768]{1,0:T(8,128)(2,1)}), bf16[128,768]{1,0:T(8,128)(2,1)}) %reduce-scatter.2.cloned.1.call-update) | async-done | bytes 196624 | tf_op jit(solution)/shard_map/reduce_scatter | solution.py:302
  193.1 1.9 reshape.47
  195.0 2.0 all-to-all-done.2
  197.0 1.6 shard_map.108
  (18 shorter events, 0.1 us)
Async XLA Ops:
  7.2 46.9 %all-gather.3.cloned.1.call-start = ((), (), s32[]{:S(2)}) async-start(), calls=%async_computation.4 | async-start | bytes 1179648 | tf_op jit(solution)/shard_map/all_gather | solution.py:232
  10.7 13.5 %copy-start.2 = (bf16[1,128,2,384]{3,2,1,0:T(2,128)(2,1)S(1)}, bf16[1,128,2,384]{3,2,1,0:T(2,128)(2,1)}, u32[]{:S(2)}) copy-start(bf16[1,128,2,384]{3,2,1,0:T(2,128)(2,1)} %param.14) | copy-start | bytes 589828
  10.7 13.6 %copy-start.3 = (bf16[1,128,384]{2,1,0:T(8,128)(2,1)S(1)}, bf16[1,128,384]{2,1,0:T(8,128)(2,1)}, u32[]{:S(2)}) copy-start(bf16[1,128,384]{2,1,0:T(8,128)(2,1)} %param.15) | copy-start | bytes 294916
  10.7 16.3 %copy-start.5 = (s32[8]{0:T(128)S(1)}, s32[8]{0:T(128)}, u32[]{:S(2)}) copy-start(s32[8]{0:T(128)} %param.11) | copy-start | bytes 100
  10.7 63.5 %all-to-all-start.1 = ((bf16[32,8,4096]{2,1,0:T(8,128)(2,1)}), bf16[32,8,4096]{2,1,0:T(8,128)(2,1)}, u32[]{:S(2)}, u32[]{:S(2)}) async-start(bf16[32,8,4096]{2,1,0:T(8,128)(2,1)} %bitcast.27), calls=%async_computation.1 | async-start | bytes 4194304 | tf_op jit(solution)/shard_map/all_to_all | solution.py:226
  24.2 77.3 %all-gather.5.cloned.1.call-start = ((), (), s32[]{:S(2)}) async-start(), calls=%async_computation.5 | async-start | bytes 5013504 | tf_op jit(solution)/shard_map/all_gather | solution.py:253
  74.2 56.0 %all-to-all-start = ((bf16[32,8,4096]{2,1,0:T(8,128)(2,1)}), bf16[32,8,4096]{2,1,0:T(8,128)(2,1)}, u32[]{:S(2)}, u32[]{:S(2)}) async-start(bf16[32,8,4096]{2,1,0:T(8,128)(2,1)} %bitcast.28), calls=%async_computation | async-start | bytes 4194304 | tf_op jit(solution)/shard_map/all_to_all | solution.py:226
  108.4 4.9 %collective-permute-start = (bf16[512,1024]{1,0:T(8,128)(2,1)}, bf16[512,1024]{1,0:T(8,128)(2,1)}, u32[]{:S(2)}, u32[]{:S(2)}) collective-permute-start(bf16[512,1024]{1,0:T(8,128)(2,1)} %get-tuple-element.27), channel_id=1, source_target_pairs={{0,1},{1,0},{2,3},{3,2},{4,5},{5,4},{6,7},{7,6},{8,9},{9,8},{10,11... | collective-permute-start | bytes 3145736 | tf_op jit(solution)/shard_map/ppermute | solution.py:278
  136.8 10.5 %collective-permute-start.1 = (bf16[512,768]{1,0:T(8,128)(2,1)}, bf16[512,768]{1,0:T(8,128)(2,1)}, u32[]{:S(2)}, u32[]{:S(2)}) collective-permute-start(bf16[512,768]{1,0:T(8,128)(2,1)} %get-tuple-element.35), channel_id=1, source_target_pairs={{0,1},{1,0},{2,3},{3,2},{4,5},{5,4},{6,7},{7,6},{8,9},{9,8},{10,11... | collective-permute-start | bytes 2359304 | tf_op jit(solution)/shard_map/ppermute | solution.py:300
  138.7 6.3 %copy-start.1 = (bf16[512,1024]{1,0:T(8,128)(2,1)S(1)}, bf16[512,1024]{1,0:T(8,128)(2,1)}, u32[]{:S(2)}) copy-start(bf16[512,1024]{1,0:T(8,128)(2,1)} %get-tuple-element.34) | copy-start | bytes 3145732
  138.7 58.2 %all-to-all-start.2 = ((bf16[32,8,4224]{2,1,0:T(8,128)(2,1)}), bf16[32,8,4224]{2,1,0:T(8,128)(2,1)S(1)}, u32[]{:S(2)}, u32[]{:S(2)}) async-start(bf16[32,8,4224]{2,1,0:T(8,128)(2,1)} %bitcast.26), calls=%async_computation.2 | async-start | bytes 4325376 | tf_op jit(solution)/shard_map/all_to_all | solution.py:226
  145.0 48.1 %reduce-scatter.2.cloned.1.call-start = ((), (), s32[]{:S(2)}) async-start(), calls=%async_computation.6 | async-start | bytes 1769472 | tf_op jit(solution)/shard_map/reduce_scatter | solution.py:302
  147.2 3.7 %copy-start.4 = (s32[2,128]{1,0:T(2,128)S(1)}, s32[2,128]{1,0:T(2,128)}, u32[]{:S(2)}) copy-start(s32[2,128]{1,0:T(2,128)} %get-tuple-element.21.target_ref) | copy-start | bytes 3076
  151.0 46.0 %copy-start = (bf16[128,2]{0,1:T(2,128)(2,1)S(1)}, bf16[128,2]{0,1:T(2,128)(2,1)}, u32[]{:S(2)}) copy-start(bf16[128,2]{0,1:T(2,128)(2,1)} %param.13) | copy-start | bytes 1540
Sparse Core Ops, SparseCore 0:
  10.1 43.9 all-gather.2
  56.8 44.6 all-gather.4
  151.1 41.9 reduce-scatter.1

commit v8 on v7

--- a/solution.py
+++ b/solution.py
@@ -9,6 +9,8 @@
 
 F32 = jnp.float32
 BF16 = jnp.bfloat16
+NX, NZ = 4, 8
+ORDER = [[x * NZ + z for z in range(NZ) for x in range(NX)]]
 NT = (((1,), (1,)), ((), ()))
 NN = (((1,), (0,)), ((), ()))
 TN = (((0,), (0,)), ((), ()))
@@ -34,7 +36,7 @@
         < lax.broadcasted_iota(jnp.int32, (tokens, tokens), 1)
     ).astype(F32)
     names.wait()
-    ids = ids_ref[...]
+    ids = ids_ref[...] % NZ * NX + ids_ref[...] // NZ
     members = [
         (lax.broadcasted_iota(jnp.int32, (experts, tokens), 0) == ids[k : k + 1]).astype(F32)
         for k in range(2)
@@ -224,7 +226,8 @@
 
     def exchange(values):
         return lax.all_to_all(
-            values.reshape(experts, cap // 2, -1), "expert", split_axis=0, concat_axis=0, tiled=True
+            values.reshape(experts, cap // 2, -1), "expert", split_axis=0, concat_axis=0,
+            axis_index_groups=ORDER, tiled=True,
         ).reshape(half, -1)
 
     seq = lax.axis_index("seq")

time: 206 us -> 205 us (level)
  no operation moved by 1% of the time
where the time goes in v8:
time: 205 us; the launch traced here: 204 us
  waiting for transfers between devices  116 us (57%)
  starting transfers between devices  29.8 us (15%)
  Pallas kernels  21.6 us (11%)
  between operations  14.6 us (7%)
  blocking collectives  10.8 us (5%)
  matrix products  5.85 us (3%)
  local copies, waits for them, and re-layouts  4.31 us (2%)
    reduce_scatter x1, waiting for transfers between devices, on_device(): lax.psum_scatter(pair, 'seq', scatter_dimension=0, tiled=True).astype(F32)  42 us
    all_to_all x3, waiting for transfers between devices, exchange(): lax.all_to_all(values.reshape(experts, cap // 2, -1), 'expert', split_axi...  34.9 us
    all_to_all x3, starting transfers between devices, exchange(): lax.all_to_all(values.reshape(experts, cap // 2, -1), 'expert', split_axi...  25.6 us
    pallas_call x5, Pallas kernels, call(): pl.pallas_call(kernel, out_shape=outs, compiler_params=pltpu.CompilerPara...  21.6 us
    all_gather x1, waiting for transfers between devices, on_device(): weights = lax.all_gather(weights, ('seq', 'dp'), axis=0, tiled=True)  21.1 us
    all_gather x1, waiting for transfers between devices, on_device(): frames = lax.all_gather(frame_grad, 'seq', axis=0, tiled=True)  14.8 us
    unnamed x1, blocking collectives  10.8 us
    dot_general x2, matrix products, mm(): return lax.dot_general(a, b, dims, preferred_element_type=F32)  5.85 us
  transfers between devices with their start and end apart: 8, of which 7 were waited for; matrix products, arithmetic and copies ran while one was open for 6% of the time, Pallas kernels for 7%

profile of v8, /device:TPU:56, one launch (start us, length us, event | category | flops | bytes accessed | tf_op | source)
XLA Modules:
  0.0 204.4 jit_solution(16622088330591684033)
XLA Ops:
  7.2 0.0 all-gather.3.cloned.1.call-start
  7.2 0.7 all-gather.3.cloned.1.call-update
  7.9 2.8 %shard_map.103 = (bf16[256,4096]{1,0:T(8,128)(2,1)}, s32[2,128]{1,0:T(2,128)}) custom-call(s32[2,128]{1,0:T(2,128)} %bitcast.32, bf16[128,2048]{1,0:T(8,128)(2,1)} %x_any.1), custom_call_target="tpu_custom_call" | custom-call | tf_op jit(solution)/shard_map/pallas_call | solution.py:191
  10.7 13.4 %all-to-all-start.1 = ((bf16[32,8,4096]{2,1,0:T(8,128)(2,1)}), bf16[32,8,4096]{2,1,0:T(8,128)(2,1)}, u32[]{:S(2)}, u32[]{:S(2)}) async-start(bf16[32,8,4096]{2,1,0:T(8,128)(2,1)} %bitcast.27), calls=%async_computation.1 | async-start | bytes 4194304 | tf_op jit(solution)/shard_map/all_to_all | solution.py:228
  24.2 0.0 all-gather.5.cloned.1.call-start
  24.3 0.7 pad_maximum_fusion
  25.0 1.3 dynamic-slice
  27.0 0.2 dynamic-update-slice
  27.2 10.8 %all-reduce = s32[64]{0:T(128)S(1)} all-reduce(s32[64]{0:T(128)S(1)} %dynamic-update-slice), channel_id=1, replica_groups=mesh['expert'=32,'seq'=8,'dp'=2] {'seq'}, use_global_device_ids=true, to_apply=%add | all-reduce | flops 64 | bytes 512
  38.0 0.1 broadcast_in_dim.3
  38.1 0.7 broadcast_in_dim_reshape.3.names_ref
  38.8 0.6 pad_add_fusion.place_ref
  39.4 14.8 %all-gather.3.cloned.1.call-done.frames_ref = bf16[256,2048]{1,0:T(8,128)(2,1)} async-done(((bf16[32,2048]{1,0:T(8,128)(2,1)}), bf16[256,2048]{1,0:T(8,128)(2,1)}) %all-gather.3.cloned.1.call-update) | async-done | bytes 1048592 | tf_op jit(solution)/shard_map/all_gather | solution.py:235
  54.1 3.6 %shard_map.104 = bf16[256,4096]{1,0:T(8,128)(2,1)} custom-call(s32[1]{0:T(128)} %bitcast.own_ref, s32[1,256]{1,0:T(1,128)} %broadcast_in_dim_reshape.3.names_ref, bf16[256,2048]{1,0:T(8,128)(2,1)} %all-gather.3.cloned.1.call-done.frames_ref, bf16[128,2048]{1,0:T(8,128)(2,1)} %lm_ref.1, s32[2,128]{1,0:T(2,128)} %get-tuple-element.21.target_ref, ...), custom_call_target="tpu_custom_call" | custom-call | flops 1099511627776 | bytes 1073741824 | tf_op jit(solution)/shard_map/pallas_call | solution.py:191
  57.8 16.5 %all-to-all-done.1 = bf16[32,8,4096]{2,1,0:T(8,128)(2,1)} async-done(((bf16[32,8,4096]{2,1,0:T(8,128)(2,1)}), bf16[32,8,4096]{2,1,0:T(8,128)(2,1)}, u32[]{:S(2)}, u32[]{:S(2)}) %all-to-all-start.1) | async-done | bytes 2097184 | tf_op jit(solution)/shard_map/all_to_all | solution.py:228
  74.3 6.1 %all-to-all-start = ((bf16[32,8,4096]{2,1,0:T(8,128)(2,1)}), bf16[32,8,4096]{2,1,0:T(8,128)(2,1)}, u32[]{:S(2)}, u32[]{:S(2)}) async-start(bf16[32,8,4096]{2,1,0:T(8,128)(2,1)} %bitcast.28), calls=%async_computation | async-start | bytes 4194304 | tf_op jit(solution)/shard_map/all_to_all | solution.py:228
  80.4 21.1 %all-gather.5.cloned.1.call-done.w_ref.w_any = bf16[2048,1152]{1,0:T(8,128)(2,1)} async-done(((bf16[128,1152]{1,0:T(8,128)(2,1)}), bf16[2048,1152]{1,0:T(8,128)(2,1)}) %all-gather.5.cloned.1.call-update) | async-done | bytes 4718608 | tf_op jit(solution)/shard_map/all_gather | solution.py:256
  101.4 7.0 %shard_map.106 = (bf16[512,384]{1,0:T(8,128)(2,1)}, f32[512,384]{1,0:T(8,128)}, f32[512,384]{1,0:T(8,128)}, bf16[512,1024]{1,0:T(8,128)(2,1)}, bf16[512,1024]{1,0:T(8,128)(2,1)}) custom-call(s32[2]{0:T(128)} %pad_add_fusion.place_ref, bf16[256,4096]{1,0:T(8,128)(2,1)} %shard_map.105.x_ref, bf16[2048,1152]{1,0:T(8,128)(2,1)} %all-gather.5.cloned.1.call-done.w_ref.w_any), custom_call_target="tpu_custom_call" | custom-call | tf_op jit(solution)/shard_map/pallas_call | solution.py:191
  108.4 2.1 %collective-permute-start = (bf16[512,1024]{1,0:T(8,128)(2,1)}, bf16[512,1024]{1,0:T(8,128)(2,1)}, u32[]{:S(2)}, u32[]{:S(2)}) collective-permute-start(bf16[512,1024]{1,0:T(8,128)(2,1)} %get-tuple-element.27), channel_id=1, source_target_pairs={{0,1},{1,0},{2,3},{3,2},{4,5},{5,4},{6,7},{7,6},{8,9},{9,8},{10,11... | collective-permute-start | bytes 3145736 | tf_op jit(solution)/shard_map/ppermute | solution.py:281
  110.5 2.7 %collective-permute-done = bf16[512,1024]{1,0:T(8,128)(2,1)} collective-permute-done((bf16[512,1024]{1,0:T(8,128)(2,1)}, bf16[512,1024]{1,0:T(8,128)(2,1)}, u32[]{:S(2)}, u32[]{:S(2)}) %collective-permute-start) | collective-permute-done | bytes 1048608 | tf_op jit(solution)/shard_map/ppermute | solution.py:281
  113.3 16.2 %all-to-all-done = bf16[32,8,4096]{2,1,0:T(8,128)(2,1)} async-done(((bf16[32,8,4096]{2,1,0:T(8,128)(2,1)}), bf16[32,8,4096]{2,1,0:T(8,128)(2,1)}, u32[]{:S(2)}, u32[]{:S(2)}) %all-to-all-start) | async-done | bytes 2097184 | tf_op jit(solution)/shard_map/all_to_all | solution.py:228
  129.5 6.6 %shard_map.107 = (bf16[256,4224]{1,0:T(8,128)(2,1)}, bf16[512,768]{1,0:T(8,128)(2,1)}) custom-call(bf16[256,4096]{1,0:T(8,128)(2,1)} %bitcast.5.y_any, bf16[2048,1152]{1,0:T(8,128)(2,1)} %all-gather.5.cloned.1.call-done.w_ref.w_any, bf16[512,384]{1,0:T(8,128)(2,1)} %get-tuple-element.28.hidden_any, f32[512,384]{1,0:T(8,128)} %get-tuple-element.29.gate_any, ...), custom_call_target="tpu_custom_call" | custom-call | tf_op jit(solution)/shard_map/pallas_call | solution.py:191
  136.1 1.9 collective-permute-start.1
  138.1 6.1 %all-to-all-start.2 = ((bf16[32,8,4224]{2,1,0:T(8,128)(2,1)}), bf16[32,8,4224]{2,1,0:T(8,128)(2,1)S(1)}, u32[]{:S(2)}, u32[]{:S(2)}) async-start(bf16[32,8,4224]{2,1,0:T(8,128)(2,1)} %bitcast.26), calls=%async_computation.2 | async-start | bytes 4325376 | tf_op jit(solution)/shard_map/all_to_all | solution.py:228
  144.1 0.0 reduce-scatter.2.cloned.1.call-start
  144.2 2.2 %fusion = f32[1024,768]{1,0:T(8,128)S(1)} fusion(bf16[512,1024]{1,0:T(8,128)(2,1)S(1)} %copy-done.1, bf16[512,768]{1,0:T(8,128)(2,1)} %get-tuple-element.35), kind=kOutput, calls=%fused_computation.3 | convolution fusion | flops 805306368 | bytes 4980736 | tf_op jit(solution)/shard_map/dot_general | solution.py:20
  146.4 3.7 %add_convert_fusion = bf16[1024,768]{1,0:T(8,128)(2,1)} fusion(f32[1024,768]{1,0:T(8,128)S(1)} %fusion, bf16[512,1024]{1,0:T(8,128)(2,1)} %collective-permute-done, bf16[512,768]{1,0:T(8,128)(2,1)} %collective-permute-done.1), kind=kOutput, calls=%fused_computation | convolution fusion | flops 806879232 | bytes 6553600 | tf_op jit(solution)/shard_map/dot_general | solution.py:20
  150.1 0.1 copy.13
  150.2 42.0 %reduce-scatter.2.cloned.1.call-done = bf16[128,768]{1,0:T(8,128)(2,1)} async-done(((bf16[1024,768]{1,0:T(8,128)(2,1)}), bf16[128,768]{1,0:T(8,128)(2,1)}) %reduce-scatter.2.cloned.1.call-update) | async-done | bytes 196624 | tf_op jit(solution)/shard_map/reduce_scatter | solution.py:305
  192.2 1.9 reshape.47
  194.1 2.2 %all-to-all-done.2 = bf16[32,8,4224]{2,1,0:T(8,128)(2,1)S(1)} async-done(((bf16[32,8,4224]{2,1,0:T(8,128)(2,1)}), bf16[32,8,4224]{2,1,0:T(8,128)(2,1)S(1)}, u32[]{:S(2)}, u32[]{:S(2)}) %all-to-all-start.2) | async-done | bytes 2162720 | tf_op jit(solution)/shard_map/all_to_all | solution.py:228
  196.3 1.6 shard_map.108
  (18 shorter events, 0.1 us)
Async XLA Ops:
  7.2 47.0 %all-gather.3.cloned.1.call-start = ((), (), s32[]{:S(2)}) async-start(), calls=%async_computation.4 | async-start | bytes 1179648 | tf_op jit(solution)/shard_map/all_gather | solution.py:235
  10.7 13.5 %copy-start.2 = (bf16[1,128,2,384]{3,2,1,0:T(2,128)(2,1)S(1)}, bf16[1,128,2,384]{3,2,1,0:T(2,128)(2,1)}, u32[]{:S(2)}) copy-start(bf16[1,128,2,384]{3,2,1,0:T(2,128)(2,1)} %param.14) | copy-start | bytes 589828
  10.7 13.6 %copy-start.3 = (bf16[1,128,384]{2,1,0:T(8,128)(2,1)S(1)}, bf16[1,128,384]{2,1,0:T(8,128)(2,1)}, u32[]{:S(2)}) copy-start(bf16[1,128,384]{2,1,0:T(8,128)(2,1)} %param.15) | copy-start | bytes 294916
  10.7 16.3 %copy-start.5 = (s32[8]{0:T(128)S(1)}, s32[8]{0:T(128)}, u32[]{:S(2)}) copy-start(s32[8]{0:T(128)} %param.11) | copy-start | bytes 100
  10.7 63.6 %all-to-all-start.1 = ((bf16[32,8,4096]{2,1,0:T(8,128)(2,1)}), bf16[32,8,4096]{2,1,0:T(8,128)(2,1)}, u32[]{:S(2)}, u32[]{:S(2)}) async-start(bf16[32,8,4096]{2,1,0:T(8,128)(2,1)} %bitcast.27), calls=%async_computation.1 | async-start | bytes 4194304 | tf_op jit(solution)/shard_map/all_to_all | solution.py:228
  24.2 77.3 %all-gather.5.cloned.1.call-start = ((), (), s32[]{:S(2)}) async-start(), calls=%async_computation.5 | async-start | bytes 5013504 | tf_op jit(solution)/shard_map/all_gather | solution.py:256
  74.3 55.2 %all-to-all-start = ((bf16[32,8,4096]{2,1,0:T(8,128)(2,1)}), bf16[32,8,4096]{2,1,0:T(8,128)(2,1)}, u32[]{:S(2)}, u32[]{:S(2)}) async-start(bf16[32,8,4096]{2,1,0:T(8,128)(2,1)} %bitcast.28), calls=%async_computation | async-start | bytes 4194304 | tf_op jit(solution)/shard_map/all_to_all | solution.py:228
  108.4 4.9 %collective-permute-start = (bf16[512,1024]{1,0:T(8,128)(2,1)}, bf16[512,1024]{1,0:T(8,128)(2,1)}, u32[]{:S(2)}, u32[]{:S(2)}) collective-permute-start(bf16[512,1024]{1,0:T(8,128)(2,1)} %get-tuple-element.27), channel_id=1, source_target_pairs={{0,1},{1,0},{2,3},{3,2},{4,5},{5,4},{6,7},{7,6},{8,9},{9,8},{10,11... | collective-permute-start | bytes 3145736 | tf_op jit(solution)/shard_map/ppermute | solution.py:281
  136.1 10.3 %collective-permute-start.1 = (bf16[512,768]{1,0:T(8,128)(2,1)}, bf16[512,768]{1,0:T(8,128)(2,1)}, u32[]{:S(2)}, u32[]{:S(2)}) collective-permute-start(bf16[512,768]{1,0:T(8,128)(2,1)} %get-tuple-element.35), channel_id=1, source_target_pairs={{0,1},{1,0},{2,3},{3,2},{4,5},{5,4},{6,7},{7,6},{8,9},{9,8},{10,11... | collective-permute-start | bytes 2359304 | tf_op jit(solution)/shard_map/ppermute | solution.py:303
  138.0 6.2 %copy-start.1 = (bf16[512,1024]{1,0:T(8,128)(2,1)S(1)}, bf16[512,1024]{1,0:T(8,128)(2,1)}, u32[]{:S(2)}) copy-start(bf16[512,1024]{1,0:T(8,128)(2,1)} %get-tuple-element.34) | copy-start | bytes 3145732
  138.1 58.2 %all-to-all-start.2 = ((bf16[32,8,4224]{2,1,0:T(8,128)(2,1)}), bf16[32,8,4224]{2,1,0:T(8,128)(2,1)S(1)}, u32[]{:S(2)}, u32[]{:S(2)}) async-start(bf16[32,8,4224]{2,1,0:T(8,128)(2,1)} %bitcast.26), calls=%async_computation.2 | async-start | bytes 4325376 | tf_op jit(solution)/shard_map/all_to_all | solution.py:228
  144.1 48.1 %reduce-scatter.2.cloned.1.call-start = ((), (), s32[]{:S(2)}) async-start(), calls=%async_computation.6 | async-start | bytes 1769472 | tf_op jit(solution)/shard_map/reduce_scatter | solution.py:305
  146.4 3.7 %copy-start.4 = (s32[2,128]{1,0:T(2,128)S(1)}, s32[2,128]{1,0:T(2,128)}, u32[]{:S(2)}) copy-start(s32[2,128]{1,0:T(2,128)} %get-tuple-element.21.target_ref) | copy-start | bytes 3076
  150.1 46.2 %copy-start = (bf16[128,2]{0,1:T(2,128)(2,1)S(1)}, bf16[128,2]{0,1:T(2,128)(2,1)}, u32[]{:S(2)}) copy-start(bf16[128,2]{0,1:T(2,128)(2,1)} %param.13) | copy-start | bytes 1540
Sparse Core Ops, SparseCore 0:
  10.1 44.0 all-gather.2
  56.8 44.5 all-gather.4
  150.2 41.9 reduce-scatter.1
